TPU v7x, 32 devices: a whole 2x2x4 slice. The times are simulated.
32 devices in a mesh: dp: 8 (over y, x, core), tensor: 4 (over z).
Axes of the slice: x: 2, y: 2, z: 4, core: 2. Of those that a mesh axis runs over, the one named last changes fastest.
Arguments:
- tokens: bfloat16 [4736, 6144], P(('dp', 'tensor')), parts along dimension 0, may hold values from -3 to 3
- query_weight: bfloat16 [6144, 3072], P(None, 'tensor'), may hold values from -0.078125 to 0.078125
- key_weight: bfloat16 [6144, 3072], P(None, 'tensor'), may hold values from -0.078125 to 0.078125
- value_weight: bfloat16 [6144, 3072], P(None, 'tensor'), may hold values from -0.078125 to 0.078125
- adapter_down_weight: bfloat16 [6144, 32], replicated, may hold values from -0.078125 to 0.078125
- query_adapter_up_weight: bfloat16 [16, 3072], P(None, 'tensor'), may hold values from -0.59765625 to 0.59765625
- value_adapter_up_weight: bfloat16 [16, 3072], P(None, 'tensor'), may hold values from -0.59765625 to 0.59765625
- query_norm_gain: float32 [3072], P('tensor'), may hold values from 1 to 2
- key_norm_gain: float32 [3072], P('tensor'), may hold values from 1 to 2
- output_weight: bfloat16 [3072, 6144], P('tensor'), may hold values from -0.109375 to 0.109375
- reassemble_weight: bfloat16 [6144, 512], P('tensor'), may hold values from -0.078125 to 0.078125
- joining_kernel: bfloat16 [3, 3, 512, 256], replicated, may hold values from -0.09375 to 0.09375
- opening_residual_kernel: bfloat16 [3, 3, 256, 256], replicated, may hold values from -0.125 to 0.125
- closing_residual_kernel: bfloat16 [3, 3, 256, 256], replicated, may hold values from -0.125 to 0.125
Outputs:
- layer_out: bfloat16 [4736, 6144], P(('dp', 'tensor')), parts along dimension 0
- joined_map: bfloat16 [64, 74, 256], P(('dp', 'tensor')), parts along dimension 0
There are 8 independent parts, one for each index of `dp`. A program takes and returns all parts, laid end to end along the dimension named above; an argument that names none is the same for every part. Nothing has to cross between parts.
All inputs are finite; a program needn't handle non-finite values.
Results may differ from a plain program's by a relative error of at most 0.018.
Values may be sent and summed in bfloat16 or wider, within the bound.
No kernel may reach another device: no remote copies, remote signals or barrier semaphores. Data moves between devices by JAX's collectives and lax.ppermute only.
A program may use at most 192 MiB of HBM per device.

v0:
```python
import math

import jax
import jax.numpy as jnp
from jax import lax
from jax.sharding import PartitionSpec as P

HEAD_DIM = 128
MAP_W = 74


epsilon = 1e-06
adapter_scale = 2.0


def padded_2(value, sides, width):
    for axis, dim in sides:
        count, length = (lax.axis_size(axis), value.shape[dim])
        up = [(i, (i + 1) % count) for i in range(count - 1)]
        down = [(j, i) for i, j in up]
        last = lax.slice_in_dim(value, length - width, length, axis=dim)
        initial = lax.slice_in_dim(value, 0, width, axis=dim)
        before = lax.ppermute(last, axis, up)
        after = lax.ppermute(initial, axis, down)
        value = jnp.concatenate([before, value, after], axis=dim)
    return value


def normalize(values):
    average = jnp.mean(values, axis=-1, keepdims=True)
    centered = values - average
    variance = jnp.mean(centered * centered, axis=-1, keepdims=True)
    return centered * lax.rsqrt(variance + epsilon)


def conv_valid(padded, kernel):
    row_count = padded.shape[0] - 2
    col_count = padded.shape[1] - 2
    running = jnp.zeros((row_count, col_count, kernel.shape[3]), jnp.float32)
    for offset_row in range(3):
        for offset_col in range(3):
            window = padded[
                offset_row : offset_row + row_count, offset_col : offset_col + col_count, :
            ]
            running = running + jnp.einsum(
                "rwc,cf->rwf",
                window,
                kernel[offset_row, offset_col],
                preferred_element_type=jnp.float32,
            )
    return running


def pad_columns(field):
    return jnp.pad(field, ((0, 0), (1, 1), (0, 0)))


def extend_rows(field):
    return padded_2(field, (("tensor", 0),), 1)


def attend(
    normalized_input,
    query_weight,
    key_weight,
    value_weight,
    adapter_down_weight,
    query_adapter_up_weight,
    value_adapter_up_weight,
    query_norm_gain,
    key_norm_gain,
):
    reduced_rows = query_adapter_up_weight.shape[0]
    reduced_output = jnp.dot(
        normalized_input, adapter_down_weight, preferred_element_type=jnp.float32
    ).astype(jnp.bfloat16)
    query_matrix = jnp.dot(
        normalized_input, query_weight, preferred_element_type=jnp.float32
    ) + adapter_scale * jnp.dot(
        reduced_output[:, :reduced_rows],
        query_adapter_up_weight,
        preferred_element_type=jnp.float32,
    )
    key_rows = jnp.dot(normalized_input, key_weight, preferred_element_type=jnp.float32)
    value_matrix = (
        jnp.dot(normalized_input, value_weight, preferred_element_type=jnp.float32)
        + adapter_scale
        * jnp.dot(
            reduced_output[:, reduced_rows:],
            value_adapter_up_weight,
            preferred_element_type=jnp.float32,
        )
    ).astype(jnp.bfloat16)
    token_count = normalized_input.shape[0]
    head_count = query_weight.shape[1] // HEAD_DIM
    shape_heads = (token_count, head_count, HEAD_DIM)
    query_heads = (
        normalize(query_matrix.reshape(shape_heads))
        * (query_norm_gain.reshape(head_count, HEAD_DIM) / math.sqrt(HEAD_DIM))
    ).astype(jnp.bfloat16)
    key_heads = (
        normalize(key_rows.reshape(shape_heads)) * key_norm_gain.reshape(head_count, HEAD_DIM)
    ).astype(jnp.bfloat16)
    scores = jnp.einsum("qhd,khd->hqk", query_heads, key_heads, preferred_element_type=jnp.float32)
    raised = jnp.exp(scores)
    softmax_weights = (raised / jnp.sum(raised, axis=-1, keepdims=True)).astype(jnp.bfloat16)
    attended = jnp.einsum(
        "hqk,khd->qhd",
        softmax_weights,
        value_matrix.reshape(shape_heads),
        preferred_element_type=jnp.float32,
    )
    return attended.astype(jnp.bfloat16).reshape(token_count, head_count * HEAD_DIM)


def on_device(
    tokens,
    query_weight,
    key_weight,
    value_weight,
    adapter_down_weight,
    query_adapter_up_weight,
    value_adapter_up_weight,
    query_norm_gain,
    key_norm_gain,
    output_weight,
    reassemble_weight,
    joining_kernel,
    opening_residual_kernel,
    closing_residual_kernel,
):
    local_rows = tokens.shape[0]
    model_width = tokens.shape[1]
    everyone = lax.all_gather(tokens, "tensor", axis=0, tiled=True)
    normalized_input = normalize(everyone.astype(jnp.float32)).astype(jnp.bfloat16)
    attended = attend(
        normalized_input,
        query_weight,
        key_weight,
        value_weight,
        adapter_down_weight,
        query_adapter_up_weight,
        value_adapter_up_weight,
        query_norm_gain,
        key_norm_gain,
    )
    partials = jnp.dot(attended, output_weight, preferred_element_type=jnp.float32)
    column_sum = lax.psum_scatter(
        partials.astype(jnp.bfloat16), "tensor", scatter_dimension=1, tiled=True
    ).astype(jnp.float32)
    slice_width = model_width // lax.axis_size("tensor")
    own_columns = lax.dynamic_slice_in_dim(
        everyone, lax.axis_index("tensor") * slice_width, slice_width, 1
    )
    layer_columns = (own_columns.astype(jnp.float32) + column_sum).astype(jnp.bfloat16)
    layer_out = lax.all_to_all(layer_columns, "tensor", split_axis=0, concat_axis=1, tiled=True)
    reassembled = lax.psum_scatter(
        jnp.dot(layer_columns, reassemble_weight, preferred_element_type=jnp.float32).astype(
            jnp.bfloat16
        ),
        "tensor",
        scatter_dimension=0,
        tiled=True,
    )
    map_strip = reassembled.reshape(local_rows // MAP_W, MAP_W, reassemble_weight.shape[1])
    rimmed = padded_2(map_strip, (("tensor", 0),), 1)
    feature = conv_valid(pad_columns(rimmed), joining_kernel).astype(jnp.bfloat16)
    inner_field = jax.nn.relu(
        conv_valid(pad_columns(extend_rows(jax.nn.relu(feature))), opening_residual_kernel)
    ).astype(jnp.bfloat16)
    joined_map = (
        conv_valid(pad_columns(extend_rows(inner_field)), closing_residual_kernel)
        + feature.astype(jnp.float32)
    ).astype(jnp.bfloat16)
    return (layer_out, joined_map)


def solution(mesh):
    return jax.shard_map(
        on_device,
        mesh=mesh,
        in_specs=(
            P(("dp", "tensor"), None),
            P(None, "tensor"),
            P(None, "tensor"),
            P(None, "tensor"),
            P(),
            P(None, "tensor"),
            P(None, "tensor"),
            P("tensor"),
            P("tensor"),
            P("tensor", None),
            P("tensor", None),
            P(),
            P(),
            P(),
        ),
        out_specs=(P(("dp", "tensor"), None), P(("dp", "tensor"), None, None)),
        check_vma=False,
    )
```

profile of v0, /device:TPU:0, one launch (start us, length us, event | category | flops | bytes accessed | tf_op | source)
XLA Modules:
  0.0 481.0 jit_solution(15820682749711515403)
XLA Ops:
  8.7 138.3 %all-gather.3.cloned.1.call-done = bf16[4,148,6144]{2,1,0:T(8,128)(2,1)} async-done(((bf16[1,148,6144]{2,1,0:T(8,128)(2,1)}), bf16[4,148,6144]{2,1,0:T(8,128)(2,1)}) %all-gather.3.cloned.1.call-update) | async-done | bytes 7274512 | tf_op jit(solution)/shard_map/all_gather | solution.py:134
  147.0 5.8 %reshape.76 = bf16[592,6144]{1,0:T(8,128)(2,1)} reshape(bf16[4,148,6144]{2,1,0:T(8,128)(2,1)} %all-gather.3.cloned.1.call-done) | data formatting | bytes 14548992
  152.8 4.3 convert_reduce_fusion
  157.9 2.0 fusion.2
  160.0 6.3 %fusion.3 = bf16[592,6144]{1,0:T(8,128)(2,1)} fusion(bf16[592,6144]{1,0:T(8,128)(2,1)S(1)} %copy-done.1, f32[592]{0:T(1024)S(1)} %add_rsqrt_fusion.2, f32[592]{0:T(1024)S(1)} %broadcast_multiply_fusion.2), kind=kLoop, calls=%fused_computation.5 | loop fusion | flops 14548992 | bytes 14553728 | tf_op jit(solution)/shard_map/convert_element_type | solution.py:135
  166.3 11.0 %fusion.140 = f32[592,768]{1,0:T(8,128)S(1)} fusion(bf16[592,6144]{1,0:T(8,128)(2,1)} %fusion.3, bf16[6144,768]{1,0:T(8,128)(2,1)} %param.17), kind=kOutput, calls=%fused_computation.192 | convolution fusion | flops 5586812928 | bytes 18530304 | tf_op jit(solution)/shard_map/dot_general | solution.py:86
  177.3 2.2 convolution_convert_fusion.2
  182.0 11.2 %fusion.142 = f32[592,768]{0,1:T(8,128)S(1)} fusion(bf16[592,6144]{1,0:T(8,128)(2,1)} %fusion.3, bf16[6144,768]{1,0:T(8,128)(2,1)} %param.16), kind=kOutput, calls=%fused_computation.194 | convolution fusion | flops 5586812928 | bytes 18530304 | tf_op jit(solution)/shard_map/dot_general | solution.py:84
  196.3 10.4 %fusion.141 = f32[592,768]{1,0:T(8,128)S(1)} fusion(bf16[592,6144]{1,0:T(8,128)(2,1)} %fusion.3, bf16[6144,768]{1,0:T(8,128)(2,1)} %param.15), kind=kOutput, calls=%fused_computation.193 | convolution fusion | flops 5586812928 | bytes 18530304 | tf_op jit(solution)/shard_map/dot_general | solution.py:77
  208.4 1.9 copy.42
  212.6 2.2 exponential_reduce_fusion
  214.8 2.0 fusion.6
  217.4 10.5 %convolution_convert_fusion = bf16[592,6144]{1,0:T(8,128)(2,1)} fusion(bf16[592,768]{0,1:T(8,128)(2,1)S(1)} %bitcast.184, bf16[768,6144]{1,0:T(8,128)(2,1)} %param.23), kind=kOutput, calls=%fused_computation.6 | convolution fusion | flops 5590450176 | bytes 17620992 | tf_op jit(solution)/shard_map/dot_general | solution.py:147
  228.0 125.0 %reduce-scatter.2.cloned.1.call-done = bf16[592,1536]{1,0:T(8,128)(2,1)} async-done(((bf16[592,6144]{1,0:T(8,128)(2,1)}), bf16[592,1536]{1,0:T(8,128)(2,1)}) %reduce-scatter.2.cloned.1.call-update) | async-done | bytes 1818640 | tf_op jit(solution)/shard_map/reduce_scatter | solution.py:148
  353.0 2.5 add_convert_fusion
  355.5 1.9 convolution_convert_fusion.1
  358.7 38.8 %all-reduce.6.cloned.1.call-done = bf16[592,512]{1,0:T(8,128)(2,1)} async-done(((bf16[592,512]{1,0:T(8,128)(2,1)}), bf16[592,512]{1,0:T(8,128)(2,1)}) %all-reduce.6.cloned.1.call-update) | async-done | bytes 606224
  400.5 5.2 %collective-permute-start = (bf16[1,74,512]{2,1,0:T(8,128)(2,1)}, bf16[1,74,512]{2,1,0:T(8,128)(2,1)}, u32[]{:S(2)}, u32[]{:S(2)}) collective-permute-start(bf16[1,74,512]{2,1,0:T(8,128)(2,1)} %get-tuple-element.10), channel_id=1, source_target_pairs={{0,1},{1,2},{2,3},{4,5},{5,6},{6,7},{8,9},{9,10},{10,11},{12,13},{... | collective-permute-start | bytes 227336 | tf_op jit(solution)/shard_map/ppermute | solution.py:23
  418.3 5.2 %collective-permute-start.2 = (bf16[1,74,256]{2,1,0:T(8,128)(2,1)}, bf16[1,74,256]{2,1,0:T(8,128)(2,1)}, u32[]{:S(2)}, u32[]{:S(2)}) collective-permute-start(bf16[1,74,256]{2,1,0:T(8,128)(2,1)} %get-tuple-element.14), channel_id=1, source_target_pairs={{0,1},{1,2},{2,3},{4,5},{5,6},{6,7},{8,9},{9,10},{10,11},{12,13},{... | collective-permute-start | bytes 113672 | tf_op jit(solution)/shard_map/ppermute | solution.py:23
  424.9 3.9 all-to-all-start
  437.2 4.6 collective-permute-start.4
  441.8 9.1 %collective-permute-done.5 = bf16[1,74,256]{2,1,0:T(8,128)(2,1)S(1)} collective-permute-done((bf16[1,74,256]{2,1,0:T(8,128)(2,1)S(1)}, bf16[1,74,256]{2,1,0:T(8,128)(2,1)S(1)}, u32[]{:S(2)}, u32[]{:S(2)}) %collective-permute-start.5) | collective-permute-done | bytes 37920 | tf_op jit(solution)/shard_map/ppermute | solution.py:24
  450.9 7.7 %collective-permute-done.4 = bf16[1,74,256]{2,1,0:T(8,128)(2,1)S(1)} collective-permute-done((bf16[1,74,256]{2,1,0:T(8,128)(2,1)S(1)}, bf16[1,74,256]{2,1,0:T(8,128)(2,1)S(1)}, u32[]{:S(2)}, u32[]{:S(2)}) %collective-permute-start.4) | collective-permute-done | bytes 37920 | tf_op jit(solution)/shard_map/ppermute | solution.py:23
  461.0 10.2 %all-to-all-done = bf16[4,148,1536]{2,1,0:T(8,128)(2,1)S(1)} async-done(((bf16[4,148,1536]{2,1,0:T(8,128)(2,1)}), bf16[4,148,1536]{2,1,0:T(8,128)(2,1)S(1)}, u32[]{:S(2)}, u32[]{:S(2)}) %all-to-all-start) | async-done | bytes 1818656 | tf_op jit(solution)/shard_map/all_to_all | solution.py:156
  (112 shorter events, 44.0 us)
Async XLA Ops:
  7.2 348.3 %copy-start = (bf16[1536,512]{1,0:T(8,128)(2,1)S(1)}, bf16[1536,512]{1,0:T(8,128)(2,1)}, u32[]{:S(2)}) copy-start(bf16[1536,512]{1,0:T(8,128)(2,1)} %param.24) | copy-start | bytes 4718596
  7.2 139.8 %all-gather.3.cloned.1.call-start = ((), (), s32[]{:S(2)}) async-start(), calls=%async_computation.3 | async-start | bytes 9338880 | tf_op jit(solution)/shard_map/all_gather | solution.py:134
  7.9 345.1 %reduce-scatter.2.cloned.1.call-start = ((), (), s32[]{:S(2)}) async-start(), calls=%async_computation.2 | async-start | bytes 9093120 | tf_op jit(solution)/shard_map/reduce_scatter | solution.py:148
  152.8 5.1 %copy-start.1 = (bf16[592,6144]{1,0:T(8,128)(2,1)S(1)}, bf16[592,6144]{1,0:T(8,128)(2,1)}, u32[]{:S(2)}) copy-start(bf16[592,6144]{1,0:T(8,128)(2,1)} %reshape.76) | copy-start | bytes 21823492
  166.3 11.0 %copy-start.2 = (bf16[592,6144]{1,0:T(8,128)(2,1)S(1)}, bf16[592,6144]{1,0:T(8,128)(2,1)}, u32[]{:S(2)}) copy-start(bf16[592,6144]{1,0:T(8,128)(2,1)} %fusion.3) | copy-start | bytes 21823492
  166.3 11.1 %copy-start.12 = (bf16[6144,32]{0,1:T(8,128)(2,1)S(1)}, bf16[6144,32]{0,1:T(8,128)(2,1)}, u32[]{:S(2)}) copy-start(bf16[6144,32]{0,1:T(8,128)(2,1)} %param.18) | copy-start | bytes 1179652
  177.3 2.9 copy-start.18
  193.3 3.0 copy-start.3
  196.3 10.4 %copy-start.14 = (bf16[592,32]{0,1:T(8,128)(2,1)S(1)}, bf16[592,32]{0,1:T(8,128)(2,1)}, u32[]{:S(2)}) copy-start(bf16[592,32]{0,1:T(8,128)(2,1)} %copy-done.13) | copy-start | bytes 113668
  196.3 10.4 %copy-start.19 = (bf16[16,768]{1,0:T(8,128)(2,1)S(1)}, bf16[16,768]{1,0:T(8,128)(2,1)}, u32[]{:S(2)}) copy-start(bf16[16,768]{1,0:T(8,128)(2,1)} %param.19) | copy-start | bytes 73732
  212.6 2.2 copy-start.10
  227.9 169.6 %all-reduce.6.cloned.1.call-start = ((), (), s32[]{:S(2)}) async-start(), calls=%async_computation.4 | async-start | bytes 1212416
  399.2 9.1 %collective-permute-start.1 = (bf16[1,74,512]{2,1,0:T(8,128)(2,1)}, bf16[1,74,512]{2,1,0:T(8,128)(2,1)}, u32[]{:S(2)}, u32[]{:S(2)}) collective-permute-start(bf16[1,74,512]{2,1,0:T(8,128)(2,1)} %get-tuple-element.11), channel_id=1, source_target_pairs={{1,0},{2,1},{3,2},{5,4},{6,5},{7,6},{9,8},{10,9},{11,10},{13,12},{... | collective-permute-start | bytes 227336 | tf_op jit(solution)/shard_map/ppermute | solution.py:24
  400.5 7.8 %collective-permute-start = (bf16[1,74,512]{2,1,0:T(8,128)(2,1)}, bf16[1,74,512]{2,1,0:T(8,128)(2,1)}, u32[]{:S(2)}, u32[]{:S(2)}) collective-permute-start(bf16[1,74,512]{2,1,0:T(8,128)(2,1)} %get-tuple-element.10), channel_id=1, source_target_pairs={{0,1},{1,2},{2,3},{4,5},{5,6},{6,7},{8,9},{9,10},{10,11},{12,13},{... | collective-permute-start | bytes 227336 | tf_op jit(solution)/shard_map/ppermute | solution.py:23
  408.2 4.7 copy-start.7
  417.0 11.7 %collective-permute-start.3 = (bf16[1,74,256]{2,1,0:T(8,128)(2,1)}, bf16[1,74,256]{2,1,0:T(8,128)(2,1)}, u32[]{:S(2)}, u32[]{:S(2)}) collective-permute-start(bf16[1,74,256]{2,1,0:T(8,128)(2,1)} %get-tuple-element.15), channel_id=1, source_target_pairs={{1,0},{2,1},{3,2},{5,4},{6,5},{7,6},{9,8},{10,9},{11,10},{13,12},{... | collective-permute-start | bytes 113672 | tf_op jit(solution)/shard_map/ppermute | solution.py:24
  418.3 10.5 %collective-permute-start.2 = (bf16[1,74,256]{2,1,0:T(8,128)(2,1)}, bf16[1,74,256]{2,1,0:T(8,128)(2,1)}, u32[]{:S(2)}, u32[]{:S(2)}) collective-permute-start(bf16[1,74,256]{2,1,0:T(8,128)(2,1)} %get-tuple-element.14), channel_id=1, source_target_pairs={{0,1},{1,2},{2,3},{4,5},{5,6},{6,7},{8,9},{9,10},{10,11},{12,13},{... | collective-permute-start | bytes 113672 | tf_op jit(solution)/shard_map/ppermute | solution.py:23
  424.9 3.9 copy-start.6
  424.9 46.3 %all-to-all-start = ((bf16[4,148,1536]{2,1,0:T(8,128)(2,1)}), bf16[4,148,1536]{2,1,0:T(8,128)(2,1)S(1)}, u32[]{:S(2)}, u32[]{:S(2)}) async-start(bf16[4,148,1536]{2,1,0:T(8,128)(2,1)} %all_to_all.14), calls=%async_computation.1 | async-start | bytes 3735552 | tf_op jit(solution)/shard_map/all_to_all | solution.py:156
  428.8 5.4 %copy-start.8 = (bf16[3,3,256,256]{3,2,1,0:T(8,128)(2,1)S(1)}, bf16[3,3,256,256]{3,2,1,0:T(8,128)(2,1)}, u32[]{:S(2)}) copy-start(bf16[3,3,256,256]{3,2,1,0:T(8,128)(2,1)} %param.26) | copy-start | bytes 3538948
  428.8 5.6 %copy-start.11 = (bf16[2,74,256]{2,1,0:T(8,128)(2,1)S(1)}, bf16[2,74,256]{2,1,0:T(8,128)(2,1)}, u32[]{:S(2)}) copy-start(bf16[2,74,256]{2,1,0:T(8,128)(2,1)} %get-tuple-element.19) | copy-start | bytes 227332
  433.0 25.7 %copy-start.9 = (bf16[3,3,256,256]{3,2,1,0:T(8,128)(2,1)S(1)}, bf16[3,3,256,256]{3,2,1,0:T(8,128)(2,1)}, u32[]{:S(2)}) copy-start(bf16[3,3,256,256]{3,2,1,0:T(8,128)(2,1)} %param.27) | copy-start | bytes 3538948
  435.9 15.0 %collective-permute-start.5 = (bf16[1,74,256]{2,1,0:T(8,128)(2,1)S(1)}, bf16[1,74,256]{2,1,0:T(8,128)(2,1)S(1)}, u32[]{:S(2)}, u32[]{:S(2)}) collective-permute-start(bf16[1,74,256]{2,1,0:T(8,128)(2,1)S(1)} %get-tuple-element.13), channel_id=1, source_target_pairs={{1,0},{2,1},{3,2},{5,4},{6,5},{7,6},{9,8},{10,9},{11,10},{13,12},{... | collective-permute-start | bytes 113672 | tf_op jit(solution)/shard_map/ppermute | solution.py:24
  437.2 21.4 %collective-permute-start.4 = (bf16[1,74,256]{2,1,0:T(8,128)(2,1)S(1)}, bf16[1,74,256]{2,1,0:T(8,128)(2,1)S(1)}, u32[]{:S(2)}, u32[]{:S(2)}) collective-permute-start(bf16[1,74,256]{2,1,0:T(8,128)(2,1)S(1)} %get-tuple-element.12), channel_id=1, source_target_pairs={{0,1},{1,2},{2,3},{4,5},{5,6},{6,7},{8,9},{9,10},{10,11},{12,13},{... | collective-permute-start | bytes 113672 | tf_op jit(solution)/shard_map/ppermute | solution.py:23
  (8 other events, 10.0 us)
Sparse Core Ops, SparseCore 0:
  9.6 137.3 all-gather.2
  228.0 124.8 reduce-scatter.1
  357.6 39.8 all-reduce.5
where the time goes:
time: 482 us; the launch traced here: 481 us
  waiting for transfers between devices  330 us (68%)
  matrix products  67.6 us (14%)
  local copies, waits for them, and re-layouts  23.8 us (5%)
  starting transfers between devices  22.7 us (5%)
  other arithmetic  22.2 us (5%)
  between operations  14.8 us (3%)
    all_gather x1, waiting for transfers between devices, on_device(): everyone = lax.all_gather(tokens, 'tensor', axis=0, tiled=True)  138 us
    reduce_scatter x1, waiting for transfers between devices, on_device(): lax.psum_scatter(partials.astype(jnp.bfloat16), 'tensor', scatter_dimensi...  125 us
    unnamed x4, waiting for transfers between devices  39.5 us
    ppermute x3, starting transfers between devices, padded_2(): before = lax.ppermute(last, axis, up)  14.9 us
    unnamed x50, local copies, waits for them, and re-layouts  14.3 us
    dot_general x27, matrix products, conv_valid(): jnp.einsum('rwc,cf->rwf', window, kernel[offset_row, offset_col], preferr...  14 us
    dot_general x1, matrix products, attend(): jnp.dot(normalized_input, key_weight, preferred_element_type=jnp.float32)  11.2 us
    dot_general x1, matrix products, attend(): jnp.dot(normalized_input, value_weight, preferred_element_type=jnp.float32)  11 us
  transfers between devices with their start and end apart: 10, of which 6 were waited for; matrix products, arithmetic and copies ran while one was open for 3% of the time, Pallas kernels for 0%

commit v1 on v0

--- a/solution.py
+++ b/solution.py
@@ -1,8 +1,11 @@
+import functools
 import math
 
 import jax
 import jax.numpy as jnp
 from jax import lax
+from jax.experimental import pallas as pl
+from jax.experimental.pallas import tpu as pltpu
 from jax.sharding import PartitionSpec as P
 
 HEAD_DIM = 128
@@ -175,9 +178,457 @@
     return (layer_out, joined_map)
 
 
+f32 = jnp.float32
+bf16 = jnp.bfloat16
+KEY_STEPS = 6
+FINISH_STEPS = 4
+PAIR_STEPS = 4
+HEADS_STEP = 2
+LAST_STEPS = 2
+ROW_BLOCK = 80
+VMEM_LIMIT = 56 * 1024 * 1024
+
+
+def round_up(value, unit):
+    return (value + unit - 1) // unit * unit
+
+
+def dot32(a, b):
+    return jnp.dot(a, b, preferred_element_type=f32)
+
+
+def rows_kernel(tokens, *outs):
+    normed = normalize(tokens[...].astype(f32)).astype(bf16)
+    begin = 0
+    for out in outs:
+        out[...] = normed[:, begin : begin + out.shape[1]]
+        begin += out.shape[1]
+
+
+def normalized_rows(tokens, widths):
+    rows, model_width = tokens.shape
+    block = lambda width: pl.BlockSpec((ROW_BLOCK, width), lambda r: (r, 0))
+    return pl.pallas_call(
+        rows_kernel,
+        grid=(pl.cdiv(rows, ROW_BLOCK),),
+        in_specs=[block(model_width)],
+        out_specs=[block(width) for width in widths],
+        out_shape=[jax.ShapeDtypeStruct((rows, width), bf16) for width in widths],
+        compiler_params=pltpu.CompilerParams(vmem_limit_bytes=VMEM_LIMIT),
+        name="normalized_rows",
+    )(tokens)
+
+
+def project_kernel(count, given, final, *refs):
+    parts = refs[:count]
+    weights = refs[count : count + 3]
+    down, query_up, value_up, query_gain, key_gain = refs[count + 3 : count + 8]
+    refs = refs[count + 8 :]
+    earlier, refs = (refs[:2], refs[2:]) if given else (None, refs)
+    outs, (totals, low) = refs[:-2], refs[-2:]
+    step = pl.program_id(0)
+
+    @pl.when(step == 0)
+    def _():
+        for i in range(count):
+            for j in range(3):
+                term = dot32(parts[i][...], weights[j][...])
+                totals[i, j] = term + earlier[0][i, j] if given else term
+            term = dot32(parts[i][...], down[...])
+            low[i] = term + earlier[1][i] if given else term
+
+    @pl.when(step > 0)
+    def _():
+        for i in range(count):
+            for j in range(3):
+                totals[i, j] += dot32(parts[i][...], weights[j][...])
+            low[i] += dot32(parts[i][...], down[...])
+
+    @pl.when(step == pl.num_programs(0) - 1)
+    def _():
+        if not final:
+            outs[0][...] = totals[...]
+            outs[1][...] = low[...]
+            return
+        for i in range(count):
+            reduced = low[i].astype(bf16)
+            query = totals[i, 0] + adapter_scale * dot32(reduced, query_up[...])
+            value = totals[i, 2] + adapter_scale * dot32(reduced, value_up[...])
+            key = totals[i, 1]
+            for h in range(query.shape[1] // HEAD_DIM):
+                lanes = slice(h * HEAD_DIM, (h + 1) * HEAD_DIM)
+                outs[3 * i][:, lanes] = (
+                    normalize(query[:, lanes]) * (query_gain[:, lanes] / math.sqrt(HEAD_DIM))
+                ).astype(bf16)
+                outs[3 * i + 1][:, lanes] = (
+                    normalize(key[:, lanes]) * key_gain[:, lanes]
+                ).astype(bf16)
+            outs[3 * i + 2][...] = value.astype(bf16)
+
+
+def project(parts, weights, down, ups, gains, first=0, earlier=(), final=True):
+    count = len(parts)
+    rows, features = parts[0].shape
+    model_width, width = weights[0].shape
+    depth = model_width // KEY_STEPS
+    offset = first // depth
+    rank = down.shape[1]
+    whole = lambda *shape: pl.BlockSpec(shape, lambda k: (0,) * len(shape))
+    sums = [(count, 3, rows, width), (count, rows, rank)]
+    results = [((rows, width), bf16)] * (3 * count) if final else [(x, f32) for x in sums]
+    result = pl.pallas_call(
+        functools.partial(project_kernel, count, len(earlier) > 0, final),
+        grid=(features // depth,),
+        in_specs=[pl.BlockSpec((rows, depth), lambda k: (0, k))] * count
+        + [pl.BlockSpec((depth, width), lambda k: (k + offset, 0))] * 3
+        + [pl.BlockSpec((depth, rank), lambda k: (k + offset, 0))]
+        + [whole(rank, width)] * 2
+        + [whole(1, width)] * 2
+        + [whole(*x.shape) for x in earlier],
+        out_specs=[whole(*shape) for shape, _ in results],
+        out_shape=[jax.ShapeDtypeStruct(*x) for x in results],
+        scratch_shapes=[pltpu.VMEM(shape, f32) for shape in sums],
+        compiler_params=pltpu.CompilerParams(vmem_limit_bytes=VMEM_LIMIT),
+        name="project",
+    )(*parts, *weights, down, *ups, *gains, *earlier)
+    if not final:
+        return result
+    return [tuple(result[3 * i : 3 * i + 3]) for i in range(count)]
+
+
+def attention_kernel(rows, slot, place, *refs):
+    blocks = refs[:15]
+    outs = refs[15:19]
+    query, key, value = refs[19:]
+    where = place[0]
+
+    @pl.when(pl.program_id(0) == 0)
+    def _():
+        for ref in (query, key, value):
+            ref[...] = jnp.zeros_like(ref)
+        lane = lax.broadcasted_iota(jnp.int32, (rows, HEAD_DIM), 1)
+        ones = jnp.where(lane == 0, 1.0, 0.0).astype(bf16)
+        for h in range(HEADS_STEP):
+            for i in range(4):
+                value[h, i * slot : i * slot + rows, HEAD_DIM:] = ones
+
+    for j in range(3):
+        own, before, after, two, last = (blocks[3 * i + j] for i in range(5))
+
+        def hold(i, ref):
+            for h in range(HEADS_STEP):
+                lanes = slice(h * HEAD_DIM, (h + 1) * HEAD_DIM)
+                if j < 2:
+                    (query, key)[j][h, i * slot : i * slot + rows] = ref[:, lanes]
+                else:
+                    value[h, i * slot : i * slot + rows, :HEAD_DIM] = ref[:, lanes]
+
+        hold(0, own)
+        hold(2, two)
+        for i, end, other in ((1, 3, after), (3, 0, before)):
+            pl.when(where == end)(functools.partial(hold, i, last))
+            pl.when(where != end)(functools.partial(hold, i, other))
+
+    inner = (where == 1) | (where == 2)
+    far = jnp.where(inner, 2, jnp.where(where == 0, 3, 1))
+    near = jnp.where(inner, jnp.where(where == 1, 1, 3), 2)
+    edge = jnp.where((where == 0) | (where == 2), 1, 3)
+    for asked, out in zip((far, near, 0, edge), outs):
+        asked_rows = pl.ds(pl.multiple_of(asked * slot, slot), slot)
+        for h in range(HEADS_STEP):
+            scores = lax.dot_general(
+                query[h, asked_rows],
+                key[h],
+                (((1,), (1,)), ((), ())),
+                preferred_element_type=f32,
+            )
+            sums = dot32(jnp.exp(scores).astype(bf16), value[h])
+            result = sums[:, :HEAD_DIM] / sums[:, HEAD_DIM : HEAD_DIM + 1]
+            lanes = slice(h * HEAD_DIM, (h + 1) * HEAD_DIM)
+            out[:, lanes] = result[:rows].astype(bf16)
+
+
+def attention(place, *qkv):
+    rows, width = qkv[0][0].shape
+    slot = round_up(rows, 16)
+    columns = HEADS_STEP * HEAD_DIM
+    block = pl.BlockSpec((rows, columns), lambda h: (0, h))
+    return pl.pallas_call(
+        functools.partial(attention_kernel, rows, slot),
+        grid=(width // columns,),
+        in_specs=[pl.BlockSpec(memory_space=pltpu.SMEM)] + [block] * 15,
+        out_specs=[block] * 4,
+        out_shape=[jax.ShapeDtypeStruct((rows, width), bf16)] * 4,
+        scratch_shapes=[
+            pltpu.VMEM((HEADS_STEP, 4 * slot, HEAD_DIM), bf16),
+            pltpu.VMEM((HEADS_STEP, 4 * slot, HEAD_DIM), bf16),
+            pltpu.VMEM((HEADS_STEP, 4 * slot, 2 * HEAD_DIM), bf16),
+        ],
+        compiler_params=pltpu.CompilerParams(vmem_limit_bytes=16 * 1024 * 1024),
+        name="attention",
+    )(place.reshape(1), *(x for block_qkv in qkv for x in block_qkv))
+
+
+def pair_kernel(mine, other, held, got, out):
+    out[...] = (dot32(mine[...], held[...]) + dot32(other[...], got[...])).astype(bf16)
+
+
+def pair_sum(mine, other, held, got):
+    rows, width = mine.shape
+    model_width = held.shape[1]
+    columns = model_width // PAIR_STEPS
+    weight = pl.BlockSpec((width, columns), lambda c: (0, c))
+    operand = pl.BlockSpec((rows, width), lambda c: (0, 0))
+    return pl.pallas_call(
+        pair_kernel,
+        grid=(PAIR_STEPS,),
+        in_specs=[operand, operand, weight, weight],
+        out_specs=pl.BlockSpec((rows, columns), lambda c: (0, c)),
+        out_shape=jax.ShapeDtypeStruct((rows, model_width), bf16),
+        compiler_params=pltpu.CompilerParams(vmem_limit_bytes=VMEM_LIMIT),
+        name="pair_sum",
+    )(mine, other, held, got)
+
+
+def finish_kernel(mine, edge, far, near, weight, layer_out, reassembled, total):
+    step = pl.program_id(0)
+    rows = reassembled.shape[1]
+    layer = (
+        mine[...] + edge[...].astype(f32) + far[...].astype(f32) + near[...].astype(f32)
+    ).astype(bf16)
+    layer_out[...] = layer
+    term = dot32(layer, weight[...])
+
+    @pl.when(step == 0)
+    def _():
+        total[...] = term
+
+    @pl.when(step > 0)
+    def _():
+        total[...] += term
+
+    @pl.when(step == pl.num_programs(0) - 1)
+    def _():
+        for r in range(reassembled.shape[0]):
+            reassembled[r] = total[r * rows : (r + 1) * rows].astype(bf16)
+
+
+def finish(mine, edge, far, near, weight):
+    rows, model_width = mine.shape
+    channels = weight.shape[1]
+    steps = FINISH_STEPS
+    depth = model_width // steps
+    block = pl.BlockSpec((rows, depth), lambda k: (0, k))
+    shape = (rows // MAP_W, MAP_W, channels)
+    return pl.pallas_call(
+        finish_kernel,
+        grid=(steps,),
+        in_specs=[block] * 4 + [pl.BlockSpec((depth, channels), lambda k: (k, 0))],
+        out_specs=[block, pl.BlockSpec(shape, lambda k: (0, 0, 0))],
+        out_shape=[
+            jax.ShapeDtypeStruct((rows, model_width), bf16),
+            jax.ShapeDtypeStruct(shape, bf16),
+        ],
+        scratch_shapes=[pltpu.VMEM((rows, channels), f32)],
+        compiler_params=pltpu.CompilerParams(vmem_limit_bytes=VMEM_LIMIT),
+        name="finish",
+    )(mine, edge, far, near, weight)
+
+
+def joining_kernel_body(total_rows, pitch, first, *refs):
+    pieces = refs[:5]
+    joining, opening, closing, out, field, feature, inner = refs[5:]
+    field[...] = jnp.zeros_like(field)
+    place = 0
+    for piece in pieces:
+        for r in range(piece.shape[0]):
+            field[place * pitch : place * pitch + MAP_W] = piece[r]
+            place += 1
+
+    def conv(source, kernel):
+        size = source.shape[0] - 2 * pitch
+        sums = []
+        for b in range(3):
+            running = None
+            for a in range(3):
+                term = dot32(source[a * pitch : a * pitch + size], kernel[a, b])
+                running = term if running is None else running + term
+            sums.append(running)
+        return sums[1] + pltpu.roll(sums[0], 1, 0) + pltpu.roll(sums[2], size - 1, 0)
+
+    def masked(values, margin):
+        size, channels = values.shape
+        shape = (size // pitch, pitch, channels)
+        row = lax.broadcasted_iota(jnp.int32, shape, 0) + (first[0] - margin)
+        column = lax.broadcasted_iota(jnp.int32, shape, 1)
+        keep = (row >= 0) & (row < total_rows) & (column < MAP_W)
+        return jnp.where(keep, values.reshape(shape), 0.0).reshape(size, channels)
+
+    feature[...] = masked(conv(field, joining), 2).astype(bf16)
+    rectified = jnp.maximum(feature[...], 0)
+    inner[...] = masked(jax.nn.relu(conv(rectified, opening)), 1).astype(bf16)
+    rows = out.shape[0]
+    result = conv(inner, closing) + feature[2 * pitch : (2 + rows) * pitch].astype(f32)
+    for r in range(rows):
+        out[r] = result[r * pitch : r * pitch + MAP_W].astype(bf16)
+
+
+def joining(reassembled, joining_weight, opening_weight, closing_weight):
+    count = lax.axis_size("tensor")
+    place = lax.axis_index("tensor")
+    rows, _, channels = reassembled.shape
+    features = joining_weight.shape[3]
+    send = lambda value, pairs: lax.ppermute(value, "tensor", pairs)
+    above = send(reassembled, [(i, i + 1) for i in range(count - 1)])
+    below = send(reassembled, [(i + 1, i) for i in range(count - 1)])
+    edge = jnp.where(place < 2, reassembled[rows - 1 :], reassembled[:1])
+    edge = send(edge, [(0, 2), (1, 3), (2, 0), (3, 1)])
+    above_far = jnp.where(place >= 2, edge, 0)
+    below_far = jnp.where(place < 2, edge, 0)
+    pitch = round_up(MAP_W + 1, 16)
+    first = (place * rows).astype(jnp.int32).reshape(1)
+    return pl.pallas_call(
+        functools.partial(joining_kernel_body, count * rows, pitch),
+        in_specs=[pl.BlockSpec(memory_space=pltpu.SMEM)]
+        + [pl.BlockSpec(memory_space=pltpu.VMEM)] * 8,
+        out_specs=pl.BlockSpec(memory_space=pltpu.VMEM),
+        out_shape=jax.ShapeDtypeStruct((rows, MAP_W, features), bf16),
+        scratch_shapes=[
+            pltpu.VMEM(((rows + 6) * pitch, channels), bf16),
+            pltpu.VMEM(((rows + 4) * pitch, features), bf16),
+            pltpu.VMEM(((rows + 2) * pitch, features), bf16),
+        ],
+        compiler_params=pltpu.CompilerParams(vmem_limit_bytes=VMEM_LIMIT),
+        name="joining",
+    )(
+        first,
+        above_far,
+        above,
+        reassembled,
+        below,
+        below_far,
+        joining_weight,
+        opening_weight,
+        closing_weight,
+    )
+
+
+def on_device_line(
+    tokens,
+    query_weight,
+    key_weight,
+    value_weight,
+    adapter_down_weight,
+    query_adapter_up_weight,
+    value_adapter_up_weight,
+    query_norm_gain,
+    key_norm_gain,
+    output_weight,
+    reassemble_weight,
+    joining_kernel,
+    opening_residual_kernel,
+    closing_residual_kernel,
+):
+    place = lax.axis_index("tensor").astype(jnp.int32)
+    images = lax.axis_size("dp")
+    image = lax.axis_index("dp")
+    rows, model_width = tokens.shape
+    heads_width = output_weight.shape[0]
+    send = lambda value, pairs: lax.ppermute(value, "tensor", pairs)
+    after = lambda value, *others: lax.optimization_barrier((value, others))[0]
+
+    rank = query_adapter_up_weight.shape[0]
+    ups = (
+        jnp.pad(query_adapter_up_weight, ((0, rank), (0, 0))),
+        jnp.pad(value_adapter_up_weight, ((rank, 0), (0, 0))),
+    )
+    gains = (query_norm_gain.reshape(1, heads_width), key_norm_gain.reshape(1, heads_width))
+    heads = lambda *parts, **kwargs: project(
+        parts,
+        (query_weight, key_weight, value_weight),
+        adapter_down_weight,
+        ups,
+        gains,
+        **kwargs,
+    )
+
+    cut = model_width // KEY_STEPS * (KEY_STEPS - LAST_STEPS)
+    rest = dict(first=cut)
+    inward, outward = [(0, 1), (3, 2)], [(1, 0), (2, 3)]
+
+    (own,) = normalized_rows(tokens, (model_width,))
+    up1 = send(own, [(0, 1), (1, 2), (2, 3)])
+    down1 = send(own, [(1, 0), (2, 1), (3, 2)])
+    (own_heads,) = heads(own)
+    share = heads_width // images
+    piece = lax.dynamic_slice_in_dim(output_weight, image * share, share, 0)
+    piece = send(after(piece, own_heads), inward)
+    share = reassemble_weight.shape[0] // images
+    small = lax.dynamic_slice_in_dim(reassemble_weight, image * share, share, 0)
+    small_end = send(after(small, own_heads), inward)
+
+    up1, down1 = after((up1, down1), own_heads)
+    up2 = send(up1, [(1, 2), (2, 3)])
+    down2 = send(down1, [(2, 1), (1, 0)])
+    before_heads, after_heads = heads(up1, down1)
+
+    two = after(up2 + down2, before_heads, after_heads)
+    partner_weight = lax.all_gather(after(piece, two), "dp", axis=0, tiled=True)
+    two = (two[:, :cut], two[:, cut:])
+    last = [send(part, outward) for part in two]
+    small_two = send(after(jnp.stack([small, small_end]), up2, down2), [(1, 2), (2, 1)])
+    two_sums = heads(two[0], final=False)
+    (two_heads,) = heads(two[1], earlier=two_sums, **rest)
+    last_sums = heads(after(last[0], two_heads), final=False)
+    (last_heads,) = heads(last[1], earlier=last_sums, **rest)
+
+    far, near, mine, edge = attention(
+        place, own_heads, before_heads, after_heads, two_heads, last_heads
+    )
+    far_got = send(far, inward)
+    near_got = send(near, inward)
+    mine_got = send(edge, inward)
+
+    held = jnp.stack([small, small_end, small_two[0], small_two[1]])
+    three = send(after(jnp.stack([small, small_two[0], small_two[1]]), last[1]), outward)
+    three, held = after((three, held), far)
+    shares = jnp.where(
+        place == 0,
+        jnp.stack([small, three[0], three[1], three[2]]),
+        jnp.where(
+            place == 1,
+            jnp.stack([held[1], held[0], held[2], held[3]]),
+            jnp.where(
+                place == 2,
+                jnp.stack([held[3], held[2], held[0], held[1]]),
+                jnp.stack([three[2], three[1], three[0], small]),
+            ),
+        ),
+    )
+    reassemble_full = lax.all_gather(shares, "dp", axis=1, tiled=True).reshape(
+        model_width, reassemble_weight.shape[1]
+    )
+
+    edge = dot32(edge, output_weight).astype(bf16)
+    edge = send(edge, outward)
+    far = pair_sum(far, far_got, output_weight, partner_weight)
+    far = send(far, [(1, 3), (2, 0)])
+    near = pair_sum(near, near_got, output_weight, partner_weight)
+    near = send(near, [(1, 2), (2, 1)])
+    mine = (
+        tokens.astype(f32) + dot32(mine, output_weight) + dot32(mine_got, partner_weight)
+    )
+    layer_out, reassembled = finish(mine, edge, far, near, reassemble_full)
+    joined_map = joining(
+        reassembled, joining_kernel, opening_residual_kernel, closing_residual_kernel
+    )
+    return (layer_out, joined_map)
+
+
 def solution(mesh):
+    body = on_device_line if mesh.shape["tensor"] == 4 else on_device
     return jax.shard_map(
-        on_device,
+        body,
         mesh=mesh,
         in_specs=(
             P(("dp", "tensor"), None),

time: 482 us -> 324 us (0.67)
  waiting for transfers between devices: 330 us -> 110 us
  Pallas kernels: 0 us -> 115 us
  matrix products: 67.6 us -> 19.8 us
  starting transfers between devices: 22.7 us -> 44.3 us
  other arithmetic: 22.2 us -> 4.35 us
  local copies, waits for them, and re-layouts: 23.8 us -> 14.1 us
    all_gather x1 -> x2, waiting for transfers between devices: 138 us -> 0.02 us  [the longest x1 0.02 us: on_device_line(): partner_weight = lax.all_gather(after(piece, two), 'dp', axis=0, tiled=True)]
    reduce_scatter x1 -> x0, waiting for transfers between devices: 125 us -> none  [on_device(): lax.psum_scatter(partials.astype(jnp.bfloat16), 'tensor', scatter_dimensi...]
    pallas_call x0 -> x12, Pallas kernels: none -> 115 us  [the longest x6 73.3 us: project(): pl.pallas_call(functools.partial(project_kernel, count, len(earlier) > 0,...]
    ppermute x6 -> x19, waiting for transfers between devices: 16.9 us -> 110 us  [the longest x16 105 us: on_device_line(): send = lambda value, pairs: lax.ppermute(value, 'tensor', pairs)]
    dot_general x37 -> x3, matrix products: 67.6 us -> 19.8 us  [dot32(): return jnp.dot(a, b, preferred_element_type=f32)]
    unnamed x4 -> x2, waiting for transfers between devices: 39.5 us -> 0.03 us
    ppermute x6 -> x19, starting transfers between devices: 18.8 us -> 44.2 us  [the longest x16 39.2 us: on_device_line(): send = lambda value, pairs: lax.ppermute(value, 'tensor', pairs)]
    all_to_all x1 -> x0, waiting for transfers between devices: 10.2 us -> none  [on_device(): lax.all_to_all(layer_columns, 'tensor', split_axis=0, concat_axis=1, tile...]
  transfers between devices with their start and end apart: 10 -> 21, of which waited for: 6 -> 10; matrix products, arithmetic and copies ran while one was open for 3% -> 10% of each run, Pallas kernels for 0% -> 30%
where the time goes in v1:
time: 324 us; the launch traced here: 323 us
  Pallas kernels  115 us (35%)
  waiting for transfers between devices  110 us (34%)
  starting transfers between devices  44.3 us (14%)
  matrix products  19.8 us (6%)
  between operations  14.7 us (5%)
  local copies, waits for them, and re-layouts  14.1 us (4%)
  other arithmetic  4.35 us (1%)
    ppermute x16, waiting for transfers between devices, on_device_line(): send = lambda value, pairs: lax.ppermute(value, 'tensor', pairs)  105 us
    pallas_call x6, Pallas kernels, project(): pl.pallas_call(functools.partial(project_kernel, count, len(earlier) > 0,...  73.3 us
    ppermute x16, starting transfers between devices, on_device_line(): send = lambda value, pairs: lax.ppermute(value, 'tensor', pairs)  39.2 us
    dot_general x3, matrix products, dot32(): return jnp.dot(a, b, preferred_element_type=f32)  19.8 us
    pallas_call x2, Pallas kernels, pair_sum(): pl.pallas_call(pair_kernel, grid=(PAIR_STEPS,), in_specs=[operand, operan...  19 us
    unnamed x74, local copies, waits for them, and re-layouts  8.9 us
    pallas_call x1, Pallas kernels, finish(): pl.pallas_call(finish_kernel, grid=(steps,), in_specs=[block] * 4 + [pl.B...  7.67 us
  transfers between devices with their start and end apart: 21, of which 10 were waited for; matrix products, arithmetic and copies ran while one was open for 10% of the time, Pallas kernels for 30%

profile of v1, /device:TPU:0, one launch (start us, length us, event | category | flops | bytes accessed | tf_op | source)
XLA Modules:
  0.0 322.7 jit_solution(8814443947973855478)
XLA Ops:
  10.9 5.2 %collective-permute-start = (bf16[148,6144]{1,0:T(8,128)(2,1)}, bf16[148,6144]{1,0:T(8,128)(2,1)S(1)}, u32[]{:S(2)}, u32[]{:S(2)}) collective-permute-start(bf16[148,6144]{1,0:T(8,128)(2,1)} %normalized_rows.1.refs_0_), channel_id=1, source_target_pairs={{0,1},{1,2},{2,3},{4,5},{5,6},{6,7},{8,9},{9,10},{10,11},{12,13},{... | collective-permute-start | bytes 5455880 | tf_op jit(solution)/shard_map/ppermute | solution.py:537
  22.2 15.1 %project.6 = (bf16[148,768]{1,0:T(8,128)(2,1)}, bf16[148,768]{1,0:T(8,128)(2,1)}, bf16[148,768]{1,0:T(8,128)(2,1)}) custom-call(bf16[148,6144]{1,0:T(8,128)(2,1)} %normalized_rows.1.refs_0_, bf16[6144,768]{1,0:T(8,128)(2,1)} %refs_1_.9, bf16[6144,768]{1,0:T(8,128)(2,1)} %refs_2_.11, bf16[6144,768]{1,0:T(8,128)(2,1)} %refs_3_.11, ...), custom_call_target="tpu_custom_call" | custom-call | tf_op jit(solution)/shard_map/project/pallas_call | solution.py:279
  37.3 18.9 %collective-permute-done.refs_0_ = bf16[148,6144]{1,0:T(8,128)(2,1)S(1)} collective-permute-done((bf16[148,6144]{1,0:T(8,128)(2,1)}, bf16[148,6144]{1,0:T(8,128)(2,1)S(1)}, u32[]{:S(2)}, u32[]{:S(2)}) %collective-permute-start) | collective-permute-done | bytes 1818656 | tf_op jit(solution)/shard_map/ppermute | solution.py:537
  56.2 4.2 %collective-permute-done.1.refs_1_ = bf16[148,6144]{1,0:T(8,128)(2,1)} collective-permute-done((bf16[148,6144]{1,0:T(8,128)(2,1)}, bf16[148,6144]{1,0:T(8,128)(2,1)}, u32[]{:S(2)}, u32[]{:S(2)}) %collective-permute-start.1) | collective-permute-done | bytes 1818656 | tf_op jit(solution)/shard_map/ppermute | solution.py:537
  64.9 7.8 %collective-permute-start.7 = (bf16[96,6144]{1,0:T(8,128)(2,1)}, bf16[96,6144]{1,0:T(8,128)(2,1)}, u32[]{:S(2)}, u32[]{:S(2)}) collective-permute-start(bf16[96,6144]{1,0:T(8,128)(2,1)} %constant_dynamic-slice_fusion.1), channel_id=1, source_target_pairs={{0,1},{3,2},{4,5},{7,6},{8,9},{11,10},{12,13},{15,14},{16,17},{19,... | collective-permute-start | bytes 3538952 | tf_op jit(solution)/shard_map/ppermute | solution.py:537
  72.7 19.3 %project.7 = (bf16[148,768]{1,0:T(8,128)(2,1)}, bf16[148,768]{1,0:T(8,128)(2,1)}, bf16[148,768]{1,0:T(8,128)(2,1)}, bf16[148,768]{1,0:T(8,128)(2,1)}, bf16[148,7...) custom-call(bf16[148,6144]{1,0:T(8,128)(2,1)} %copy-done.24, bf16[148,6144]{1,0:T(8,128)(2,1)} %collective-permute-done.1.refs_1_, ...), custom_call_target="tpu_custom_call" | custom-call | tf_op jit(solution)/shard_map/project/pallas_call | solution.py:279
  92.0 14.9 %collective-permute-done.3 = bf16[148,6144]{1,0:T(8,128)(2,1)S(1)} collective-permute-done((bf16[148,6144]{1,0:T(8,128)(2,1)}, bf16[148,6144]{1,0:T(8,128)(2,1)S(1)}, u32[]{:S(2)}, u32[]{:S(2)}) %collective-permute-start.3) | collective-permute-done | bytes 1818656 | tf_op jit(solution)/shard_map/ppermute | solution.py:537
  116.0 14.2 %collective-permute-done.4.refs_0_ = bf16[148,2048]{1,0:T(8,128)(2,1)S(1)} collective-permute-done((bf16[148,2048]{1,0:T(8,128)(2,1)S(1)}, bf16[148,2048]{1,0:T(8,128)(2,1)S(1)}, u32[]{:S(2)}, u32[]{:S(2)}) %collective-permute-start.4) | collective-permute-done | bytes 606240 | tf_op jit(solution)/shard_map/ppermute | solution.py:537
  131.7 11.7 %project.8 = (f32[1,3,148,768]{3,2,1,0:T(8,128)}, f32[1,148,32]{2,1,0:T(8,128)}) custom-call(bf16[148,4096]{1,0:T(8,128)(2,1)} %copy-done.20, bf16[6144,768]{1,0:T(8,128)(2,1)} %refs_1_.9, bf16[6144,768]{1,0:T(8,128)(2,1)} %refs_2_.11, bf16[6144,768]{1,0:T(8,128)(2,1)} %refs_3_.11, bf16[6144,32]{1,0:T(8,128)(2,1)} %copy.16.refs_4_.refs_5_, ...), custom_call_target="tpu_custom_call" | custom-call | tf_op jit(solution)/shard_map/project/pallas_call | solution.py:279
  143.4 8.1 %project.9 = (bf16[148,768]{1,0:T(8,128)(2,1)}, bf16[148,768]{1,0:T(8,128)(2,1)}, bf16[148,768]{1,0:T(8,128)(2,1)}) custom-call(bf16[148,2048]{1,0:T(8,128)(2,1)} %copy-done.23, bf16[6144,768]{1,0:T(8,128)(2,1)} %refs_1_.9, bf16[6144,768]{1,0:T(8,128)(2,1)} %refs_2_.11, bf16[6144,768]{1,0:T(8,128)(2,1)} %refs_3_.11, bf16[6144,32]{1,0:T(8,128)(2,1)} %copy.16.refs_4_.refs_5_, ...), custom_call_target="tpu_custom_call" | custom-call | tf_op jit(solution)/shard_map/project/pallas_call | solution.py:279
  151.6 5.4 %collective-permute-done.5.refs_0_ = bf16[148,4096]{1,0:T(8,128)(2,1)} collective-permute-done((bf16[148,4096]{1,0:T(8,128)(2,1)S(1)}, bf16[148,4096]{1,0:T(8,128)(2,1)}, u32[]{:S(2)}, u32[]{:S(2)}) %collective-permute-start.5) | collective-permute-done | bytes 1212448 | tf_op jit(solution)/shard_map/ppermute | solution.py:537
  157.0 11.1 %project.10 = (f32[1,3,148,768]{3,2,1,0:T(8,128)}, f32[1,148,32]{2,1,0:T(8,128)}) custom-call(bf16[148,4096]{1,0:T(8,128)(2,1)} %collective-permute-done.5.refs_0_, bf16[6144,768]{1,0:T(8,128)(2,1)} %refs_1_.9, bf16[6144,768]{1,0:T(8,128)(2,1)} %refs_2_.11, bf16[6144,768]{1,0:T(8,128)(2,1)} %refs_3_.11, bf16[6144,32]{1,0:T(8,128)(2,1)} %copy.16.refs_4_.refs_5_, ...), custom_call_target="tpu_custom_call" | custom-call | tf_op jit(solution)/shard_map/project/pallas_call | solution.py:279
  168.2 8.0 %project.11 = (bf16[148,768]{1,0:T(8,128)(2,1)}, bf16[148,768]{1,0:T(8,128)(2,1)}, bf16[148,768]{1,0:T(8,128)(2,1)}) custom-call(bf16[148,2048]{1,0:T(8,128)(2,1)} %copy-done.27, bf16[6144,768]{1,0:T(8,128)(2,1)} %refs_1_.9, bf16[6144,768]{1,0:T(8,128)(2,1)} %refs_2_.11, bf16[6144,768]{1,0:T(8,128)(2,1)} %refs_3_.11, bf16[6144,32]{1,0:T(8,128)(2,1)} %copy.16.refs_4_.refs_5_, ...), custom_call_target="tpu_custom_call" | custom-call | tf_op jit(solution)/shard_map/project/pallas_call | solution.py:279
  179.1 5.6 %attention.1 = (bf16[148,768]{1,0:T(8,128)(2,1)S(1)}, bf16[148,768]{1,0:T(8,128)(2,1)S(1)}, bf16[148,768]{1,0:T(8,128)(2,1)S(1)}, bf16[148,768]{1,0:T(8,128)(2,1)S(1)}) custom-call(s32[1]{0:T(128)} %bitcast.place, bf16[148,768]{1,0:T(8,128)(2,1)S(1)} %copy-done.4, bf16[148,768]{1,0:T(8,128)(2,1)S(1)} %copy-done.5, bf16[148,768]{1,0:T(8,128)(2,1)S(1)} %copy-done.6, ...), custom_call_target="tpu_custom_call" | custom-call | tf_op jit(solution)/shard_map/attention/pallas_call | solution.py:356
  189.1 7.1 %convolution_convert_fusion = bf16[148,6144]{1,0:T(8,128)(2,1)} fusion(bf16[148,768]{1,0:T(8,128)(2,1)S(1)} %get-tuple-element.62, bf16[768,6144]{1,0:T(8,128)(2,1)} %held.3), kind=kOutput, calls=%fused_computation.2 | convolution fusion | flops 1397612544 | bytes 11483136 | tf_op jit(solution)/shard_map/dot_general | solution.py:197
  198.2 9.4 %pair_sum.3 = bf16[148,6144]{1,0:T(8,128)(2,1)} custom-call(bf16[148,768]{1,0:T(8,128)(2,1)} %copy-done.3, bf16[148,768]{1,0:T(8,128)(2,1)} %copy-done.29, bf16[768,6144]{1,0:T(8,128)(2,1)} %held.3, bf16[768,6144]{1,0:T(8,128)(2,1)} %all-gather.3.cloned.1.call-done.got), custom_call_target="tpu_custom_call" | custom-call | tf_op jit(solution)/shard_map/pair_sum/pallas_call | solution.py:382
  210.4 9.5 %pair_sum.2 = bf16[148,6144]{1,0:T(8,128)(2,1)} custom-call(bf16[148,768]{1,0:T(8,128)(2,1)} %copy-done.2, bf16[148,768]{1,0:T(8,128)(2,1)} %copy-done.28, bf16[768,6144]{1,0:T(8,128)(2,1)} %held.3, bf16[768,6144]{1,0:T(8,128)(2,1)} %all-gather.3.cloned.1.call-done.got), custom_call_target="tpu_custom_call" | custom-call | tf_op jit(solution)/shard_map/pair_sum/pallas_call | solution.py:382
  221.2 7.0 %collective-permute-start.6 = (bf16[148,768]{1,0:T(8,128)(2,1)S(1)}, bf16[148,768]{1,0:T(8,128)(2,1)S(1)}, u32[]{:S(2)}, u32[]{:S(2)}) collective-permute-start(bf16[148,768]{1,0:T(8,128)(2,1)S(1)} %get-tuple-element.62), channel_id=1, source_target_pairs={{0,1},{3,2},{4,5},{7,6},{8,9},{11,10},{12,13},{15,14},{16,17},{19,... | collective-permute-start | bytes 681992 | tf_op jit(solution)/shard_map/ppermute | solution.py:537
  228.2 5.4 %convolution_add_fusion.1 = f32[148,6144]{1,0:T(8,128)S(1)} fusion(bf16[148,768]{1,0:T(8,128)(2,1)S(1)} %get-tuple-element.61, bf16[768,6144]{1,0:T(8,128)(2,1)} %held.3, bf16[148,6144]{1,0:T(8,128)(2,1)S(1)} %copy-done.19), kind=kOutput, calls=%fused_computation.1 | convolution fusion | flops 1398521856 | bytes 15120384 | tf_op jit(solution)/shard_map/dot_general | solution.py:197
  233.7 7.3 %convolution_add_fusion.mine = f32[148,6144]{1,0:T(8,128)} fusion(f32[148,6144]{1,0:T(8,128)S(1)} %convolution_add_fusion.1, bf16[148,768]{1,0:T(8,128)(2,1)S(1)} %collective-permute-done.6, bf16[768,6144]{1,0:T(8,128)(2,1)} %all-gather.3.cloned.1.call-done.got), kind=kOutput, calls=%fused_computation | convolution fusion | flops 1397612544 | bytes 16939008 | tf_op jit(solution)/shard_map/dot_general | solution.py:197
  241.0 46.9 %collective-permute-done.10.far = bf16[148,6144]{1,0:T(8,128)(2,1)} collective-permute-done((bf16[148,6144]{1,0:T(8,128)(2,1)}, bf16[148,6144]{1,0:T(8,128)(2,1)}, u32[]{:S(2)}, u32[]{:S(2)}) %collective-permute-start.10) | collective-permute-done | bytes 1818656 | tf_op jit(solution)/shard_map/ppermute | solution.py:537
  287.9 7.7 %finish.1 = (bf16[148,6144]{1,0:T(8,128)(2,1)}, bf16[2,74,512]{2,1,0:T(8,128)(2,1)}) custom-call(f32[148,6144]{1,0:T(8,128)} %convolution_add_fusion.mine, bf16[148,6144]{1,0:T(8,128)(2,1)} %collective-permute-done.8.edge, bf16[148,6144]{1,0:T(8,128)(2,1)} %collective-permute-done.10.far, bf16[148,6144]{1,0:T(8,128)(2,1)} %collective-permute-done.12.near, ...), custom_call_target="tpu_custom_call" | custom-call | tf_op jit(solution)/shard_map/finish/pallas_call | solution.py:423
  303.4 4.3 %collective-permute-done.18.refs_3_ = bf16[2,74,512]{2,1,0:T(8,128)(2,1)S(1)} collective-permute-done((bf16[2,74,512]{2,1,0:T(8,128)(2,1)}, bf16[2,74,512]{2,1,0:T(8,128)(2,1)S(1)}, u32[]{:S(2)}, u32[]{:S(2)}) %collective-permute-start.18) | collective-permute-done | bytes 151584 | tf_op jit(solution)/shard_map/ppermute | solution.py:481
  308.3 6.0 %joining.1 = bf16[2,74,256]{2,1,0:T(8,128)(2,1)} custom-call(s32[1]{0:T(128)} %bitcast.4.first, bf16[1,74,512]{2,1,0:T(8,128)(2,1)} %get-tuple-element.86.refs_0_, bf16[2,74,512]{2,1,0:T(8,128)(2,1)} %copy-done.30, bf16[2,74,512]{2,1,0:T(8,128)(2,1)} %get-tuple-element.73.refs_2_, bf16[2,74,512]{2,1,0:T(8,128)(2,1)} %copy-done.31, ...), custom_call_target="tpu_custom_call" | custom-call | tf_op jit(solution)/shard_map/joining/pallas_call | solution.py:490
  (127 shorter events, 47.9 us)
Async XLA Ops:
  7.2 100.3 %copy-start = (bf16[1536,512]{1,0:T(8,128)(2,1)S(1)}, bf16[1536,512]{1,0:T(8,128)(2,1)}, u32[]{:S(2)}) copy-start(bf16[1536,512]{1,0:T(8,128)(2,1)} %param.24) | copy-start | bytes 4718596
  7.2 190.3 %all-gather.3.cloned.1.call-start = ((), (), s32[]{:S(2)}) async-start(), calls=%async_computation | async-start | bytes 10616832 | tf_op jit(solution)/shard_map/all_gather | solution.py:576
  10.9 45.3 %collective-permute-start = (bf16[148,6144]{1,0:T(8,128)(2,1)}, bf16[148,6144]{1,0:T(8,128)(2,1)S(1)}, u32[]{:S(2)}, u32[]{:S(2)}) collective-permute-start(bf16[148,6144]{1,0:T(8,128)(2,1)} %normalized_rows.1.refs_0_), channel_id=1, source_target_pairs={{0,1},{1,2},{2,3},{4,5},{5,6},{6,7},{8,9},{9,10},{10,11},{12,13},{... | collective-permute-start | bytes 5455880 | tf_op jit(solution)/shard_map/ppermute | solution.py:537
  16.1 44.4 %collective-permute-start.1 = (bf16[148,6144]{1,0:T(8,128)(2,1)}, bf16[148,6144]{1,0:T(8,128)(2,1)}, u32[]{:S(2)}, u32[]{:S(2)}) collective-permute-start(bf16[148,6144]{1,0:T(8,128)(2,1)} %normalized_rows.1.refs_0_), channel_id=1, source_target_pairs={{1,0},{2,1},{3,2},{5,4},{6,5},{7,6},{9,8},{10,9},{11,10},{13,12},{... | collective-permute-start | bytes 5455880 | tf_op jit(solution)/shard_map/ppermute | solution.py:537
  60.5 31.5 %collective-permute-start.2 = (bf16[148,6144]{1,0:T(8,128)(2,1)S(1)}, bf16[148,6144]{1,0:T(8,128)(2,1)S(1)}, u32[]{:S(2)}, u32[]{:S(2)}) collective-permute-start(bf16[148,6144]{1,0:T(8,128)(2,1)S(1)} %collective-permute-done.refs_0_), channel_id=1, source_target_pairs={{1,2},{2,3},{5,6},{6,7},{9,10},{10,11},{13,14},{14,15},{17,18},{18... | collective-permute-start | bytes 5455880 | tf_op jit(solution)/shard_map/ppermute | solution.py:537
  61.2 45.6 %collective-permute-start.3 = (bf16[148,6144]{1,0:T(8,128)(2,1)}, bf16[148,6144]{1,0:T(8,128)(2,1)S(1)}, u32[]{:S(2)}, u32[]{:S(2)}) collective-permute-start(bf16[148,6144]{1,0:T(8,128)(2,1)} %collective-permute-done.1.refs_1_), channel_id=1, source_target_pairs={{2,1},{1,0},{6,5},{5,4},{10,9},{9,8},{14,13},{13,12},{18,17},{17,1... | collective-permute-start | bytes 5455880 | tf_op jit(solution)/shard_map/ppermute | solution.py:537
  64.9 42.5 %collective-permute-start.7 = (bf16[96,6144]{1,0:T(8,128)(2,1)}, bf16[96,6144]{1,0:T(8,128)(2,1)}, u32[]{:S(2)}, u32[]{:S(2)}) collective-permute-start(bf16[96,6144]{1,0:T(8,128)(2,1)} %constant_dynamic-slice_fusion.1), channel_id=1, source_target_pairs={{0,1},{3,2},{4,5},{7,6},{8,9},{11,10},{12,13},{15,14},{16,17},{19,... | collective-permute-start | bytes 3538952 | tf_op jit(solution)/shard_map/ppermute | solution.py:537
  107.4 133.6 %all-gather.5.cloned.1.call-start = ((), (), s32[]{:S(2)}) async-start(), calls=%async_computation.1 | async-start | bytes 7077888 | tf_op jit(solution)/shard_map/all_gather | solution.py:608
  107.5 6.8 %collective-permute-start.13 = (bf16[192,512]{1,0:T(8,128)(2,1)S(1)}, bf16[192,512]{1,0:T(8,128)(2,1)S(1)}, u32[]{:S(2)}, u32[]{:S(2)}) collective-permute-start(bf16[192,512]{1,0:T(8,128)(2,1)S(1)} %constant_dynamic-slice_fusion), channel_id=1, source_target_pairs={{0,1},{3,2},{4,5},{7,6},{8,9},{11,10},{12,13},{15,14},{16,17},{19,... | collective-permute-start | bytes 589832 | tf_op jit(solution)/shard_map/ppermute | solution.py:537
  111.3 20.4 %copy-start.20 = (bf16[148,4096]{1,0:T(8,128)(2,1)}, bf16[148,4096]{1,0:T(8,128)(2,1)S(1)}, u32[]{:S(2)}) copy-start(bf16[148,4096]{1,0:T(8,128)(2,1)S(1)} %slice.54.refs_0_) | copy-start | bytes 3637252
  111.4 18.9 %collective-permute-start.4 = (bf16[148,2048]{1,0:T(8,128)(2,1)S(1)}, bf16[148,2048]{1,0:T(8,128)(2,1)S(1)}, u32[]{:S(2)}, u32[]{:S(2)}) collective-permute-start(bf16[148,2048]{1,0:T(8,128)(2,1)S(1)} %slice.53.refs_0_), channel_id=1, source_target_pairs={{1,0},{2,3},{5,4},{6,7},{9,8},{10,11},{13,12},{14,15},{17,16},{18,... | collective-permute-start | bytes 1818632 | tf_op jit(solution)/shard_map/ppermute | solution.py:537
  112.7 44.4 %collective-permute-start.5 = (bf16[148,4096]{1,0:T(8,128)(2,1)S(1)}, bf16[148,4096]{1,0:T(8,128)(2,1)}, u32[]{:S(2)}, u32[]{:S(2)}) collective-permute-start(bf16[148,4096]{1,0:T(8,128)(2,1)S(1)} %slice.54.refs_0_), channel_id=1, source_target_pairs={{1,0},{2,3},{5,4},{6,7},{9,8},{10,11},{13,12},{14,15},{17,16},{18,... | collective-permute-start | bytes 3637256 | tf_op jit(solution)/shard_map/ppermute | solution.py:537
  114.4 0.7 collective-permute-start.14
  130.2 54.5 %collective-permute-start.15 = (bf16[3,192,512]{2,1,0:T(8,128)(2,1)}, bf16[3,192,512]{2,1,0:T(8,128)(2,1)S(1)}, u32[]{:S(2)}, u32[]{:S(2)}) collective-permute-start(bf16[3,192,512]{2,1,0:T(8,128)(2,1)} %pad_maximum_fusion.2), channel_id=1, source_target_pairs={{1,0},{2,3},{5,4},{6,7},{9,8},{10,11},{13,12},{14,15},{17,16},{18,... | collective-permute-start | bytes 1769480 | tf_op jit(solution)/shard_map/ppermute | solution.py:537
  186.2 23.4 %collective-permute-start.9 = (bf16[148,768]{1,0:T(8,128)(2,1)S(1)}, bf16[148,768]{1,0:T(8,128)(2,1)S(1)}, u32[]{:S(2)}, u32[]{:S(2)}) collective-permute-start(bf16[148,768]{1,0:T(8,128)(2,1)S(1)} %get-tuple-element.65.mine), channel_id=1, source_target_pairs={{0,1},{3,2},{4,5},{7,6},{8,9},{11,10},{12,13},{15,14},{16,17},{19,... | collective-permute-start | bytes 681992 | tf_op jit(solution)/shard_map/ppermute | solution.py:537
  187.6 9.9 %collective-permute-start.11 = (bf16[148,768]{1,0:T(8,128)(2,1)S(1)}, bf16[148,768]{1,0:T(8,128)(2,1)S(1)}, u32[]{:S(2)}, u32[]{:S(2)}) collective-permute-start(bf16[148,768]{1,0:T(8,128)(2,1)S(1)} %get-tuple-element.66.mine), channel_id=1, source_target_pairs={{0,1},{3,2},{4,5},{7,6},{8,9},{11,10},{12,13},{15,14},{16,17},{19,... | collective-permute-start | bytes 681992 | tf_op jit(solution)/shard_map/ppermute | solution.py:537
  196.2 44.8 %collective-permute-start.8 = (bf16[148,6144]{1,0:T(8,128)(2,1)}, bf16[148,6144]{1,0:T(8,128)(2,1)}, u32[]{:S(2)}, u32[]{:S(2)}) collective-permute-start(bf16[148,6144]{1,0:T(8,128)(2,1)} %convolution_convert_fusion), channel_id=1, source_target_pairs={{1,0},{2,3},{5,4},{6,7},{9,8},{10,11},{13,12},{14,15},{17,16},{18,... | collective-permute-start | bytes 5455880 | tf_op jit(solution)/shard_map/ppermute | solution.py:537
  207.6 20.6 %copy-start.19 = (bf16[148,6144]{1,0:T(8,128)(2,1)S(1)}, bf16[148,6144]{1,0:T(8,128)(2,1)}, u32[]{:S(2)}) copy-start(bf16[148,6144]{1,0:T(8,128)(2,1)} %tokens.1) | copy-start | bytes 5455876
  207.6 33.3 %collective-permute-start.12 = (bf16[148,6144]{1,0:T(8,128)(2,1)}, bf16[148,6144]{1,0:T(8,128)(2,1)}, u32[]{:S(2)}, u32[]{:S(2)}) collective-permute-start(bf16[148,6144]{1,0:T(8,128)(2,1)} %pair_sum.3), channel_id=1, source_target_pairs={{1,2},{2,1},{5,6},{6,5},{9,10},{10,9},{13,14},{14,13},{17,18},{18,... | collective-permute-start | bytes 5455880 | tf_op jit(solution)/shard_map/ppermute | solution.py:537
  219.9 68.0 %collective-permute-start.10 = (bf16[148,6144]{1,0:T(8,128)(2,1)}, bf16[148,6144]{1,0:T(8,128)(2,1)}, u32[]{:S(2)}, u32[]{:S(2)}) collective-permute-start(bf16[148,6144]{1,0:T(8,128)(2,1)} %pair_sum.2), channel_id=1, source_target_pairs={{1,3},{2,0},{5,7},{6,4},{9,11},{10,8},{13,15},{14,12},{17,19},{18,... | collective-permute-start | bytes 5455880 | tf_op jit(solution)/shard_map/ppermute | solution.py:537
  221.2 12.4 %collective-permute-start.6 = (bf16[148,768]{1,0:T(8,128)(2,1)S(1)}, bf16[148,768]{1,0:T(8,128)(2,1)S(1)}, u32[]{:S(2)}, u32[]{:S(2)}) collective-permute-start(bf16[148,768]{1,0:T(8,128)(2,1)S(1)} %get-tuple-element.62), channel_id=1, source_target_pairs={{0,1},{3,2},{4,5},{7,6},{8,9},{11,10},{12,13},{15,14},{16,17},{19,... | collective-permute-start | bytes 681992 | tf_op jit(solution)/shard_map/ppermute | solution.py:537
  296.5 5.4 %collective-permute-start.16 = (bf16[1,74,512]{2,1,0:T(8,128)(2,1)S(1)}, bf16[1,74,512]{2,1,0:T(8,128)(2,1)S(1)}, u32[]{:S(2)}, u32[]{:S(2)}) collective-permute-start(bf16[1,74,512]{2,1,0:T(8,128)(2,1)S(1)} %slice_select_fusion), channel_id=1, source_target_pairs={{0,2},{1,3},{2,0},{3,1},{4,6},{5,7},{6,4},{7,5},{8,10},{9,11},{10,... | collective-permute-start | bytes 227336 | tf_op jit(solution)/shard_map/ppermute | solution.py:481
  296.6 6.8 %collective-permute-start.17 = (bf16[2,74,512]{2,1,0:T(8,128)(2,1)}, bf16[2,74,512]{2,1,0:T(8,128)(2,1)S(1)}, u32[]{:S(2)}, u32[]{:S(2)}) collective-permute-start(bf16[2,74,512]{2,1,0:T(8,128)(2,1)} %get-tuple-element.73.refs_2_), channel_id=1, source_target_pairs={{0,1},{1,2},{2,3},{4,5},{5,6},{6,7},{8,9},{9,10},{10,11},{12,13},{... | collective-permute-start | bytes 454664 | tf_op jit(solution)/shard_map/ppermute | solution.py:481
  300.2 7.4 %collective-permute-start.18 = (bf16[2,74,512]{2,1,0:T(8,128)(2,1)}, bf16[2,74,512]{2,1,0:T(8,128)(2,1)S(1)}, u32[]{:S(2)}, u32[]{:S(2)}) collective-permute-start(bf16[2,74,512]{2,1,0:T(8,128)(2,1)} %get-tuple-element.73.refs_2_), channel_id=1, source_target_pairs={{1,0},{2,1},{3,2},{5,4},{6,5},{7,6},{9,8},{10,9},{11,10},{13,12},{... | collective-permute-start | bytes 454664 | tf_op jit(solution)/shard_map/ppermute | solution.py:481
  (33 other events, 228.7 us)
Sparse Core Ops, SparseCore 0:
  107.5 58.2 all-gather.2
  186.4 43.7 all-gather.4

commit v2 on v1

--- a/solution.py
+++ b/solution.py
@@ -219,11 +219,13 @@
     )(tokens)
 
 
-def project_kernel(count, given, final, *refs):
-    parts = refs[:count]
-    weights = refs[count : count + 3]
-    down, query_up, value_up, query_gain, key_gain = refs[count + 3 : count + 8]
-    refs = refs[count + 8 :]
+def project_kernel(count, cuts, given, final, *refs):
+    pieces = len(cuts) - 1
+    parts = refs[: count * pieces]
+    refs = refs[count * pieces :]
+    weights = refs[:3]
+    down, query_up, value_up, query_gain, key_gain = refs[3:8]
+    refs = refs[8:]
     earlier, refs = (refs[:2], refs[2:]) if given else (None, refs)
     outs, (totals, low) = refs[:-2], refs[-2:]
     step = pl.program_id(0)
@@ -232,17 +234,20 @@
     def _():
         for i in range(count):
             for j in range(3):
-                term = dot32(parts[i][...], weights[j][...])
+                term = dot32(parts[i * pieces][...], weights[j][...])
                 totals[i, j] = term + earlier[0][i, j] if given else term
-            term = dot32(parts[i][...], down[...])
+            term = dot32(parts[i * pieces][...], down[...])
             low[i] = term + earlier[1][i] if given else term
 
-    @pl.when(step > 0)
-    def _():
-        for i in range(count):
-            for j in range(3):
-                totals[i, j] += dot32(parts[i][...], weights[j][...])
-            low[i] += dot32(parts[i][...], down[...])
+    for p in range(pieces):
+
+        @pl.when((step >= max(cuts[p], 1)) & (step < cuts[p + 1]))
+        def _():
+            for i in range(count):
+                part = parts[i * pieces + p]
+                for j in range(3):
+                    totals[i, j] += dot32(part[...], weights[j][...])
+                low[i] += dot32(part[...], down[...])
 
     @pl.when(step == pl.num_programs(0) - 1)
     def _():
@@ -257,29 +262,35 @@
             key = totals[i, 1]
             for h in range(query.shape[1] // HEAD_DIM):
                 lanes = slice(h * HEAD_DIM, (h + 1) * HEAD_DIM)
-                outs[3 * i][:, lanes] = (
+                outs[i][0, :, lanes] = (
                     normalize(query[:, lanes]) * (query_gain[:, lanes] / math.sqrt(HEAD_DIM))
                 ).astype(bf16)
-                outs[3 * i + 1][:, lanes] = (
+                outs[i][1, :, lanes] = (
                     normalize(key[:, lanes]) * key_gain[:, lanes]
                 ).astype(bf16)
-            outs[3 * i + 2][...] = value.astype(bf16)
+            outs[i][2] = value.astype(bf16)
 
 
 def project(parts, weights, down, ups, gains, first=0, earlier=(), final=True):
     count = len(parts)
-    rows, features = parts[0].shape
+    rows = parts[0][0].shape[0]
     model_width, width = weights[0].shape
     depth = model_width // KEY_STEPS
+    cuts = [0]
+    for piece in parts[0]:
+        cuts.append(cuts[-1] + piece.shape[1] // depth)
     offset = first // depth
     rank = down.shape[1]
     whole = lambda *shape: pl.BlockSpec(shape, lambda k: (0,) * len(shape))
+    piece_spec = lambda p: pl.BlockSpec(
+        (rows, depth), lambda k: (0, jnp.clip(k - cuts[p], 0, cuts[p + 1] - cuts[p] - 1))
+    )
     sums = [(count, 3, rows, width), (count, rows, rank)]
-    results = [((rows, width), bf16)] * (3 * count) if final else [(x, f32) for x in sums]
+    results = [((3, rows, width), bf16)] * count if final else [(x, f32) for x in sums]
     result = pl.pallas_call(
-        functools.partial(project_kernel, count, len(earlier) > 0, final),
-        grid=(features // depth,),
-        in_specs=[pl.BlockSpec((rows, depth), lambda k: (0, k))] * count
+        functools.partial(project_kernel, count, cuts, len(earlier) > 0, final),
+        grid=(cuts[-1],),
+        in_specs=[piece_spec(p) for p in range(len(cuts) - 1)] * count
         + [pl.BlockSpec((depth, width), lambda k: (k + offset, 0))] * 3
         + [pl.BlockSpec((depth, rank), lambda k: (k + offset, 0))]
         + [whole(rank, width)] * 2
@@ -290,16 +301,14 @@
         scratch_shapes=[pltpu.VMEM(shape, f32) for shape in sums],
         compiler_params=pltpu.CompilerParams(vmem_limit_bytes=VMEM_LIMIT),
         name="project",
-    )(*parts, *weights, down, *ups, *gains, *earlier)
-    if not final:
-        return result
-    return [tuple(result[3 * i : 3 * i + 3]) for i in range(count)]
+    )(*(piece for block in parts for piece in block), *weights, down, *ups, *gains, *earlier)
+    return result
 
 
 def attention_kernel(rows, slot, place, *refs):
-    blocks = refs[:15]
-    outs = refs[15:19]
-    query, key, value = refs[19:]
+    blocks = refs[:5]
+    outs = refs[5:9]
+    query, key, value = refs[9:]
     where = place[0]
 
     @pl.when(pl.program_id(0) == 0)
@@ -313,7 +322,7 @@
                 value[h, i * slot : i * slot + rows, HEAD_DIM:] = ones
 
     for j in range(3):
-        own, before, after, two, last = (blocks[3 * i + j] for i in range(5))
+        own, before, after, two, last = (block.at[j] for block in blocks)
 
         def hold(i, ref):
             for h in range(HEADS_STEP):
@@ -349,50 +358,123 @@
 
 
 def attention(place, *qkv):
-    rows, width = qkv[0][0].shape
+    _, rows, width = qkv[0].shape
     slot = round_up(rows, 16)
     columns = HEADS_STEP * HEAD_DIM
-    block = pl.BlockSpec((rows, columns), lambda h: (0, h))
+    block = pl.BlockSpec((3, rows, columns), lambda h: (0, 0, h))
     return pl.pallas_call(
         functools.partial(attention_kernel, rows, slot),
         grid=(width // columns,),
-        in_specs=[pl.BlockSpec(memory_space=pltpu.SMEM)] + [block] * 15,
-        out_specs=[block] * 4,
+        in_specs=[pl.BlockSpec(memory_space=pltpu.SMEM)] + [block] * 5,
+        out_specs=[pl.BlockSpec((rows, columns), lambda h: (0, h))] * 4,
         out_shape=[jax.ShapeDtypeStruct((rows, width), bf16)] * 4,
         scratch_shapes=[
             pltpu.VMEM((HEADS_STEP, 4 * slot, HEAD_DIM), bf16),
             pltpu.VMEM((HEADS_STEP, 4 * slot, HEAD_DIM), bf16),
             pltpu.VMEM((HEADS_STEP, 4 * slot, 2 * HEAD_DIM), bf16),
         ],
-        compiler_params=pltpu.CompilerParams(vmem_limit_bytes=16 * 1024 * 1024),
+        compiler_params=pltpu.CompilerParams(vmem_limit_bytes=VMEM_LIMIT),
         name="attention",
-    )(place.reshape(1), *(x for block_qkv in qkv for x in block_qkv))
-
-
-def pair_kernel(mine, other, held, got, out):
-    out[...] = (dot32(mine[...], held[...]) + dot32(other[...], got[...])).astype(bf16)
-
-
-def pair_sum(mine, other, held, got):
+    )(place.reshape(1), *qkv)
+
+
+def own_sums_kernel(rows, slot, edge, mine, tokens, weight, edge_out, mine_out, held):
+    @pl.when(pl.program_id(0) == 0)
+    def _():
+        held[...] = jnp.zeros_like(held)
+        held[0:rows] = edge[...]
+        held[slot : slot + rows] = mine[...]
+
+    result = dot32(held[...], weight[...])
+    edge_out[...] = result[:rows].astype(bf16)
+    mine_out[...] = tokens[...].astype(f32) + result[slot : slot + rows]
+
+
+def own_sums(edge, mine, tokens, weight):
     rows, width = mine.shape
-    model_width = held.shape[1]
+    model_width = weight.shape[1]
+    slot = round_up(rows, 16)
     columns = model_width // PAIR_STEPS
-    weight = pl.BlockSpec((width, columns), lambda c: (0, c))
     operand = pl.BlockSpec((rows, width), lambda c: (0, 0))
+    block = pl.BlockSpec((rows, columns), lambda c: (0, c))
     return pl.pallas_call(
-        pair_kernel,
+        functools.partial(own_sums_kernel, rows, slot),
         grid=(PAIR_STEPS,),
-        in_specs=[operand, operand, weight, weight],
-        out_specs=pl.BlockSpec((rows, columns), lambda c: (0, c)),
-        out_shape=jax.ShapeDtypeStruct((rows, model_width), bf16),
+        in_specs=[operand] * 2 + [block, pl.BlockSpec((width, columns), lambda c: (0, c))],
+        out_specs=[block] * 2,
+        out_shape=[
+            jax.ShapeDtypeStruct((rows, model_width), bf16),
+            jax.ShapeDtypeStruct((rows, model_width), f32),
+        ],
+        scratch_shapes=[pltpu.VMEM((2 * slot, width), bf16)],
         compiler_params=pltpu.CompilerParams(vmem_limit_bytes=VMEM_LIMIT),
-        name="pair_sum",
-    )(mine, other, held, got)
-
-
-def finish_kernel(mine, edge, far, near, weight, layer_out, reassembled, total):
+        name="own_sums",
+    )(edge, mine, tokens, weight)
+
+
+def pair_sums_kernel(rows, slot, far, near, far_got, near_got, own, got, *refs):
+    far_out, near_out, held, held_got = refs
+
+    @pl.when(pl.program_id(0) == 0)
+    def _():
+        for ref, first, second in ((held, far, near), (held_got, far_got, near_got)):
+            ref[...] = jnp.zeros_like(ref)
+            ref[0:rows] = first[...]
+            ref[slot : slot + rows] = second[...]
+
+    result = dot32(held[...], own[...]) + dot32(held_got[...], got[...])
+    far_out[...] = result[:rows].astype(bf16)
+    near_out[...] = result[slot : slot + rows].astype(bf16)
+
+
+def pair_sums(far, near, far_got, near_got, own, got, half):
+    rows, width = far.shape
+    model_width = own.shape[1]
+    slot = round_up(rows, 16)
+    columns = model_width // PAIR_STEPS
+    steps = PAIR_STEPS // 2
+    operand = pl.BlockSpec((rows, width), lambda c: (0, 0))
+    weight = pl.BlockSpec((width, columns), lambda c: (0, c + half * steps))
+    block = pl.BlockSpec((rows, columns), lambda c: (0, c))
+    return pl.pallas_call(
+        functools.partial(pair_sums_kernel, rows, slot),
+        grid=(steps,),
+        in_specs=[operand] * 4 + [weight] * 2,
+        out_specs=[block] * 2,
+        out_shape=[jax.ShapeDtypeStruct((rows, model_width // 2), bf16)] * 2,
+        scratch_shapes=[pltpu.VMEM((2 * slot, width), bf16)] * 2,
+        compiler_params=pltpu.CompilerParams(vmem_limit_bytes=VMEM_LIMIT),
+        name="pair_sums",
+    )(far, near, far_got, near_got, own, got)
+
+
+def add_kernel(mine, other, weight, out):
+    out[...] = mine[...] + dot32(other[...], weight[...])
+
+
+def add_sums(mine, other, weight):
+    rows, width = other.shape
+    model_width = weight.shape[1]
+    columns = model_width // PAIR_STEPS
+    block = pl.BlockSpec((rows, columns), lambda c: (0, c))
+    return pl.pallas_call(
+        add_kernel,
+        grid=(PAIR_STEPS,),
+        in_specs=[
+            block,
+            pl.BlockSpec((rows, width), lambda c: (0, 0)),
+            pl.BlockSpec((width, columns), lambda c: (0, c)),
+        ],
+        out_specs=block,
+        out_shape=jax.ShapeDtypeStruct((rows, model_width), f32),
+        compiler_params=pltpu.CompilerParams(vmem_limit_bytes=VMEM_LIMIT),
+        name="add_sums",
+    )(mine, other, weight)
+
+
+def finish_kernel(half, mine, edge, far, near, weight, *refs):
+    layer_out, reassembled, total = refs[-3:]
     step = pl.program_id(0)
-    rows = reassembled.shape[1]
     layer = (
         mine[...] + edge[...].astype(f32) + far[...].astype(f32) + near[...].astype(f32)
     ).astype(bf16)
@@ -401,7 +483,7 @@
 
     @pl.when(step == 0)
     def _():
-        total[...] = term
+        total[...] = term + refs[0][...] if half else term
 
     @pl.when(step > 0)
     def _():
@@ -409,30 +491,39 @@
 
     @pl.when(step == pl.num_programs(0) - 1)
     def _():
-        for r in range(reassembled.shape[0]):
-            reassembled[r] = total[r * rows : (r + 1) * rows].astype(bf16)
-
-
-def finish(mine, edge, far, near, weight):
+        if half:
+            rows = reassembled.shape[1]
+            for r in range(reassembled.shape[0]):
+                reassembled[r] = total[r * rows : (r + 1) * rows].astype(bf16)
+        else:
+            reassembled[...] = total[...]
+
+
+def finish(mine, edge, far, near, weight, half, earlier=()):
     rows, model_width = mine.shape
     channels = weight.shape[1]
-    steps = FINISH_STEPS
-    depth = model_width // steps
+    depth = model_width // FINISH_STEPS
+    steps = FINISH_STEPS // 2
+    wide = pl.BlockSpec((rows, depth), lambda k: (0, k + half * steps))
     block = pl.BlockSpec((rows, depth), lambda k: (0, k))
-    shape = (rows // MAP_W, MAP_W, channels)
+    shape = (rows // MAP_W, MAP_W, channels) if half else (rows, channels)
+    whole = lambda *x: pl.BlockSpec(x, lambda k: (0,) * len(x))
     return pl.pallas_call(
-        finish_kernel,
+        functools.partial(finish_kernel, half),
         grid=(steps,),
-        in_specs=[block] * 4 + [pl.BlockSpec((depth, channels), lambda k: (k, 0))],
-        out_specs=[block, pl.BlockSpec(shape, lambda k: (0, 0, 0))],
+        in_specs=[wide, wide, block, block]
+        + [pl.BlockSpec((depth, channels), lambda k: (k + half * steps, 0))]
+        + ([whole(rows, channels), pl.BlockSpec(memory_space=pl.ANY)] if half else []),
+        out_specs=[wide, whole(*shape)],
         out_shape=[
             jax.ShapeDtypeStruct((rows, model_width), bf16),
-            jax.ShapeDtypeStruct(shape, bf16),
+            jax.ShapeDtypeStruct(shape, bf16 if half else f32),
         ],
         scratch_shapes=[pltpu.VMEM((rows, channels), f32)],
+        input_output_aliases={6: 0} if half else {},
         compiler_params=pltpu.CompilerParams(vmem_limit_bytes=VMEM_LIMIT),
         name="finish",
-    )(mine, edge, far, near, weight)
+    )(mine, edge, far, near, weight, *earlier)
 
 
 def joining_kernel_body(total_rows, pitch, first, *refs):
@@ -559,7 +650,7 @@
     (own,) = normalized_rows(tokens, (model_width,))
     up1 = send(own, [(0, 1), (1, 2), (2, 3)])
     down1 = send(own, [(1, 0), (2, 1), (3, 2)])
-    (own_heads,) = heads(own)
+    (own_heads,) = heads([own])
     share = heads_width // images
     piece = lax.dynamic_slice_in_dim(output_weight, image * share, share, 0)
     piece = send(after(piece, own_heads), inward)
@@ -570,28 +661,43 @@
     up1, down1 = after((up1, down1), own_heads)
     up2 = send(up1, [(1, 2), (2, 3)])
     down2 = send(down1, [(2, 1), (1, 0)])
-    before_heads, after_heads = heads(up1, down1)
+    before_heads, after_heads = heads([up1], [down1])
 
     two = after(up2 + down2, before_heads, after_heads)
     partner_weight = lax.all_gather(after(piece, two), "dp", axis=0, tiled=True)
     two = (two[:, :cut], two[:, cut:])
-    last = [send(part, outward) for part in two]
+    last = [send(two[0], outward)]
     small_two = send(after(jnp.stack([small, small_end]), up2, down2), [(1, 2), (2, 1)])
-    two_sums = heads(two[0], final=False)
-    (two_heads,) = heads(two[1], earlier=two_sums, **rest)
-    last_sums = heads(after(last[0], two_heads), final=False)
-    (last_heads,) = heads(last[1], earlier=last_sums, **rest)
+    two_sums = heads([two[0]], final=False)
+    last.append(send(after(two[1], two_sums), outward))
+    (two_heads,) = heads([two[1]], earlier=two_sums, **rest)
+    last_sums = heads([after(last[0], two_heads)], final=False)
+    (last_heads,) = heads([last[1]], earlier=last_sums, **rest)
+
+    three = jnp.stack([small, small_two[0], small_two[1]])
+    three = send(after(three, last_heads), outward)
 
     far, near, mine, edge = attention(
         place, own_heads, before_heads, after_heads, two_heads, last_heads
     )
     far_got = send(far, inward)
     near_got = send(near, inward)
-    mine_got = send(edge, inward)
+    edge_rows = edge
+    edge, mine = own_sums(edge, mine, tokens, output_weight)
+    far_got, near_got = after((far_got, near_got), edge)
+    edge = send(after(edge, far_got), outward)
+    parts = []
+    for half in range(2):
+        if half == 1:
+            far = after(far, sums)
+        sums = pair_sums(far, near, far_got, near_got, output_weight, partner_weight, half)
+        parts.append((send(sums[0], [(1, 3), (2, 0)]), send(sums[1], [(1, 2), (2, 1)])))
+        if half == 0:
+            mine_got = send(after(edge_rows, parts[0][0]), inward)
+    small, small_end, small_two, three = after((small, small_end, small_two, three), far_got)
+    mine = add_sums(mine, mine_got, partner_weight)
 
     held = jnp.stack([small, small_end, small_two[0], small_two[1]])
-    three = send(after(jnp.stack([small, small_two[0], small_two[1]]), last[1]), outward)
-    three, held = after((three, held), far)
     shares = jnp.where(
         place == 0,
         jnp.stack([small, three[0], three[1], three[2]]),
@@ -609,16 +715,8 @@
         model_width, reassemble_weight.shape[1]
     )
 
-    edge = dot32(edge, output_weight).astype(bf16)
-    edge = send(edge, outward)
-    far = pair_sum(far, far_got, output_weight, partner_weight)
-    far = send(far, [(1, 3), (2, 0)])
-    near = pair_sum(near, near_got, output_weight, partner_weight)
-    near = send(near, [(1, 2), (2, 1)])
-    mine = (
-        tokens.astype(f32) + dot32(mine, output_weight) + dot32(mine_got, partner_weight)
-    )
-    layer_out, reassembled = finish(mine, edge, far, near, reassemble_full)
+    layer_out, sums = finish(mine, edge, *parts[0], reassemble_full, 0)
+    layer_out, reassembled = finish(mine, edge, *parts[1], reassemble_full, 1, (sums, layer_out))
     joined_map = joining(
         reassembled, joining_kernel, opening_residual_kernel, closing_residual_kernel
     )

time: 324 us -> 308 us (0.951)
  matrix products: 19.8 us -> 0 us
  Pallas kernels: 115 us -> 129 us
  waiting for transfers between devices: 110 us -> 96.8 us
  starting transfers between devices: 44.3 us -> 48.9 us
    dot_general x3 -> x0, matrix products: 19.8 us -> none  [dot32(): return jnp.dot(a, b, preferred_element_type=f32)]
    ppermute x16 -> x18, waiting for transfers between devices: 105 us -> 91.3 us  [on_device_line(): send = lambda value, pairs: lax.ppermute(value, 'tensor', pairs)]
    pallas_call x9 -> x12, Pallas kernels: 99.9 us -> 112 us  [the longest x6 72.1 us: project(): pl.pallas_call(functools.partial(project_kernel, count, cuts, len(earlier...]
    ppermute x16 -> x18, starting transfers between devices: 39.2 us -> 41.3 us  [on_device_line(): send = lambda value, pairs: lax.ppermute(value, 'tensor', pairs)]
    unnamed x74 -> x44, local copies, waits for them, and re-layouts: 8.9 us -> 8.53 us
  transfers between devices with their start and end apart: 21 -> 23, of which waited for: 10 -> 10; matrix products, arithmetic and copies ran while one was open for 10% -> 4% of each run, Pallas kernels for 30% -> 37%
where the time goes in v2:
time: 308 us; the launch traced here: 307 us
  Pallas kernels  129 us (42%)
  waiting for transfers between devices  96.8 us (31%)
  starting transfers between devices  48.9 us (16%)
  local copies, waits for them, and re-layouts  14.6 us (5%)
  between operations  14.4 us (5%)
  other arithmetic  3.42 us (1%)
    ppermute x18, waiting for transfers between devices, on_device_line(): send = lambda value, pairs: lax.ppermute(value, 'tensor', pairs)  91.3 us
    pallas_call x6, Pallas kernels, project(): pl.pallas_call(functools.partial(project_kernel, count, cuts, len(earlier...  72.1 us
    ppermute x18, starting transfers between devices, on_device_line(): send = lambda value, pairs: lax.ppermute(value, 'tensor', pairs)  41.3 us
    pallas_call x2, Pallas kernels, pair_sums(): pl.pallas_call(functools.partial(pair_sums_kernel, rows, slot), grid=(ste...  14 us
    pallas_call x2, Pallas kernels, finish(): pl.pallas_call(functools.partial(finish_kernel, half), grid=(steps,), in_...  9.38 us
    pallas_call x1, Pallas kernels, own_sums(): pl.pallas_call(functools.partial(own_sums_kernel, rows, slot), grid=(PAIR...  8.63 us
    unnamed x44, local copies, waits for them, and re-layouts  8.53 us
    pallas_call x1, Pallas kernels, add_sums(): pl.pallas_call(add_kernel, grid=(PAIR_STEPS,), in_specs=[block, pl.BlockS...  7.79 us
  transfers between devices with their start and end apart: 23, of which 10 were waited for; matrix products, arithmetic and copies ran while one was open for 4% of the time, Pallas kernels for 37%

profile of v2, /device:TPU:0, one launch (start us, length us, event | category | flops | bytes accessed | tf_op | source)
XLA Modules:
  0.0 306.9 jit_solution(17529437524042728037)
XLA Ops:
  10.9 5.2 %collective-permute-start = (bf16[148,6144]{1,0:T(8,128)(2,1)}, bf16[148,6144]{1,0:T(8,128)(2,1)S(1)}, u32[]{:S(2)}, u32[]{:S(2)}) collective-permute-start(bf16[148,6144]{1,0:T(8,128)(2,1)} %normalized_rows.1.refs_0_), channel_id=1, source_target_pairs={{0,1},{1,2},{2,3},{4,5},{5,6},{6,7},{8,9},{9,10},{10,11},{12,13},{... | collective-permute-start | bytes 5455880 | tf_op jit(solution)/shard_map/ppermute | solution.py:628
  22.2 15.1 %project.6.refs_0_ = bf16[3,148,768]{2,1,0:T(8,128)(2,1)} custom-call(bf16[148,6144]{1,0:T(8,128)(2,1)} %normalized_rows.1.refs_0_, bf16[6144,768]{1,0:T(8,128)(2,1)} %refs_1_.9, bf16[6144,768]{1,0:T(8,128)(2,1)} %refs_2_.11, bf16[6144,768]{1,0:T(8,128)(2,1)} %refs_3_.11, bf16[6144,32]{1,0:T(8,128)(2,1)} %copy.17.refs_4_.refs_5_, ...), custom_call_target="tpu_custom_call" | custom-call | tf_op jit(solution)/shard_map/project/pallas_call | solution.py:290
  37.3 18.9 %collective-permute-done.refs_0_ = bf16[148,6144]{1,0:T(8,128)(2,1)S(1)} collective-permute-done((bf16[148,6144]{1,0:T(8,128)(2,1)}, bf16[148,6144]{1,0:T(8,128)(2,1)S(1)}, u32[]{:S(2)}, u32[]{:S(2)}) %collective-permute-start) | collective-permute-done | bytes 1818656 | tf_op jit(solution)/shard_map/ppermute | solution.py:628
  64.9 7.8 %collective-permute-start.8 = (bf16[96,6144]{1,0:T(8,128)(2,1)}, bf16[96,6144]{1,0:T(8,128)(2,1)}, u32[]{:S(2)}, u32[]{:S(2)}) collective-permute-start(bf16[96,6144]{1,0:T(8,128)(2,1)} %constant_dynamic-slice_fusion.1), channel_id=1, source_target_pairs={{0,1},{3,2},{4,5},{7,6},{8,9},{11,10},{12,13},{15,14},{16,17},{19,... | collective-permute-start | bytes 3538952 | tf_op jit(solution)/shard_map/ppermute | solution.py:628
  72.7 19.3 %project.7 = (bf16[3,148,768]{2,1,0:T(8,128)(2,1)}, bf16[3,148,768]{2,1,0:T(8,128)(2,1)}) custom-call(bf16[148,6144]{1,0:T(8,128)(2,1)} %copy-done.4, bf16[148,6144]{1,0:T(8,128)(2,1)} %collective-permute-done.1.refs_1_, bf16[6144,768]{1,0:T(8,128)(2,1)} %refs_1_.9, bf16[6144,768]{1,0:T(8,128)(2,1)} %refs_2_.11, bf16[6144,768]{1,0:T(8,128)(2,1)} %refs_3_.11, ...), custom_call_target="tpu_custom_call" | custom-call | tf_op jit(solution)/shard_map/project/pallas_call | solution.py:290
  92.0 14.8 %collective-permute-done.3 = bf16[148,6144]{1,0:T(8,128)(2,1)S(1)} collective-permute-done((bf16[148,6144]{1,0:T(8,128)(2,1)}, bf16[148,6144]{1,0:T(8,128)(2,1)S(1)}, u32[]{:S(2)}, u32[]{:S(2)}) %collective-permute-start.3) | collective-permute-done | bytes 1818656 | tf_op jit(solution)/shard_map/ppermute | solution.py:628
  109.9 5.8 %collective-permute-start.14 = (bf16[192,512]{1,0:T(8,128)(2,1)S(1)}, bf16[192,512]{1,0:T(8,128)(2,1)S(1)}, u32[]{:S(2)}, u32[]{:S(2)}) collective-permute-start(bf16[192,512]{1,0:T(8,128)(2,1)S(1)} %constant_dynamic-slice_fusion), channel_id=1, source_target_pairs={{0,1},{3,2},{4,5},{7,6},{8,9},{11,10},{12,13},{15,14},{16,17},{19,... | collective-permute-start | bytes 589832 | tf_op jit(solution)/shard_map/ppermute | solution.py:628
  115.8 11.2 %project.8 = (f32[1,3,148,768]{3,2,1,0:T(8,128)}, f32[1,148,32]{2,1,0:T(8,128)}) custom-call(bf16[148,4096]{1,0:T(8,128)(2,1)} %slice.36.refs_0_, bf16[6144,768]{1,0:T(8,128)(2,1)} %refs_1_.9, bf16[6144,768]{1,0:T(8,128)(2,1)} %refs_2_.11, bf16[6144,768]{1,0:T(8,128)(2,1)} %refs_3_.11, bf16[6144,32]{1,0:T(8,128)(2,1)} %copy.17.refs_4_.refs_5_, ...), custom_call_target="tpu_custom_call" | custom-call | tf_op jit(solution)/shard_map/project/pallas_call | solution.py:290
  129.1 7.8 %project.9.refs_3_ = bf16[3,148,768]{2,1,0:T(8,128)(2,1)} custom-call(bf16[148,2048]{1,0:T(8,128)(2,1)} %copy-done.3, bf16[6144,768]{1,0:T(8,128)(2,1)} %refs_1_.9, bf16[6144,768]{1,0:T(8,128)(2,1)} %refs_2_.11, bf16[6144,768]{1,0:T(8,128)(2,1)} %refs_3_.11, bf16[6144,32]{1,0:T(8,128)(2,1)} %copy.17.refs_4_.refs_5_, bf16[32,768]{1,0:T(8,128)(2,1)} %pad.8.refs_5_.refs_6_, ...), custom_call_target="tpu_custom_call" | custom-call | tf_op jit(solution)/shard_map/project/pallas_call | solution.py:290
  141.1 10.9 %project.10 = (f32[1,3,148,768]{3,2,1,0:T(8,128)}, f32[1,148,32]{2,1,0:T(8,128)}) custom-call(bf16[148,4096]{1,0:T(8,128)(2,1)} %collective-permute-done.5.refs_0_, bf16[6144,768]{1,0:T(8,128)(2,1)} %refs_1_.9, bf16[6144,768]{1,0:T(8,128)(2,1)} %refs_2_.11, bf16[6144,768]{1,0:T(8,128)(2,1)} %refs_3_.11, bf16[6144,32]{1,0:T(8,128)(2,1)} %copy.17.refs_4_.refs_5_, ...), custom_call_target="tpu_custom_call" | custom-call | tf_op jit(solution)/shard_map/project/pallas_call | solution.py:290
  152.9 7.8 %project.11.refs_4_ = bf16[3,148,768]{2,1,0:T(8,128)(2,1)} custom-call(bf16[148,2048]{1,0:T(8,128)(2,1)} %copy-done.12, bf16[6144,768]{1,0:T(8,128)(2,1)} %refs_1_.9, bf16[6144,768]{1,0:T(8,128)(2,1)} %refs_2_.11, bf16[6144,768]{1,0:T(8,128)(2,1)} %refs_3_.11, bf16[6144,32]{1,0:T(8,128)(2,1)} %copy.17.refs_4_.refs_5_, bf16[32,768]{1,0:T(8,128)(2,1)} %pad.8.refs_5_.refs_6_, ...), custom_call_target="tpu_custom_call" | custom-call | tf_op jit(solution)/shard_map/project/pallas_call | solution.py:290
  162.0 7.0 %attention.1 = (bf16[148,768]{1,0:T(8,128)(2,1)}, bf16[148,768]{1,0:T(8,128)(2,1)}, bf16[148,768]{1,0:T(8,128)(2,1)}, bf16[148,768]{1,0:T(8,128)(2,1)}) custom-call(s32[1]{0:T(128)} %bitcast.place, bf16[3,148,768]{2,1,0:T(8,128)(2,1)} %project.6.refs_0_, bf16[3,148,768]{2,1,0:T(8,128)(2,1)} %get-tuple-element.43.refs_1_, ...), custom_call_target="tpu_custom_call" | custom-call | tf_op jit(solution)/shard_map/attention/pallas_call | solution.py:365
  169.0 4.6 %collective-permute-start.6 = (bf16[148,768]{1,0:T(8,128)(2,1)}, bf16[148,768]{1,0:T(8,128)(2,1)S(1)}, u32[]{:S(2)}, u32[]{:S(2)}) collective-permute-start(bf16[148,768]{1,0:T(8,128)(2,1)} %get-tuple-element.66.far), channel_id=1, source_target_pairs={{0,1},{3,2},{4,5},{7,6},{8,9},{11,10},{12,13},{15,14},{16,17},{19,... | collective-permute-start | bytes 681992 | tf_op jit(solution)/shard_map/ppermute | solution.py:628
  175.2 8.6 %own_sums.1 = (bf16[148,6144]{1,0:T(8,128)(2,1)}, f32[148,6144]{1,0:T(8,128)}) custom-call(bf16[148,768]{1,0:T(8,128)(2,1)} %get-tuple-element.63.edge, bf16[148,768]{1,0:T(8,128)(2,1)} %get-tuple-element.53.mine, bf16[148,6144]{1,0:T(8,128)(2,1)} %tokens.3, bf16[768,6144]{1,0:T(8,128)(2,1)} %own.3), custom_call_target="tpu_custom_call" | custom-call | tf_op jit(solution)/shard_map/own_sums/pallas_call | solution.py:400
  187.6 7.0 %pair_sums.2 = (bf16[148,3072]{1,0:T(8,128)(2,1)}, bf16[148,3072]{1,0:T(8,128)(2,1)}) custom-call(bf16[148,768]{1,0:T(8,128)(2,1)} %get-tuple-element.66.far, bf16[148,768]{1,0:T(8,128)(2,1)} %get-tuple-element.56.near, bf16[148,768]{1,0:T(8,128)(2,1)} %copy-done.6, bf16[148,768]{1,0:T(8,128)(2,1)} %copy-done.7, bf16[768,6144]{1,0:T(8,128)(2,1)} %own.3, ...), custom_call_target="tpu_custom_call" | custom-call | tf_op jit(solution)/shard_map/pair_sums/pallas_call | solution.py:439
  197.6 7.0 %pair_sums.3 = (bf16[148,3072]{1,0:T(8,128)(2,1)}, bf16[148,3072]{1,0:T(8,128)(2,1)}) custom-call(bf16[148,768]{1,0:T(8,128)(2,1)} %get-tuple-element.66.far, bf16[148,768]{1,0:T(8,128)(2,1)} %get-tuple-element.56.near, bf16[148,768]{1,0:T(8,128)(2,1)} %copy-done.6, bf16[148,768]{1,0:T(8,128)(2,1)} %copy-done.7, bf16[768,6144]{1,0:T(8,128)(2,1)} %own.3, ...), custom_call_target="tpu_custom_call" | custom-call | tf_op jit(solution)/shard_map/pair_sums/pallas_call | solution.py:439
  207.5 13.7 %collective-permute-done.9.far = bf16[148,3072]{1,0:T(8,128)(2,1)S(1)} collective-permute-done((bf16[148,3072]{1,0:T(8,128)(2,1)}, bf16[148,3072]{1,0:T(8,128)(2,1)S(1)}, u32[]{:S(2)}, u32[]{:S(2)}) %collective-permute-start.9) | collective-permute-done | bytes 909344 | tf_op jit(solution)/shard_map/ppermute | solution.py:628
  226.7 7.8 %add_sums.1.mine = f32[148,6144]{1,0:T(8,128)} custom-call(f32[148,6144]{1,0:T(8,128)} %get-tuple-element.54.mine, bf16[148,768]{1,0:T(8,128)(2,1)} %copy-done.14, bf16[768,6144]{1,0:T(8,128)(2,1)} %all-gather.3.cloned.1.call-done.got.weight), custom_call_target="tpu_custom_call" | custom-call | tf_op jit(solution)/shard_map/add_sums/pallas_call | solution.py:460
  234.5 32.0 %collective-permute-done.11.edge = bf16[148,6144]{1,0:T(8,128)(2,1)S(1)} collective-permute-done((bf16[148,6144]{1,0:T(8,128)(2,1)}, bf16[148,6144]{1,0:T(8,128)(2,1)S(1)}, u32[]{:S(2)}, u32[]{:S(2)}) %collective-permute-start.11) | collective-permute-done | bytes 1818656 | tf_op jit(solution)/shard_map/ppermute | solution.py:628
  267.8 4.7 %finish.2 = (bf16[148,6144]{1,0:T(8,128)(2,1)}, f32[148,512]{1,0:T(8,128)}) custom-call(f32[148,6144]{1,0:T(8,128)} %add_sums.1.mine, bf16[148,6144]{1,0:T(8,128)(2,1)} %copy-done.2, bf16[148,3072]{1,0:T(8,128)(2,1)} %copy-done.5, bf16[148,3072]{1,0:T(8,128)(2,1)} %collective-permute-done.17.near, bf16[6144,512]{1,0:T(8,128)(2,1)} %bitcast.8), custom_call_target="tpu_custom_call" | custom-call | tf_op jit(solution)/shard_map/finish/pallas_call | solution.py:511
  272.4 4.7 %finish.3 = (bf16[148,6144]{1,0:T(8,128)(2,1)}, bf16[2,74,512]{2,1,0:T(8,128)(2,1)}) custom-call(f32[148,6144]{1,0:T(8,128)} %add_sums.1.mine, bf16[148,6144]{1,0:T(8,128)(2,1)} %copy-done.2, bf16[148,3072]{1,0:T(8,128)(2,1)} %collective-permute-done.12.far, bf16[148,3072]{1,0:T(8,128)(2,1)} %collective-permute-done.13.near, ...), custom_call_target="tpu_custom_call", output_to_operand_aliasing={{0}: (6, {})} | custom-call | tf_op jit(solution)/shard_map/finish/pallas_call | solution.py:511
  278.1 5.0 %collective-permute-start.18 = (bf16[1,74,512]{2,1,0:T(8,128)(2,1)S(1)}, bf16[1,74,512]{2,1,0:T(8,128)(2,1)S(1)}, u32[]{:S(2)}, u32[]{:S(2)}) collective-permute-start(bf16[1,74,512]{2,1,0:T(8,128)(2,1)S(1)} %slice_select_fusion), channel_id=1, source_target_pairs={{0,2},{1,3},{2,0},{3,1},{4,6},{5,7},{6,4},{7,5},{8,10},{9,11},{10,... | collective-permute-start | bytes 227336 | tf_op jit(solution)/shard_map/ppermute | solution.py:572
  287.5 4.3 %collective-permute-done.20.refs_3_ = bf16[2,74,512]{2,1,0:T(8,128)(2,1)S(1)} collective-permute-done((bf16[2,74,512]{2,1,0:T(8,128)(2,1)}, bf16[2,74,512]{2,1,0:T(8,128)(2,1)S(1)}, u32[]{:S(2)}, u32[]{:S(2)}) %collective-permute-start.20) | collective-permute-done | bytes 151584 | tf_op jit(solution)/shard_map/ppermute | solution.py:572
  292.4 6.0 %joining.1 = bf16[2,74,256]{2,1,0:T(8,128)(2,1)} custom-call(s32[1]{0:T(128)} %bitcast.6.first, bf16[1,74,512]{2,1,0:T(8,128)(2,1)} %get-tuple-element.88.refs_0_, bf16[2,74,512]{2,1,0:T(8,128)(2,1)} %copy-done.15, bf16[2,74,512]{2,1,0:T(8,128)(2,1)} %get-tuple-element.79.refs_2_, bf16[2,74,512]{2,1,0:T(8,128)(2,1)} %copy-done.16, ...), custom_call_target="tpu_custom_call" | custom-call | tf_op jit(solution)/shard_map/joining/pallas_call | solution.py:581
  (99 shorter events, 55.4 us)
Async XLA Ops:
  7.2 102.7 %copy-start = (bf16[1536,512]{1,0:T(8,128)(2,1)S(1)}, bf16[1536,512]{1,0:T(8,128)(2,1)}, u32[]{:S(2)}) copy-start(bf16[1536,512]{1,0:T(8,128)(2,1)} %param.24) | copy-start | bytes 4718596
  7.2 180.4 %all-gather.3.cloned.1.call-start = ((), (), s32[]{:S(2)}) async-start(), calls=%async_computation | async-start | bytes 10616832 | tf_op jit(solution)/shard_map/all_gather | solution.py:667
  10.9 45.3 %collective-permute-start = (bf16[148,6144]{1,0:T(8,128)(2,1)}, bf16[148,6144]{1,0:T(8,128)(2,1)S(1)}, u32[]{:S(2)}, u32[]{:S(2)}) collective-permute-start(bf16[148,6144]{1,0:T(8,128)(2,1)} %normalized_rows.1.refs_0_), channel_id=1, source_target_pairs={{0,1},{1,2},{2,3},{4,5},{5,6},{6,7},{8,9},{9,10},{10,11},{12,13},{... | collective-permute-start | bytes 5455880 | tf_op jit(solution)/shard_map/ppermute | solution.py:628
  16.1 44.4 %collective-permute-start.1 = (bf16[148,6144]{1,0:T(8,128)(2,1)}, bf16[148,6144]{1,0:T(8,128)(2,1)}, u32[]{:S(2)}, u32[]{:S(2)}) collective-permute-start(bf16[148,6144]{1,0:T(8,128)(2,1)} %normalized_rows.1.refs_0_), channel_id=1, source_target_pairs={{1,0},{2,1},{3,2},{5,4},{6,5},{7,6},{9,8},{10,9},{11,10},{13,12},{... | collective-permute-start | bytes 5455880 | tf_op jit(solution)/shard_map/ppermute | solution.py:628
  60.5 31.6 %collective-permute-start.2 = (bf16[148,6144]{1,0:T(8,128)(2,1)S(1)}, bf16[148,6144]{1,0:T(8,128)(2,1)S(1)}, u32[]{:S(2)}, u32[]{:S(2)}) collective-permute-start(bf16[148,6144]{1,0:T(8,128)(2,1)S(1)} %collective-permute-done.refs_0_), channel_id=1, source_target_pairs={{1,2},{2,3},{5,6},{6,7},{9,10},{10,11},{13,14},{14,15},{17,18},{18... | collective-permute-start | bytes 5455880 | tf_op jit(solution)/shard_map/ppermute | solution.py:628
  61.2 45.6 %collective-permute-start.3 = (bf16[148,6144]{1,0:T(8,128)(2,1)}, bf16[148,6144]{1,0:T(8,128)(2,1)S(1)}, u32[]{:S(2)}, u32[]{:S(2)}) collective-permute-start(bf16[148,6144]{1,0:T(8,128)(2,1)} %collective-permute-done.1.refs_1_), channel_id=1, source_target_pairs={{2,1},{1,0},{6,5},{5,4},{10,9},{9,8},{14,13},{13,12},{18,17},{17,1... | collective-permute-start | bytes 5455880 | tf_op jit(solution)/shard_map/ppermute | solution.py:628
  64.9 42.5 %collective-permute-start.8 = (bf16[96,6144]{1,0:T(8,128)(2,1)}, bf16[96,6144]{1,0:T(8,128)(2,1)}, u32[]{:S(2)}, u32[]{:S(2)}) collective-permute-start(bf16[96,6144]{1,0:T(8,128)(2,1)} %constant_dynamic-slice_fusion.1), channel_id=1, source_target_pairs={{0,1},{3,2},{4,5},{7,6},{8,9},{11,10},{12,13},{15,14},{16,17},{19,... | collective-permute-start | bytes 3538952 | tf_op jit(solution)/shard_map/ppermute | solution.py:628
  107.4 159.1 %all-gather.5.cloned.1.call-start = ((), (), s32[]{:S(2)}) async-start(), calls=%async_computation.1 | async-start | bytes 7077888 | tf_op jit(solution)/shard_map/all_gather | solution.py:714
  108.6 32.5 %collective-permute-start.5 = (bf16[148,4096]{1,0:T(8,128)(2,1)}, bf16[148,4096]{1,0:T(8,128)(2,1)}, u32[]{:S(2)}, u32[]{:S(2)}) collective-permute-start(bf16[148,4096]{1,0:T(8,128)(2,1)} %slice.36.refs_0_), channel_id=1, source_target_pairs={{1,0},{2,3},{5,4},{6,7},{9,8},{10,11},{13,12},{14,15},{17,16},{18,... | collective-permute-start | bytes 3637256 | tf_op jit(solution)/shard_map/ppermute | solution.py:628
  109.9 18.4 %collective-permute-start.14 = (bf16[192,512]{1,0:T(8,128)(2,1)S(1)}, bf16[192,512]{1,0:T(8,128)(2,1)S(1)}, u32[]{:S(2)}, u32[]{:S(2)}) collective-permute-start(bf16[192,512]{1,0:T(8,128)(2,1)S(1)} %constant_dynamic-slice_fusion), channel_id=1, source_target_pairs={{0,1},{3,2},{4,5},{7,6},{8,9},{11,10},{12,13},{15,14},{16,17},{19,... | collective-permute-start | bytes 589832 | tf_op jit(solution)/shard_map/ppermute | solution.py:628
  127.0 25.0 %collective-permute-start.4 = (bf16[148,2048]{1,0:T(8,128)(2,1)S(1)}, bf16[148,2048]{1,0:T(8,128)(2,1)S(1)}, u32[]{:S(2)}, u32[]{:S(2)}) collective-permute-start(bf16[148,2048]{1,0:T(8,128)(2,1)S(1)} %slice.35.refs_0_), channel_id=1, source_target_pairs={{1,0},{2,3},{5,4},{6,7},{9,8},{10,11},{13,12},{14,15},{17,16},{18,... | collective-permute-start | bytes 1818632 | tf_op jit(solution)/shard_map/ppermute | solution.py:628
  128.4 8.5 %collective-permute-start.15 = (bf16[2,192,512]{2,1,0:T(8,128)(2,1)S(1)}, bf16[2,192,512]{2,1,0:T(8,128)(2,1)S(1)}, u32[]{:S(2)}, u32[]{:S(2)}) collective-permute-start(bf16[2,192,512]{2,1,0:T(8,128)(2,1)S(1)} %pad_maximum_fusion.1), channel_id=1, source_target_pairs={{1,2},{2,1},{5,6},{6,5},{9,10},{10,9},{13,14},{14,13},{17,18},{18,... | collective-permute-start | bytes 1179656 | tf_op jit(solution)/shard_map/ppermute | solution.py:628
  160.7 23.1 %collective-permute-start.16 = (bf16[3,192,512]{2,1,0:T(8,128)(2,1)S(1)}, bf16[3,192,512]{2,1,0:T(8,128)(2,1)S(1)}, u32[]{:S(2)}, u32[]{:S(2)}) collective-permute-start(bf16[3,192,512]{2,1,0:T(8,128)(2,1)S(1)} %pad_maximum_fusion), channel_id=1, source_target_pairs={{1,0},{2,3},{5,4},{6,7},{9,8},{10,11},{13,12},{14,15},{17,16},{18,... | collective-permute-start | bytes 1769480 | tf_op jit(solution)/shard_map/ppermute | solution.py:628
  169.0 14.8 %collective-permute-start.6 = (bf16[148,768]{1,0:T(8,128)(2,1)}, bf16[148,768]{1,0:T(8,128)(2,1)S(1)}, u32[]{:S(2)}, u32[]{:S(2)}) collective-permute-start(bf16[148,768]{1,0:T(8,128)(2,1)} %get-tuple-element.66.far), channel_id=1, source_target_pairs={{0,1},{3,2},{4,5},{7,6},{8,9},{11,10},{12,13},{15,14},{16,17},{19,... | collective-permute-start | bytes 681992 | tf_op jit(solution)/shard_map/ppermute | solution.py:628
  173.6 10.2 %collective-permute-start.7 = (bf16[148,768]{1,0:T(8,128)(2,1)}, bf16[148,768]{1,0:T(8,128)(2,1)S(1)}, u32[]{:S(2)}, u32[]{:S(2)}) collective-permute-start(bf16[148,768]{1,0:T(8,128)(2,1)} %get-tuple-element.56.near), channel_id=1, source_target_pairs={{0,1},{3,2},{4,5},{7,6},{8,9},{11,10},{12,13},{15,14},{16,17},{19,... | collective-permute-start | bytes 681992 | tf_op jit(solution)/shard_map/ppermute | solution.py:628
  186.2 80.3 %collective-permute-start.11 = (bf16[148,6144]{1,0:T(8,128)(2,1)}, bf16[148,6144]{1,0:T(8,128)(2,1)S(1)}, u32[]{:S(2)}, u32[]{:S(2)}) collective-permute-start(bf16[148,6144]{1,0:T(8,128)(2,1)} %get-tuple-element.64), channel_id=1, source_target_pairs={{1,0},{2,3},{5,4},{6,7},{9,8},{10,11},{13,12},{14,15},{17,16},{18,... | collective-permute-start | bytes 5455880 | tf_op jit(solution)/shard_map/ppermute | solution.py:628
  194.6 26.6 %collective-permute-start.9 = (bf16[148,3072]{1,0:T(8,128)(2,1)}, bf16[148,3072]{1,0:T(8,128)(2,1)S(1)}, u32[]{:S(2)}, u32[]{:S(2)}) collective-permute-start(bf16[148,3072]{1,0:T(8,128)(2,1)} %get-tuple-element.62), channel_id=1, source_target_pairs={{1,3},{2,0},{5,7},{6,4},{9,11},{10,8},{13,15},{14,12},{17,19},{18,... | collective-permute-start | bytes 2727944 | tf_op jit(solution)/shard_map/ppermute | solution.py:628
  195.9 70.7 %collective-permute-start.17 = (bf16[148,3072]{1,0:T(8,128)(2,1)}, bf16[148,3072]{1,0:T(8,128)(2,1)}, u32[]{:S(2)}, u32[]{:S(2)}) collective-permute-start(bf16[148,3072]{1,0:T(8,128)(2,1)} %get-tuple-element.65), channel_id=1, source_target_pairs={{1,2},{2,1},{5,6},{6,5},{9,10},{10,9},{13,14},{14,13},{17,18},{18,... | collective-permute-start | bytes 2727944 | tf_op jit(solution)/shard_map/ppermute | solution.py:628
  204.6 67.8 %collective-permute-start.12 = (bf16[148,3072]{1,0:T(8,128)(2,1)}, bf16[148,3072]{1,0:T(8,128)(2,1)}, u32[]{:S(2)}, u32[]{:S(2)}) collective-permute-start(bf16[148,3072]{1,0:T(8,128)(2,1)} %get-tuple-element.67), channel_id=1, source_target_pairs={{1,3},{2,0},{5,7},{6,4},{9,11},{10,8},{13,15},{14,12},{17,19},{18,... | collective-permute-start | bytes 2727944 | tf_op jit(solution)/shard_map/ppermute | solution.py:628
  205.9 66.5 %collective-permute-start.13 = (bf16[148,3072]{1,0:T(8,128)(2,1)}, bf16[148,3072]{1,0:T(8,128)(2,1)}, u32[]{:S(2)}, u32[]{:S(2)}) collective-permute-start(bf16[148,3072]{1,0:T(8,128)(2,1)} %get-tuple-element.68), channel_id=1, source_target_pairs={{1,2},{2,1},{5,6},{6,5},{9,10},{10,9},{13,14},{14,13},{17,18},{18,... | collective-permute-start | bytes 2727944 | tf_op jit(solution)/shard_map/ppermute | solution.py:628
  221.2 4.9 %collective-permute-start.10 = (bf16[148,768]{1,0:T(8,128)(2,1)S(1)}, bf16[148,768]{1,0:T(8,128)(2,1)S(1)}, u32[]{:S(2)}, u32[]{:S(2)}) collective-permute-start(bf16[148,768]{1,0:T(8,128)(2,1)S(1)} %copy-done.13), channel_id=1, source_target_pairs={{0,1},{3,2},{4,5},{7,6},{8,9},{11,10},{12,13},{15,14},{16,17},{19,... | collective-permute-start | bytes 681992 | tf_op jit(solution)/shard_map/ppermute | solution.py:628
  278.1 8.3 %collective-permute-start.18 = (bf16[1,74,512]{2,1,0:T(8,128)(2,1)S(1)}, bf16[1,74,512]{2,1,0:T(8,128)(2,1)S(1)}, u32[]{:S(2)}, u32[]{:S(2)}) collective-permute-start(bf16[1,74,512]{2,1,0:T(8,128)(2,1)S(1)} %slice_select_fusion), channel_id=1, source_target_pairs={{0,2},{1,3},{2,0},{3,1},{4,6},{5,7},{6,4},{7,5},{8,10},{9,11},{10,... | collective-permute-start | bytes 227336 | tf_op jit(solution)/shard_map/ppermute | solution.py:572
  283.1 4.4 %collective-permute-start.19 = (bf16[2,74,512]{2,1,0:T(8,128)(2,1)}, bf16[2,74,512]{2,1,0:T(8,128)(2,1)S(1)}, u32[]{:S(2)}, u32[]{:S(2)}) collective-permute-start(bf16[2,74,512]{2,1,0:T(8,128)(2,1)} %get-tuple-element.79.refs_2_), channel_id=1, source_target_pairs={{0,1},{1,2},{2,3},{4,5},{5,6},{6,7},{8,9},{9,10},{10,11},{12,13},{... | collective-permute-start | bytes 454664 | tf_op jit(solution)/shard_map/ppermute | solution.py:572
  284.4 7.4 %collective-permute-start.20 = (bf16[2,74,512]{2,1,0:T(8,128)(2,1)}, bf16[2,74,512]{2,1,0:T(8,128)(2,1)S(1)}, u32[]{:S(2)}, u32[]{:S(2)}) collective-permute-start(bf16[2,74,512]{2,1,0:T(8,128)(2,1)} %get-tuple-element.79.refs_2_), channel_id=1, source_target_pairs={{1,0},{2,1},{3,2},{5,4},{6,5},{7,6},{9,8},{10,9},{11,10},{13,12},{... | collective-permute-start | bytes 454664 | tf_op jit(solution)/shard_map/ppermute | solution.py:572
  (20 other events, 154.4 us)
Sparse Core Ops, SparseCore 0:
  107.5 58.1 all-gather.2
  186.4 43.8 all-gather.4

commit v3 on v2

--- a/solution.py
+++ b/solution.py
@@ -183,6 +183,7 @@
 KEY_STEPS = 6
 FINISH_STEPS = 4
 PAIR_STEPS = 4
+EDGE_STEPS = 4
 HEADS_STEP = 2
 LAST_STEPS = 2
 ROW_BLOCK = 80
@@ -378,38 +379,26 @@
     )(place.reshape(1), *qkv)
 
 
-def own_sums_kernel(rows, slot, edge, mine, tokens, weight, edge_out, mine_out, held):
-    @pl.when(pl.program_id(0) == 0)
-    def _():
-        held[...] = jnp.zeros_like(held)
-        held[0:rows] = edge[...]
-        held[slot : slot + rows] = mine[...]
-
-    result = dot32(held[...], weight[...])
-    edge_out[...] = result[:rows].astype(bf16)
-    mine_out[...] = tokens[...].astype(f32) + result[slot : slot + rows]
-
-
-def own_sums(edge, mine, tokens, weight):
-    rows, width = mine.shape
+def edge_kernel(edge, weight, out):
+    out[...] = dot32(edge[...], weight[...]).astype(bf16)
+
+
+def edge_sums(edge, weight):
+    rows, width = edge.shape
     model_width = weight.shape[1]
-    slot = round_up(rows, 16)
-    columns = model_width // PAIR_STEPS
-    operand = pl.BlockSpec((rows, width), lambda c: (0, 0))
-    block = pl.BlockSpec((rows, columns), lambda c: (0, c))
+    columns = model_width // EDGE_STEPS
     return pl.pallas_call(
-        functools.partial(own_sums_kernel, rows, slot),
-        grid=(PAIR_STEPS,),
-        in_specs=[operand] * 2 + [block, pl.BlockSpec((width, columns), lambda c: (0, c))],
-        out_specs=[block] * 2,
-        out_shape=[
-            jax.ShapeDtypeStruct((rows, model_width), bf16),
-            jax.ShapeDtypeStruct((rows, model_width), f32),
+        edge_kernel,
+        grid=(EDGE_STEPS,),
+        in_specs=[
+            pl.BlockSpec((rows, width), lambda c: (0, 0)),
+            pl.BlockSpec((width, columns), lambda c: (0, c)),
         ],
-        scratch_shapes=[pltpu.VMEM((2 * slot, width), bf16)],
+        out_specs=pl.BlockSpec((rows, columns), lambda c: (0, c)),
+        out_shape=jax.ShapeDtypeStruct((rows, model_width), bf16),
         compiler_params=pltpu.CompilerParams(vmem_limit_bytes=VMEM_LIMIT),
-        name="own_sums",
-    )(edge, mine, tokens, weight)
+        name="edge_sums",
+    )(edge, weight)
 
 
 def pair_sums_kernel(rows, slot, far, near, far_got, near_got, own, got, *refs):
@@ -448,32 +437,35 @@
     )(far, near, far_got, near_got, own, got)
 
 
-def add_kernel(mine, other, weight, out):
-    out[...] = mine[...] + dot32(other[...], weight[...])
-
-
-def add_sums(mine, other, weight):
-    rows, width = other.shape
-    model_width = weight.shape[1]
+def own_kernel(tokens, mine, other, own, got, out):
+    out[...] = tokens[...].astype(f32) + (
+        dot32(mine[...], own[...]) + dot32(other[...], got[...])
+    )
+
+
+def own_sums(tokens, mine, other, own, got):
+    rows, width = mine.shape
+    model_width = own.shape[1]
     columns = model_width // PAIR_STEPS
+    operand = pl.BlockSpec((rows, width), lambda c: (0, 0))
+    weight = pl.BlockSpec((width, columns), lambda c: (0, c))
     block = pl.BlockSpec((rows, columns), lambda c: (0, c))
     return pl.pallas_call(
-        add_kernel,
+        own_kernel,
         grid=(PAIR_STEPS,),
-        in_specs=[
-            block,
-            pl.BlockSpec((rows, width), lambda c: (0, 0)),
-            pl.BlockSpec((width, columns), lambda c: (0, c)),
-        ],
+        in_specs=[block, operand, operand, weight, weight],
         out_specs=block,
         out_shape=jax.ShapeDtypeStruct((rows, model_width), f32),
         compiler_params=pltpu.CompilerParams(vmem_limit_bytes=VMEM_LIMIT),
-        name="add_sums",
-    )(mine, other, weight)
+        name="own_sums",
+    )(tokens, mine, other, own, got)
 
 
 def finish_kernel(half, mine, edge, far, near, weight, *refs):
-    layer_out, reassembled, total = refs[-3:]
+    if half:
+        place, earlier, _, layer_out, reassembled, far_row, total = refs
+    else:
+        layer_out, reassembled, total = refs
     step = pl.program_id(0)
     layer = (
         mine[...] + edge[...].astype(f32) + far[...].astype(f32) + near[...].astype(f32)
@@ -483,7 +475,7 @@
 
     @pl.when(step == 0)
     def _():
-        total[...] = term + refs[0][...] if half else term
+        total[...] = term + earlier[...] if half else term
 
     @pl.when(step > 0)
     def _():
@@ -493,8 +485,10 @@
     def _():
         if half:
             rows = reassembled.shape[1]
-            for r in range(reassembled.shape[0]):
+            count = reassembled.shape[0]
+            for r in range(count):
                 reassembled[r] = total[r * rows : (r + 1) * rows].astype(bf16)
+            far_row[0] = jnp.where(place[0] < 2, reassembled[count - 1], reassembled[0])
         else:
             reassembled[...] = total[...]
 
@@ -506,102 +500,113 @@
     steps = FINISH_STEPS // 2
     wide = pl.BlockSpec((rows, depth), lambda k: (0, k + half * steps))
     block = pl.BlockSpec((rows, depth), lambda k: (0, k))
-    shape = (rows // MAP_W, MAP_W, channels) if half else (rows, channels)
+    shapes = [(rows // MAP_W, MAP_W, channels), (1, MAP_W, channels)] if half else [(rows, channels)]
     whole = lambda *x: pl.BlockSpec(x, lambda k: (0,) * len(x))
     return pl.pallas_call(
         functools.partial(finish_kernel, half),
         grid=(steps,),
         in_specs=[wide, wide, block, block]
         + [pl.BlockSpec((depth, channels), lambda k: (k + half * steps, 0))]
-        + ([whole(rows, channels), pl.BlockSpec(memory_space=pl.ANY)] if half else []),
-        out_specs=[wide, whole(*shape)],
-        out_shape=[
-            jax.ShapeDtypeStruct((rows, model_width), bf16),
-            jax.ShapeDtypeStruct(shape, bf16 if half else f32),
-        ],
+        + (
+            [
+                pl.BlockSpec(memory_space=pltpu.SMEM),
+                whole(rows, channels),
+                pl.BlockSpec(memory_space=pl.ANY),
+            ]
+            if half
+            else []
+        ),
+        out_specs=[wide] + [whole(*x) for x in shapes],
+        out_shape=[jax.ShapeDtypeStruct((rows, model_width), bf16)]
+        + [jax.ShapeDtypeStruct(x, bf16 if half else f32) for x in shapes],
         scratch_shapes=[pltpu.VMEM((rows, channels), f32)],
-        input_output_aliases={6: 0} if half else {},
+        input_output_aliases={7: 0} if half else {},
         compiler_params=pltpu.CompilerParams(vmem_limit_bytes=VMEM_LIMIT),
         name="finish",
     )(mine, edge, far, near, weight, *earlier)
 
 
-def joining_kernel_body(total_rows, pitch, first, *refs):
-    pieces = refs[:5]
-    joining, opening, closing, out, field, feature, inner = refs[5:]
+def joining_kernel_body(total_rows, pitch, place, above_far, above, middle, below, below_far, *refs):
+    joining, opening, closing, out, field, feature, inner = refs[:7]
+    kernels, semaphores = refs[7:10], refs[10]
+    copies = [
+        pltpu.make_async_copy(joining.at[a], kernels[0].at[a], semaphores.at[a]) for a in range(3)
+    ]
+    copies.append(pltpu.make_async_copy(opening, kernels[1], semaphores.at[3]))
+    copies.append(pltpu.make_async_copy(closing, kernels[2], semaphores.at[4]))
+    for copy in copies:
+        copy.start()
+
+    rows = middle.shape[0]
     field[...] = jnp.zeros_like(field)
-    place = 0
-    for piece in pieces:
+    begin = 0
+    for piece in (above_far, above, middle, below, below_far):
         for r in range(piece.shape[0]):
-            field[place * pitch : place * pitch + MAP_W] = piece[r]
-            place += 1
-
-    def conv(source, kernel):
+            field[begin : begin + MAP_W] = piece[r]
+            begin += pitch
+
+    def conv(source, kernel, waits):
         size = source.shape[0] - 2 * pitch
-        sums = []
-        for b in range(3):
-            running = None
-            for a in range(3):
-                term = dot32(source[a * pitch : a * pitch + size], kernel[a, b])
-                running = term if running is None else running + term
-            sums.append(running)
+        sums = [None] * 3
+        for a in range(3):
+            for copy in waits[a]:
+                copy.wait()
+            window = source[a * pitch : a * pitch + size]
+            for b in range(3):
+                term = dot32(window, kernel[a, b])
+                sums[b] = term if sums[b] is None else sums[b] + term
         return sums[1] + pltpu.roll(sums[0], 1, 0) + pltpu.roll(sums[2], size - 1, 0)
 
     def masked(values, margin):
         size, channels = values.shape
         shape = (size // pitch, pitch, channels)
-        row = lax.broadcasted_iota(jnp.int32, shape, 0) + (first[0] - margin)
+        row = lax.broadcasted_iota(jnp.int32, shape, 0) + (place[0] * rows - margin)
         column = lax.broadcasted_iota(jnp.int32, shape, 1)
         keep = (row >= 0) & (row < total_rows) & (column < MAP_W)
         return jnp.where(keep, values.reshape(shape), 0.0).reshape(size, channels)
 
-    feature[...] = masked(conv(field, joining), 2).astype(bf16)
+    waits = [[copy] for copy in copies[:3]]
+    feature[...] = masked(conv(field, kernels[0], waits), 2).astype(bf16)
     rectified = jnp.maximum(feature[...], 0)
-    inner[...] = masked(jax.nn.relu(conv(rectified, opening)), 1).astype(bf16)
-    rows = out.shape[0]
-    result = conv(inner, closing) + feature[2 * pitch : (2 + rows) * pitch].astype(f32)
-    for r in range(rows):
-        out[r] = result[r * pitch : r * pitch + MAP_W].astype(bf16)
-
-
-def joining(reassembled, joining_weight, opening_weight, closing_weight):
+    opened = conv(rectified, kernels[1], [[copies[3]], [], []])
+    inner[...] = masked(jax.nn.relu(opened), 1).astype(bf16)
+    result = conv(inner, kernels[2], [[copies[4]], [], []])
+    result += feature[2 * pitch : (2 + rows) * pitch].astype(f32)
+    strips = [result[r * pitch : r * pitch + MAP_W] for r in range(rows)]
+    out[...] = jnp.stack(strips, axis=1).astype(bf16)
+
+
+def joining(reassembled, far_row, joining_weight, opening_weight, closing_weight):
     count = lax.axis_size("tensor")
-    place = lax.axis_index("tensor")
+    place = lax.axis_index("tensor").astype(jnp.int32)
     rows, _, channels = reassembled.shape
     features = joining_weight.shape[3]
     send = lambda value, pairs: lax.ppermute(value, "tensor", pairs)
     above = send(reassembled, [(i, i + 1) for i in range(count - 1)])
     below = send(reassembled, [(i + 1, i) for i in range(count - 1)])
-    edge = jnp.where(place < 2, reassembled[rows - 1 :], reassembled[:1])
-    edge = send(edge, [(0, 2), (1, 3), (2, 0), (3, 1)])
-    above_far = jnp.where(place >= 2, edge, 0)
-    below_far = jnp.where(place < 2, edge, 0)
+    far_row = send(far_row, [(0, 2), (1, 3), (2, 0), (3, 1)])
+    above_far = jnp.where(place >= 2, far_row, 0)
+    below_far = jnp.where(place < 2, far_row, 0)
     pitch = round_up(MAP_W + 1, 16)
-    first = (place * rows).astype(jnp.int32).reshape(1)
-    return pl.pallas_call(
+    weights = (joining_weight, opening_weight, closing_weight)
+    result = pl.pallas_call(
         functools.partial(joining_kernel_body, count * rows, pitch),
         in_specs=[pl.BlockSpec(memory_space=pltpu.SMEM)]
-        + [pl.BlockSpec(memory_space=pltpu.VMEM)] * 8,
+        + [pl.BlockSpec(memory_space=pltpu.VMEM)] * 5
+        + [pl.BlockSpec(memory_space=pl.ANY)] * 3,
         out_specs=pl.BlockSpec(memory_space=pltpu.VMEM),
-        out_shape=jax.ShapeDtypeStruct((rows, MAP_W, features), bf16),
+        out_shape=jax.ShapeDtypeStruct((MAP_W, rows, features), bf16),
         scratch_shapes=[
             pltpu.VMEM(((rows + 6) * pitch, channels), bf16),
             pltpu.VMEM(((rows + 4) * pitch, features), bf16),
             pltpu.VMEM(((rows + 2) * pitch, features), bf16),
-        ],
+        ]
+        + [pltpu.VMEM(weight.shape, bf16) for weight in weights]
+        + [pltpu.SemaphoreType.DMA((5,))],
         compiler_params=pltpu.CompilerParams(vmem_limit_bytes=VMEM_LIMIT),
         name="joining",
-    )(
-        first,
-        above_far,
-        above,
-        reassembled,
-        below,
-        below_far,
-        joining_weight,
-        opening_weight,
-        closing_weight,
-    )
+    )(place.reshape(1), above_far, above, reassembled, below, below_far, *weights)
+    return jnp.transpose(result, (1, 0, 2))
 
 
 def on_device_line(
@@ -661,19 +666,21 @@
     up1, down1 = after((up1, down1), own_heads)
     up2 = send(up1, [(1, 2), (2, 3)])
     down2 = send(down1, [(2, 1), (1, 0)])
+    up1, down1 = after((up1, down1), small_end)
     before_heads, after_heads = heads([up1], [down1])
 
-    two = after(up2 + down2, before_heads, after_heads)
-    partner_weight = lax.all_gather(after(piece, two), "dp", axis=0, tiled=True)
-    two = (two[:, :cut], two[:, cut:])
+    two = up2[:, :cut] + down2[:, :cut]
+    two = [after(two, before_heads, after_heads)]
     last = [send(two[0], outward)]
-    small_two = send(after(jnp.stack([small, small_end]), up2, down2), [(1, 2), (2, 1)])
+    partner_weight = lax.all_gather(after(piece, two[0]), "dp", axis=0, tiled=True)
+    small_two = send(after(jnp.stack([small, small_end]), two[0]), [(1, 2), (2, 1)])
     two_sums = heads([two[0]], final=False)
-    last.append(send(after(two[1], two_sums), outward))
+    up2, down2 = after((up2, down2), two_sums)
+    two.append(up2[:, cut:] + down2[:, cut:])
+    last.append(send(two[1], outward))
     (two_heads,) = heads([two[1]], earlier=two_sums, **rest)
     last_sums = heads([after(last[0], two_heads)], final=False)
     (last_heads,) = heads([last[1]], earlier=last_sums, **rest)
-
     three = jnp.stack([small, small_two[0], small_two[1]])
     three = send(after(three, last_heads), outward)
 
@@ -683,7 +690,7 @@
     far_got = send(far, inward)
     near_got = send(near, inward)
     edge_rows = edge
-    edge, mine = own_sums(edge, mine, tokens, output_weight)
+    edge = edge_sums(edge, output_weight)
     far_got, near_got = after((far_got, near_got), edge)
     edge = send(after(edge, far_got), outward)
     parts = []
@@ -695,7 +702,7 @@
         if half == 0:
             mine_got = send(after(edge_rows, parts[0][0]), inward)
     small, small_end, small_two, three = after((small, small_end, small_two, three), far_got)
-    mine = add_sums(mine, mine_got, partner_weight)
+    mine = own_sums(tokens, mine, mine_got, output_weight, partner_weight)
 
     held = jnp.stack([small, small_end, small_two[0], small_two[1]])
     shares = jnp.where(
@@ -716,9 +723,11 @@
     )
 
     layer_out, sums = finish(mine, edge, *parts[0], reassemble_full, 0)
-    layer_out, reassembled = finish(mine, edge, *parts[1], reassemble_full, 1, (sums, layer_out))
+    layer_out, reassembled, far_row = finish(
+        mine, edge, *parts[1], reassemble_full, 1, (place.reshape(1), sums, layer_out)
+    )
     joined_map = joining(
-        reassembled, joining_kernel, opening_residual_kernel, closing_residual_kernel
+        reassembled, far_row, joining_kernel, opening_residual_kernel, closing_residual_kernel
     )
     return (layer_out, joined_map)
 

time: 308 us -> 304 us (0.987)
  waiting for transfers between devices: 96.8 us -> 90.7 us
  starting transfers between devices: 48.9 us -> 44.3 us
  other arithmetic: 3.42 us -> 7.4 us
    ppermute x18, waiting for transfers between devices: 91.3 us -> 85.2 us  [on_device_line(): send = lambda value, pairs: lax.ppermute(value, 'tensor', pairs)]
    ppermute x18, starting transfers between devices: 41.3 us -> 37.7 us  [on_device_line(): send = lambda value, pairs: lax.ppermute(value, 'tensor', pairs)]
    unnamed x44 -> x43, local copies, waits for them, and re-layouts: 8.53 us -> 10.4 us
  transfers between devices with their start and end apart: 23 -> 23, of which waited for: 10 -> 11; matrix products, arithmetic and copies ran while one was open for 4% -> 5% of each run, Pallas kernels for 37% -> 38%
where the time goes in v3:
time: 304 us; the launch traced here: 303 us
  Pallas kernels  131 us (43%)
  waiting for transfers between devices  90.7 us (30%)
  starting transfers between devices  44.3 us (15%)
  local copies, waits for them, and re-layouts  15 us (5%)
  between operations  14.4 us (5%)
  other arithmetic  7.4 us (2%)
    ppermute x18, waiting for transfers between devices, on_device_line(): send = lambda value, pairs: lax.ppermute(value, 'tensor', pairs)  85.2 us
    pallas_call x6, Pallas kernels, project(): pl.pallas_call(functools.partial(project_kernel, count, cuts, len(earlier...  72.8 us
    ppermute x18, starting transfers between devices, on_device_line(): send = lambda value, pairs: lax.ppermute(value, 'tensor', pairs)  37.7 us
    pallas_call x2, Pallas kernels, pair_sums(): pl.pallas_call(functools.partial(pair_sums_kernel, rows, slot), grid=(ste...  14.3 us
    pallas_call x1, Pallas kernels, own_sums(): pl.pallas_call(own_kernel, grid=(PAIR_STEPS,), in_specs=[block, operand,...  11.1 us
    unnamed x43, local copies, waits for them, and re-layouts  10.4 us
    pallas_call x2, Pallas kernels, finish(): pl.pallas_call(functools.partial(finish_kernel, half), grid=(steps,), in_...  9.41 us
    pallas_call x1, Pallas kernels, attention(): pl.pallas_call(functools.partial(attention_kernel, rows, slot), grid=(wid...  7.05 us
  transfers between devices with their start and end apart: 23, of which 11 were waited for; matrix products, arithmetic and copies ran while one was open for 5% of the time, Pallas kernels for 38%

profile of v3, /device:TPU:0, one launch (start us, length us, event | category | flops | bytes accessed | tf_op | source)
XLA Modules:
  0.0 302.8 jit_solution(6940418447149588163)
XLA Ops:
  7.2 3.6 %normalized_rows.1.refs_0_ = bf16[148,6144]{1,0:T(8,128)(2,1)} custom-call(bf16[148,6144]{1,0:T(8,128)(2,1)} %tokens.3), custom_call_target="tpu_custom_call" | custom-call | tf_op jit(solution)/shard_map/normalized_rows/pallas_call | solution.py:212
  10.9 5.2 %collective-permute-start = (bf16[148,6144]{1,0:T(8,128)(2,1)}, bf16[148,6144]{1,0:T(8,128)(2,1)S(1)}, u32[]{:S(2)}, u32[]{:S(2)}) collective-permute-start(bf16[148,6144]{1,0:T(8,128)(2,1)} %normalized_rows.1.refs_0_), channel_id=1, source_target_pairs={{0,1},{1,2},{2,3},{4,5},{5,6},{6,7},{8,9},{9,10},{10,11},{12,13},{... | collective-permute-start | bytes 5455880 | tf_op jit(solution)/shard_map/ppermute | solution.py:633
  22.3 15.1 %project.6.refs_0_ = bf16[3,148,768]{2,1,0:T(8,128)(2,1)} custom-call(bf16[148,6144]{1,0:T(8,128)(2,1)} %normalized_rows.1.refs_0_, bf16[6144,768]{1,0:T(8,128)(2,1)} %refs_1_.10, bf16[6144,768]{1,0:T(8,128)(2,1)} %refs_2_.12, bf16[6144,768]{1,0:T(8,128)(2,1)} %refs_3_.11, bf16[6144,32]{1,0:T(8,128)(2,1)} %copy.17.refs_4_.refs_5_, ...), custom_call_target="tpu_custom_call" | custom-call | tf_op jit(solution)/shard_map/project/pallas_call | solution.py:291
  37.4 18.9 %collective-permute-done.refs_0_ = bf16[148,6144]{1,0:T(8,128)(2,1)S(1)} collective-permute-done((bf16[148,6144]{1,0:T(8,128)(2,1)}, bf16[148,6144]{1,0:T(8,128)(2,1)S(1)}, u32[]{:S(2)}, u32[]{:S(2)}) %collective-permute-start) | collective-permute-done | bytes 1818656 | tf_op jit(solution)/shard_map/ppermute | solution.py:633
  63.3 7.5 %collective-permute-start.2 = (bf16[192,512]{1,0:T(8,128)(2,1)}, bf16[192,512]{1,0:T(8,128)(2,1)}, u32[]{:S(2)}, u32[]{:S(2)}) collective-permute-start(bf16[192,512]{1,0:T(8,128)(2,1)} %constant_dynamic-slice_fusion.1), channel_id=1, source_target_pairs={{0,1},{3,2},{4,5},{7,6},{8,9},{11,10},{12,13},{15,14},{16,17},{19,... | collective-permute-start | bytes 589832 | tf_op jit(solution)/shard_map/ppermute | solution.py:633
  75.2 19.2 %project.7 = (bf16[3,148,768]{2,1,0:T(8,128)(2,1)}, bf16[3,148,768]{2,1,0:T(8,128)(2,1)}) custom-call(bf16[148,6144]{1,0:T(8,128)(2,1)} %copy-done.6, bf16[148,6144]{1,0:T(8,128)(2,1)} %collective-permute-done.1.refs_1_, bf16[6144,768]{1,0:T(8,128)(2,1)} %refs_1_.10, bf16[6144,768]{1,0:T(8,128)(2,1)} %refs_2_.12, bf16[6144,768]{1,0:T(8,128)(2,1)} %refs_3_.11, ...), custom_call_target="tpu_custom_call" | custom-call | tf_op jit(solution)/shard_map/project/pallas_call | solution.py:291
  95.7 11.3 %collective-permute-done.4 = bf16[148,6144]{1,0:T(8,128)(2,1)} collective-permute-done((bf16[148,6144]{1,0:T(8,128)(2,1)}, bf16[148,6144]{1,0:T(8,128)(2,1)}, u32[]{:S(2)}, u32[]{:S(2)}) %collective-permute-start.4) | collective-permute-done | bytes 1818656 | tf_op jit(solution)/shard_map/ppermute | solution.py:633
  110.4 11.8 %project.8 = (f32[1,3,148,768]{3,2,1,0:T(8,128)}, f32[1,148,32]{2,1,0:T(8,128)}) custom-call(bf16[148,4096]{1,0:T(8,128)(2,1)} %copy-done.3, bf16[6144,768]{1,0:T(8,128)(2,1)} %refs_1_.10, bf16[6144,768]{1,0:T(8,128)(2,1)} %refs_2_.12, bf16[6144,768]{1,0:T(8,128)(2,1)} %refs_3_.11, bf16[6144,32]{1,0:T(8,128)(2,1)} %copy.17.refs_4_.refs_5_, ...), custom_call_target="tpu_custom_call" | custom-call | tf_op jit(solution)/shard_map/project/pallas_call | solution.py:291
  126.5 7.9 %project.9.refs_3_ = bf16[3,148,768]{2,1,0:T(8,128)(2,1)} custom-call(bf16[148,2048]{1,0:T(8,128)(2,1)} %copy-done.4, bf16[6144,768]{1,0:T(8,128)(2,1)} %refs_1_.10, bf16[6144,768]{1,0:T(8,128)(2,1)} %refs_2_.12, bf16[6144,768]{1,0:T(8,128)(2,1)} %refs_3_.11, bf16[6144,32]{1,0:T(8,128)(2,1)} %copy.17.refs_4_.refs_5_, bf16[32,768]{1,0:T(8,128)(2,1)} %pad.8.refs_5_.refs_6_, ...), custom_call_target="tpu_custom_call" | custom-call | tf_op jit(solution)/shard_map/project/pallas_call | solution.py:291
  134.4 6.7 %collective-permute-done.6.refs_0_ = bf16[148,4096]{1,0:T(8,128)(2,1)S(1)} collective-permute-done((bf16[148,4096]{1,0:T(8,128)(2,1)S(1)}, bf16[148,4096]{1,0:T(8,128)(2,1)S(1)}, u32[]{:S(2)}, u32[]{:S(2)}) %collective-permute-start.6) | collective-permute-done | bytes 1212448 | tf_op jit(solution)/shard_map/ppermute | solution.py:633
  142.1 11.0 %project.10 = (f32[1,3,148,768]{3,2,1,0:T(8,128)}, f32[1,148,32]{2,1,0:T(8,128)}) custom-call(bf16[148,4096]{1,0:T(8,128)(2,1)} %copy-done.7, bf16[6144,768]{1,0:T(8,128)(2,1)} %refs_1_.10, bf16[6144,768]{1,0:T(8,128)(2,1)} %refs_2_.12, bf16[6144,768]{1,0:T(8,128)(2,1)} %refs_3_.11, bf16[6144,32]{1,0:T(8,128)(2,1)} %copy.17.refs_4_.refs_5_, ...), custom_call_target="tpu_custom_call" | custom-call | tf_op jit(solution)/shard_map/project/pallas_call | solution.py:291
  154.0 7.8 %project.11.refs_4_ = bf16[3,148,768]{2,1,0:T(8,128)(2,1)} custom-call(bf16[148,2048]{1,0:T(8,128)(2,1)} %copy-done.12, bf16[6144,768]{1,0:T(8,128)(2,1)} %refs_1_.10, bf16[6144,768]{1,0:T(8,128)(2,1)} %refs_2_.12, bf16[6144,768]{1,0:T(8,128)(2,1)} %refs_3_.11, bf16[6144,32]{1,0:T(8,128)(2,1)} %copy.17.refs_4_.refs_5_, bf16[32,768]{1,0:T(8,128)(2,1)} %pad.8.refs_5_.refs_6_, ...), custom_call_target="tpu_custom_call" | custom-call | tf_op jit(solution)/shard_map/project/pallas_call | solution.py:291
  163.1 7.1 %attention.1 = (bf16[148,768]{1,0:T(8,128)(2,1)}, bf16[148,768]{1,0:T(8,128)(2,1)}, bf16[148,768]{1,0:T(8,128)(2,1)}, bf16[148,768]{1,0:T(8,128)(2,1)}) custom-call(s32[1]{0:T(128)} %bitcast.place.refs_0_, bf16[3,148,768]{2,1,0:T(8,128)(2,1)} %project.6.refs_0_, bf16[3,148,768]{2,1,0:T(8,128)(2,1)} %get-tuple-element.48.refs_1_, ...), custom_call_target="tpu_custom_call" | custom-call | tf_op jit(solution)/shard_map/attention/pallas_call | solution.py:366
  170.1 4.6 %collective-permute-start.7 = (bf16[148,768]{1,0:T(8,128)(2,1)}, bf16[148,768]{1,0:T(8,128)(2,1)S(1)}, u32[]{:S(2)}, u32[]{:S(2)}) collective-permute-start(bf16[148,768]{1,0:T(8,128)(2,1)} %get-tuple-element.70.far), channel_id=1, source_target_pairs={{0,1},{3,2},{4,5},{7,6},{8,9},{11,10},{12,13},{15,14},{16,17},{19,... | collective-permute-start | bytes 681992 | tf_op jit(solution)/shard_map/ppermute | solution.py:633
  176.3 6.4 %edge_sums.1 = bf16[148,6144]{1,0:T(8,128)(2,1)} custom-call(bf16[148,768]{1,0:T(8,128)(2,1)} %get-tuple-element.67.edge, bf16[768,6144]{1,0:T(8,128)(2,1)} %own.5), custom_call_target="tpu_custom_call" | custom-call | tf_op jit(solution)/shard_map/edge_sums/pallas_call | solution.py:390
  186.7 7.2 %pair_sums.2 = (bf16[148,3072]{1,0:T(8,128)(2,1)}, bf16[148,3072]{1,0:T(8,128)(2,1)}) custom-call(bf16[148,768]{1,0:T(8,128)(2,1)} %get-tuple-element.70.far, bf16[148,768]{1,0:T(8,128)(2,1)} %get-tuple-element.61.near, bf16[148,768]{1,0:T(8,128)(2,1)} %copy-done.10, bf16[148,768]{1,0:T(8,128)(2,1)} %copy-done.11, bf16[768,6144]{1,0:T(8,128)(2,1)} %own.5, ...), custom_call_target="tpu_custom_call" | custom-call | tf_op jit(solution)/shard_map/pair_sums/pallas_call | solution.py:428
  197.0 7.1 %pair_sums.3 = (bf16[148,3072]{1,0:T(8,128)(2,1)}, bf16[148,3072]{1,0:T(8,128)(2,1)}) custom-call(bf16[148,768]{1,0:T(8,128)(2,1)} %get-tuple-element.70.far, bf16[148,768]{1,0:T(8,128)(2,1)} %get-tuple-element.61.near, bf16[148,768]{1,0:T(8,128)(2,1)} %copy-done.10, bf16[148,768]{1,0:T(8,128)(2,1)} %copy-done.11, bf16[768,6144]{1,0:T(8,128)(2,1)} %own.5, ...), custom_call_target="tpu_custom_call" | custom-call | tf_op jit(solution)/shard_map/pair_sums/pallas_call | solution.py:428
  207.0 13.6 %collective-permute-done.10.far = bf16[148,3072]{1,0:T(8,128)(2,1)S(1)} collective-permute-done((bf16[148,3072]{1,0:T(8,128)(2,1)}, bf16[148,3072]{1,0:T(8,128)(2,1)S(1)}, u32[]{:S(2)}, u32[]{:S(2)}) %collective-permute-start.10) | collective-permute-done | bytes 909344 | tf_op jit(solution)/shard_map/ppermute | solution.py:633
  226.1 11.1 %own_sums.1.mine = f32[148,6144]{1,0:T(8,128)} custom-call(bf16[148,6144]{1,0:T(8,128)(2,1)} %tokens.3, bf16[148,768]{1,0:T(8,128)(2,1)} %get-tuple-element.58.mine, bf16[148,768]{1,0:T(8,128)(2,1)} %copy-done.14, bf16[768,6144]{1,0:T(8,128)(2,1)} %own.5, bf16[768,6144]{1,0:T(8,128)(2,1)} %all-gather.3.cloned.1.call-done.got), custom_call_target="tpu_custom_call" | custom-call | tf_op jit(solution)/shard_map/own_sums/pallas_call | solution.py:453
  237.1 27.5 %collective-permute-done.12.edge = bf16[148,6144]{1,0:T(8,128)(2,1)S(1)} collective-permute-done((bf16[148,6144]{1,0:T(8,128)(2,1)}, bf16[148,6144]{1,0:T(8,128)(2,1)S(1)}, u32[]{:S(2)}, u32[]{:S(2)}) %collective-permute-start.12) | collective-permute-done | bytes 1818656 | tf_op jit(solution)/shard_map/ppermute | solution.py:633
  265.9 4.7 %finish.2 = (bf16[148,6144]{1,0:T(8,128)(2,1)}, f32[148,512]{1,0:T(8,128)}) custom-call(f32[148,6144]{1,0:T(8,128)} %own_sums.1.mine, bf16[148,6144]{1,0:T(8,128)(2,1)} %copy-done.2, bf16[148,3072]{1,0:T(8,128)(2,1)} %copy-done.9, bf16[148,3072]{1,0:T(8,128)(2,1)} %collective-permute-done.17.near, bf16[6144,512]{1,0:T(8,128)(2,1)} %bitcast.8), custom_call_target="tpu_custom_call" | custom-call | tf_op jit(solution)/shard_map/finish/pallas_call | solution.py:505
  271.5 4.7 %finish.3 = (bf16[148,6144]{1,0:T(8,128)(2,1)}, bf16[2,74,512]{2,1,0:T(8,128)(2,1)}, bf16[1,74,512]{2,1,0:T(8,128)(2,1)}) custom-call(f32[148,6144]{1,0:T(8,128)} %own_sums.1.mine, bf16[148,6144]{1,0:T(8,128)(2,1)} %copy-done.2, bf16[148,3072]{1,0:T(8,128)(2,1)} %copy-done.8, ...), custom_call_target="tpu_custom_call", output_to_operand_aliasing={{0}: (7, {})} | custom-call | tf_op jit(solution)/shard_map/finish/pallas_call | solution.py:505
  284.6 4.3 %collective-permute-done.20.below = bf16[2,74,512]{2,1,0:T(8,128)(2,1)S(1)} collective-permute-done((bf16[2,74,512]{2,1,0:T(8,128)(2,1)}, bf16[2,74,512]{2,1,0:T(8,128)(2,1)S(1)}, u32[]{:S(2)}, u32[]{:S(2)}) %collective-permute-start.20) | collective-permute-done | bytes 151584 | tf_op jit(solution)/shard_map/ppermute | solution.py:584
  289.6 6.3 %joining.1 = bf16[74,2,256]{2,1,0:T(2,128)(2,1)} custom-call(s32[1]{0:T(128)} %bitcast.place.refs_0_, bf16[1,74,512]{2,1,0:T(8,128)(2,1)} %get-tuple-element.90.above_far, bf16[2,74,512]{2,1,0:T(8,128)(2,1)} %copy-done.15, bf16[2,74,512]{2,1,0:T(8,128)(2,1)} %get-tuple-element.83.middle, bf16[2,74,512]{2,1,0:T(8,128)(2,1)} %copy-done.16, ...), custom_call_target="tpu_custom_call" | custom-call | tf_op jit(solution)/shard_map/joining/pallas_call | solution.py:592
  (96 shorter events, 58.1 us)
Async XLA Ops:
  7.2 55.4 %copy-start = (bf16[1536,512]{1,0:T(8,128)(2,1)S(1)}, bf16[1536,512]{1,0:T(8,128)(2,1)}, u32[]{:S(2)}) copy-start(bf16[1536,512]{1,0:T(8,128)(2,1)} %param.24) | copy-start | bytes 4718596
  7.2 179.5 %all-gather.3.cloned.1.call-start = ((), (), s32[]{:S(2)}) async-start(), calls=%async_computation | async-start | bytes 10616832 | tf_op jit(solution)/shard_map/all_gather | solution.py:675
  10.9 45.3 %collective-permute-start = (bf16[148,6144]{1,0:T(8,128)(2,1)}, bf16[148,6144]{1,0:T(8,128)(2,1)S(1)}, u32[]{:S(2)}, u32[]{:S(2)}) collective-permute-start(bf16[148,6144]{1,0:T(8,128)(2,1)} %normalized_rows.1.refs_0_), channel_id=1, source_target_pairs={{0,1},{1,2},{2,3},{4,5},{5,6},{6,7},{8,9},{9,10},{10,11},{12,13},{... | collective-permute-start | bytes 5455880 | tf_op jit(solution)/shard_map/ppermute | solution.py:633
  16.1 44.4 %collective-permute-start.1 = (bf16[148,6144]{1,0:T(8,128)(2,1)}, bf16[148,6144]{1,0:T(8,128)(2,1)}, u32[]{:S(2)}, u32[]{:S(2)}) collective-permute-start(bf16[148,6144]{1,0:T(8,128)(2,1)} %normalized_rows.1.refs_0_), channel_id=1, source_target_pairs={{1,0},{2,1},{3,2},{5,4},{6,5},{7,6},{9,8},{10,9},{11,10},{13,12},{... | collective-permute-start | bytes 5455880 | tf_op jit(solution)/shard_map/ppermute | solution.py:633
  60.5 34.0 %collective-permute-start.3 = (bf16[148,6144]{1,0:T(8,128)(2,1)}, bf16[148,6144]{1,0:T(8,128)(2,1)S(1)}, u32[]{:S(2)}, u32[]{:S(2)}) collective-permute-start(bf16[148,6144]{1,0:T(8,128)(2,1)} %copy-done.6), channel_id=1, source_target_pairs={{1,2},{2,3},{5,6},{6,7},{9,10},{10,11},{13,14},{14,15},{17,18},{18... | collective-permute-start | bytes 5455880 | tf_op jit(solution)/shard_map/ppermute | solution.py:633
  61.2 45.7 %collective-permute-start.4 = (bf16[148,6144]{1,0:T(8,128)(2,1)}, bf16[148,6144]{1,0:T(8,128)(2,1)}, u32[]{:S(2)}, u32[]{:S(2)}) collective-permute-start(bf16[148,6144]{1,0:T(8,128)(2,1)} %collective-permute-done.1.refs_1_), channel_id=1, source_target_pairs={{2,1},{1,0},{6,5},{5,4},{10,9},{9,8},{14,13},{13,12},{18,17},{17,1... | collective-permute-start | bytes 5455880 | tf_op jit(solution)/shard_map/ppermute | solution.py:633
  63.3 12.0 %collective-permute-start.2 = (bf16[192,512]{1,0:T(8,128)(2,1)}, bf16[192,512]{1,0:T(8,128)(2,1)}, u32[]{:S(2)}, u32[]{:S(2)}) collective-permute-start(bf16[192,512]{1,0:T(8,128)(2,1)} %constant_dynamic-slice_fusion.1), channel_id=1, source_target_pairs={{0,1},{3,2},{4,5},{7,6},{8,9},{11,10},{12,13},{15,14},{16,17},{19,... | collective-permute-start | bytes 589832 | tf_op jit(solution)/shard_map/ppermute | solution.py:633
  72.1 36.7 %collective-permute-start.9 = (bf16[96,6144]{1,0:T(8,128)(2,1)S(1)}, bf16[96,6144]{1,0:T(8,128)(2,1)}, u32[]{:S(2)}, u32[]{:S(2)}) collective-permute-start(bf16[96,6144]{1,0:T(8,128)(2,1)S(1)} %constant_dynamic-slice_fusion), channel_id=1, source_target_pairs={{0,1},{3,2},{4,5},{7,6},{8,9},{11,10},{12,13},{15,14},{16,17},{19,... | collective-permute-start | bytes 3538952 | tf_op jit(solution)/shard_map/ppermute | solution.py:633
  108.8 155.8 %all-gather.5.cloned.1.call-start = ((), (), s32[]{:S(2)}) async-start(), calls=%async_computation.1 | async-start | bytes 7077888 | tf_op jit(solution)/shard_map/all_gather | solution.py:721
  108.9 32.2 %collective-permute-start.6 = (bf16[148,4096]{1,0:T(8,128)(2,1)S(1)}, bf16[148,4096]{1,0:T(8,128)(2,1)S(1)}, u32[]{:S(2)}, u32[]{:S(2)}) collective-permute-start(bf16[148,4096]{1,0:T(8,128)(2,1)S(1)} %slice_add_fusion.refs_0_), channel_id=1, source_target_pairs={{1,0},{2,3},{5,4},{6,7},{9,8},{10,11},{13,12},{14,15},{17,16},{18,... | collective-permute-start | bytes 3637256 | tf_op jit(solution)/shard_map/ppermute | solution.py:633
  123.5 29.6 %collective-permute-start.5 = (bf16[148,2048]{1,0:T(8,128)(2,1)S(1)}, bf16[148,2048]{1,0:T(8,128)(2,1)S(1)}, u32[]{:S(2)}, u32[]{:S(2)}) collective-permute-start(bf16[148,2048]{1,0:T(8,128)(2,1)S(1)} %slice_add_fusion.1.refs_0_), channel_id=1, source_target_pairs={{1,0},{2,3},{5,4},{6,7},{9,8},{10,11},{13,12},{14,15},{17,16},{18,... | collective-permute-start | bytes 1818632 | tf_op jit(solution)/shard_map/ppermute | solution.py:633
  125.8 8.6 %collective-permute-start.15 = (bf16[2,192,512]{2,1,0:T(8,128)(2,1)S(1)}, bf16[2,192,512]{2,1,0:T(8,128)(2,1)S(1)}, u32[]{:S(2)}, u32[]{:S(2)}) collective-permute-start(bf16[2,192,512]{2,1,0:T(8,128)(2,1)S(1)} %pad_maximum_fusion.1), channel_id=1, source_target_pairs={{1,2},{2,1},{5,6},{6,5},{9,10},{10,9},{13,14},{14,13},{17,18},{18,... | collective-permute-start | bytes 1179656 | tf_op jit(solution)/shard_map/ppermute | solution.py:633
  161.8 20.9 %collective-permute-start.16 = (bf16[3,192,512]{2,1,0:T(8,128)(2,1)S(1)}, bf16[3,192,512]{2,1,0:T(8,128)(2,1)S(1)}, u32[]{:S(2)}, u32[]{:S(2)}) collective-permute-start(bf16[3,192,512]{2,1,0:T(8,128)(2,1)S(1)} %pad_maximum_fusion), channel_id=1, source_target_pairs={{1,0},{2,3},{5,4},{6,7},{9,8},{10,11},{13,12},{14,15},{17,16},{18,... | collective-permute-start | bytes 1769480 | tf_op jit(solution)/shard_map/ppermute | solution.py:633
  170.1 12.5 %collective-permute-start.7 = (bf16[148,768]{1,0:T(8,128)(2,1)}, bf16[148,768]{1,0:T(8,128)(2,1)S(1)}, u32[]{:S(2)}, u32[]{:S(2)}) collective-permute-start(bf16[148,768]{1,0:T(8,128)(2,1)} %get-tuple-element.70.far), channel_id=1, source_target_pairs={{0,1},{3,2},{4,5},{7,6},{8,9},{11,10},{12,13},{15,14},{16,17},{19,... | collective-permute-start | bytes 681992 | tf_op jit(solution)/shard_map/ppermute | solution.py:633
  174.7 7.9 %collective-permute-start.8 = (bf16[148,768]{1,0:T(8,128)(2,1)}, bf16[148,768]{1,0:T(8,128)(2,1)S(1)}, u32[]{:S(2)}, u32[]{:S(2)}) collective-permute-start(bf16[148,768]{1,0:T(8,128)(2,1)} %get-tuple-element.61.near), channel_id=1, source_target_pairs={{0,1},{3,2},{4,5},{7,6},{8,9},{11,10},{12,13},{15,14},{16,17},{19,... | collective-permute-start | bytes 681992 | tf_op jit(solution)/shard_map/ppermute | solution.py:633
  185.4 79.2 %collective-permute-start.12 = (bf16[148,6144]{1,0:T(8,128)(2,1)}, bf16[148,6144]{1,0:T(8,128)(2,1)S(1)}, u32[]{:S(2)}, u32[]{:S(2)}) collective-permute-start(bf16[148,6144]{1,0:T(8,128)(2,1)} %edge_sums.1), channel_id=1, source_target_pairs={{1,0},{2,3},{5,4},{6,7},{9,8},{10,11},{13,12},{14,15},{17,16},{18,... | collective-permute-start | bytes 5455880 | tf_op jit(solution)/shard_map/ppermute | solution.py:633
  193.9 26.6 %collective-permute-start.10 = (bf16[148,3072]{1,0:T(8,128)(2,1)}, bf16[148,3072]{1,0:T(8,128)(2,1)S(1)}, u32[]{:S(2)}, u32[]{:S(2)}) collective-permute-start(bf16[148,3072]{1,0:T(8,128)(2,1)} %get-tuple-element.66), channel_id=1, source_target_pairs={{1,3},{2,0},{5,7},{6,4},{9,11},{10,8},{13,15},{14,12},{17,19},{18,... | collective-permute-start | bytes 2727944 | tf_op jit(solution)/shard_map/ppermute | solution.py:633
  195.2 69.4 %collective-permute-start.17 = (bf16[148,3072]{1,0:T(8,128)(2,1)}, bf16[148,3072]{1,0:T(8,128)(2,1)}, u32[]{:S(2)}, u32[]{:S(2)}) collective-permute-start(bf16[148,3072]{1,0:T(8,128)(2,1)} %get-tuple-element.69), channel_id=1, source_target_pairs={{1,2},{2,1},{5,6},{6,5},{9,10},{10,9},{13,14},{14,13},{17,18},{18,... | collective-permute-start | bytes 2727944 | tf_op jit(solution)/shard_map/ppermute | solution.py:633
  204.0 66.5 %collective-permute-start.13 = (bf16[148,3072]{1,0:T(8,128)(2,1)}, bf16[148,3072]{1,0:T(8,128)(2,1)S(1)}, u32[]{:S(2)}, u32[]{:S(2)}) collective-permute-start(bf16[148,3072]{1,0:T(8,128)(2,1)} %get-tuple-element.71), channel_id=1, source_target_pairs={{1,3},{2,0},{5,7},{6,4},{9,11},{10,8},{13,15},{14,12},{17,19},{18,... | collective-permute-start | bytes 2727944 | tf_op jit(solution)/shard_map/ppermute | solution.py:633
  205.3 65.3 %collective-permute-start.14 = (bf16[148,3072]{1,0:T(8,128)(2,1)}, bf16[148,3072]{1,0:T(8,128)(2,1)}, u32[]{:S(2)}, u32[]{:S(2)}) collective-permute-start(bf16[148,3072]{1,0:T(8,128)(2,1)} %get-tuple-element.72), channel_id=1, source_target_pairs={{1,2},{2,1},{5,6},{6,5},{9,10},{10,9},{13,14},{14,13},{17,18},{18,... | collective-permute-start | bytes 2727944 | tf_op jit(solution)/shard_map/ppermute | solution.py:633
  220.5 4.9 %collective-permute-start.11 = (bf16[148,768]{1,0:T(8,128)(2,1)S(1)}, bf16[148,768]{1,0:T(8,128)(2,1)S(1)}, u32[]{:S(2)}, u32[]{:S(2)}) collective-permute-start(bf16[148,768]{1,0:T(8,128)(2,1)S(1)} %copy-done.13), channel_id=1, source_target_pairs={{0,1},{3,2},{4,5},{7,6},{8,9},{11,10},{12,13},{15,14},{16,17},{19,... | collective-permute-start | bytes 681992 | tf_op jit(solution)/shard_map/ppermute | solution.py:633
  276.3 6.8 %collective-permute-start.18 = (bf16[1,74,512]{2,1,0:T(8,128)(2,1)}, bf16[1,74,512]{2,1,0:T(8,128)(2,1)S(1)}, u32[]{:S(2)}, u32[]{:S(2)}) collective-permute-start(bf16[1,74,512]{2,1,0:T(8,128)(2,1)} %get-tuple-element.82), channel_id=1, source_target_pairs={{0,2},{1,3},{2,0},{3,1},{4,6},{5,7},{6,4},{7,5},{8,10},{9,11},{10,... | collective-permute-start | bytes 227336 | tf_op jit(solution)/shard_map/ppermute | solution.py:584
  279.7 5.0 %collective-permute-start.19 = (bf16[2,74,512]{2,1,0:T(8,128)(2,1)}, bf16[2,74,512]{2,1,0:T(8,128)(2,1)S(1)}, u32[]{:S(2)}, u32[]{:S(2)}) collective-permute-start(bf16[2,74,512]{2,1,0:T(8,128)(2,1)} %get-tuple-element.83.middle), channel_id=1, source_target_pairs={{0,1},{1,2},{2,3},{4,5},{5,6},{6,7},{8,9},{9,10},{10,11},{12,13},{... | collective-permute-start | bytes 454664 | tf_op jit(solution)/shard_map/ppermute | solution.py:584
  281.5 7.4 %collective-permute-start.20 = (bf16[2,74,512]{2,1,0:T(8,128)(2,1)}, bf16[2,74,512]{2,1,0:T(8,128)(2,1)S(1)}, u32[]{:S(2)}, u32[]{:S(2)}) collective-permute-start(bf16[2,74,512]{2,1,0:T(8,128)(2,1)} %get-tuple-element.83.middle), channel_id=1, source_target_pairs={{1,0},{2,1},{3,2},{5,4},{6,5},{7,6},{9,8},{10,9},{11,10},{13,12},{... | collective-permute-start | bytes 454664 | tf_op jit(solution)/shard_map/ppermute | solution.py:584
  (20 other events, 110.8 us)
Sparse Core Ops, SparseCore 0:
  108.9 58.1 all-gather.2
  185.5 43.9 all-gather.4

commit v4 on v3

--- a/solution.py
+++ b/solution.py
@@ -401,40 +401,26 @@
     )(edge, weight)
 
 
-def pair_sums_kernel(rows, slot, far, near, far_got, near_got, own, got, *refs):
-    far_out, near_out, held, held_got = refs
-
-    @pl.when(pl.program_id(0) == 0)
-    def _():
-        for ref, first, second in ((held, far, near), (held_got, far_got, near_got)):
-            ref[...] = jnp.zeros_like(ref)
-            ref[0:rows] = first[...]
-            ref[slot : slot + rows] = second[...]
-
-    result = dot32(held[...], own[...]) + dot32(held_got[...], got[...])
-    far_out[...] = result[:rows].astype(bf16)
-    near_out[...] = result[slot : slot + rows].astype(bf16)
-
-
-def pair_sums(far, near, far_got, near_got, own, got, half):
-    rows, width = far.shape
+def pair_sum_kernel(mine, other, own, got, out):
+    out[...] = (dot32(mine[...], own[...]) + dot32(other[...], got[...])).astype(bf16)
+
+
+def pair_sum(mine, other, own, got, half):
+    rows, width = mine.shape
     model_width = own.shape[1]
-    slot = round_up(rows, 16)
     columns = model_width // PAIR_STEPS
     steps = PAIR_STEPS // 2
     operand = pl.BlockSpec((rows, width), lambda c: (0, 0))
     weight = pl.BlockSpec((width, columns), lambda c: (0, c + half * steps))
-    block = pl.BlockSpec((rows, columns), lambda c: (0, c))
     return pl.pallas_call(
-        functools.partial(pair_sums_kernel, rows, slot),
+        pair_sum_kernel,
         grid=(steps,),
-        in_specs=[operand] * 4 + [weight] * 2,
-        out_specs=[block] * 2,
-        out_shape=[jax.ShapeDtypeStruct((rows, model_width // 2), bf16)] * 2,
-        scratch_shapes=[pltpu.VMEM((2 * slot, width), bf16)] * 2,
+        in_specs=[operand] * 2 + [weight] * 2,
+        out_specs=pl.BlockSpec((rows, columns), lambda c: (0, c)),
+        out_shape=jax.ShapeDtypeStruct((rows, model_width // 2), bf16),
         compiler_params=pltpu.CompilerParams(vmem_limit_bytes=VMEM_LIMIT),
-        name="pair_sums",
-    )(far, near, far_got, near_got, own, got)
+        name="pair_sum",
+    )(mine, other, own, got)
 
 
 def own_kernel(tokens, mine, other, own, got, out):
@@ -696,9 +682,11 @@
     parts = []
     for half in range(2):
         if half == 1:
-            far = after(far, sums)
-        sums = pair_sums(far, near, far_got, near_got, output_weight, partner_weight, half)
-        parts.append((send(sums[0], [(1, 3), (2, 0)]), send(sums[1], [(1, 2), (2, 1)])))
+            far = after(far, near_sum)
+        far_sum = pair_sum(far, far_got, output_weight, partner_weight, half)
+        near = after(near, far_sum)
+        near_sum = pair_sum(near, near_got, output_weight, partner_weight, half)
+        parts.append((send(far_sum, [(1, 3), (2, 0)]), send(near_sum, [(1, 2), (2, 1)])))
         if half == 0:
             mine_got = send(after(edge_rows, parts[0][0]), inward)
     small, small_end, small_two, three = after((small, small_end, small_two, three), far_got)

time: 304 us -> 302 us (level)
  waiting for transfers between devices: 90.7 us -> 78.5 us
  Pallas kernels: 131 us -> 140 us
    ppermute x18, waiting for transfers between devices: 85.2 us -> 73 us  [on_device_line(): send = lambda value, pairs: lax.ppermute(value, 'tensor', pairs)]
    pallas_call x2 -> x4, Pallas kernels: 14.3 us -> 23.6 us  [pair_sum(): pl.pallas_call(pair_sum_kernel, grid=(steps,), in_specs=[operand] * 2 + [...]
  transfers between devices with their start and end apart: 23 -> 23, of which waited for: 11 -> 11; matrix products, arithmetic and copies ran while one was open for 5% -> 5% of each run, Pallas kernels for 38% -> 42%
where the time goes in v4:
time: 302 us; the launch traced here: 301 us
  Pallas kernels  140 us (46%)
  waiting for transfers between devices  78.5 us (26%)
  starting transfers between devices  45.8 us (15%)
  local copies, waits for them, and re-layouts  15 us (5%)
  between operations  14.4 us (5%)
  other arithmetic  7.39 us (2%)
    ppermute x18, waiting for transfers between devices, on_device_line(): send = lambda value, pairs: lax.ppermute(value, 'tensor', pairs)  73 us
    pallas_call x6, Pallas kernels, project(): pl.pallas_call(functools.partial(project_kernel, count, cuts, len(earlier...  72.7 us
    ppermute x18, starting transfers between devices, on_device_line(): send = lambda value, pairs: lax.ppermute(value, 'tensor', pairs)  40.6 us
    pallas_call x4, Pallas kernels, pair_sum(): pl.pallas_call(pair_sum_kernel, grid=(steps,), in_specs=[operand] * 2 + [...  23.6 us
    pallas_call x1, Pallas kernels, own_sums(): pl.pallas_call(own_kernel, grid=(PAIR_STEPS,), in_specs=[block, operand,...  11.1 us
    unnamed x43, local copies, waits for them, and re-layouts  10.4 us
    pallas_call x2, Pallas kernels, finish(): pl.pallas_call(functools.partial(finish_kernel, half), grid=(steps,), in_...  9.4 us
    pallas_call x1, Pallas kernels, attention(): pl.pallas_call(functools.partial(attention_kernel, rows, slot), grid=(wid...  7.07 us
  transfers between devices with their start and end apart: 23, of which 11 were waited for; matrix products, arithmetic and copies ran while one was open for 5% of the time, Pallas kernels for 42%

profile of v4, /device:TPU:0, one launch (start us, length us, event | category | flops | bytes accessed | tf_op | source)
XLA Modules:
  0.0 301.3 jit_solution(1876739013074082198)
XLA Ops:
  10.9 5.2 %collective-permute-start = (bf16[148,6144]{1,0:T(8,128)(2,1)}, bf16[148,6144]{1,0:T(8,128)(2,1)S(1)}, u32[]{:S(2)}, u32[]{:S(2)}) collective-permute-start(bf16[148,6144]{1,0:T(8,128)(2,1)} %normalized_rows.1.refs_0_), channel_id=1, source_target_pairs={{0,1},{1,2},{2,3},{4,5},{5,6},{6,7},{8,9},{9,10},{10,11},{12,13},{... | collective-permute-start | bytes 5455880 | tf_op jit(solution)/shard_map/ppermute | solution.py:619
  22.3 15.1 %project.6.refs_0_ = bf16[3,148,768]{2,1,0:T(8,128)(2,1)} custom-call(bf16[148,6144]{1,0:T(8,128)(2,1)} %normalized_rows.1.refs_0_, bf16[6144,768]{1,0:T(8,128)(2,1)} %refs_1_.10, bf16[6144,768]{1,0:T(8,128)(2,1)} %refs_2_.12, bf16[6144,768]{1,0:T(8,128)(2,1)} %refs_3_.11, bf16[6144,32]{1,0:T(8,128)(2,1)} %copy.17.refs_4_.refs_5_, ...), custom_call_target="tpu_custom_call" | custom-call | tf_op jit(solution)/shard_map/project/pallas_call | solution.py:291
  37.4 18.9 %collective-permute-done.refs_0_ = bf16[148,6144]{1,0:T(8,128)(2,1)S(1)} collective-permute-done((bf16[148,6144]{1,0:T(8,128)(2,1)}, bf16[148,6144]{1,0:T(8,128)(2,1)S(1)}, u32[]{:S(2)}, u32[]{:S(2)}) %collective-permute-start) | collective-permute-done | bytes 1818656 | tf_op jit(solution)/shard_map/ppermute | solution.py:619
  63.2 7.5 %collective-permute-start.2 = (bf16[192,512]{1,0:T(8,128)(2,1)}, bf16[192,512]{1,0:T(8,128)(2,1)}, u32[]{:S(2)}, u32[]{:S(2)}) collective-permute-start(bf16[192,512]{1,0:T(8,128)(2,1)} %constant_dynamic-slice_fusion.1), channel_id=1, source_target_pairs={{0,1},{3,2},{4,5},{7,6},{8,9},{11,10},{12,13},{15,14},{16,17},{19,... | collective-permute-start | bytes 589832 | tf_op jit(solution)/shard_map/ppermute | solution.py:619
  75.2 19.2 %project.7 = (bf16[3,148,768]{2,1,0:T(8,128)(2,1)}, bf16[3,148,768]{2,1,0:T(8,128)(2,1)}) custom-call(bf16[148,6144]{1,0:T(8,128)(2,1)} %copy-done.6, bf16[148,6144]{1,0:T(8,128)(2,1)} %collective-permute-done.1.refs_1_, bf16[6144,768]{1,0:T(8,128)(2,1)} %refs_1_.10, bf16[6144,768]{1,0:T(8,128)(2,1)} %refs_2_.12, bf16[6144,768]{1,0:T(8,128)(2,1)} %refs_3_.11, ...), custom_call_target="tpu_custom_call" | custom-call | tf_op jit(solution)/shard_map/project/pallas_call | solution.py:291
  95.7 11.3 %collective-permute-done.4 = bf16[148,6144]{1,0:T(8,128)(2,1)} collective-permute-done((bf16[148,6144]{1,0:T(8,128)(2,1)}, bf16[148,6144]{1,0:T(8,128)(2,1)}, u32[]{:S(2)}, u32[]{:S(2)}) %collective-permute-start.4) | collective-permute-done | bytes 1818656 | tf_op jit(solution)/shard_map/ppermute | solution.py:619
  110.4 11.7 %project.8 = (f32[1,3,148,768]{3,2,1,0:T(8,128)}, f32[1,148,32]{2,1,0:T(8,128)}) custom-call(bf16[148,4096]{1,0:T(8,128)(2,1)} %copy-done.3, bf16[6144,768]{1,0:T(8,128)(2,1)} %refs_1_.10, bf16[6144,768]{1,0:T(8,128)(2,1)} %refs_2_.12, bf16[6144,768]{1,0:T(8,128)(2,1)} %refs_3_.11, bf16[6144,32]{1,0:T(8,128)(2,1)} %copy.17.refs_4_.refs_5_, ...), custom_call_target="tpu_custom_call" | custom-call | tf_op jit(solution)/shard_map/project/pallas_call | solution.py:291
  126.4 7.8 %project.9.refs_3_ = bf16[3,148,768]{2,1,0:T(8,128)(2,1)} custom-call(bf16[148,2048]{1,0:T(8,128)(2,1)} %copy-done.4, bf16[6144,768]{1,0:T(8,128)(2,1)} %refs_1_.10, bf16[6144,768]{1,0:T(8,128)(2,1)} %refs_2_.12, bf16[6144,768]{1,0:T(8,128)(2,1)} %refs_3_.11, bf16[6144,32]{1,0:T(8,128)(2,1)} %copy.17.refs_4_.refs_5_, bf16[32,768]{1,0:T(8,128)(2,1)} %pad.8.refs_5_.refs_6_, ...), custom_call_target="tpu_custom_call" | custom-call | tf_op jit(solution)/shard_map/project/pallas_call | solution.py:291
  134.3 6.8 %collective-permute-done.6.refs_0_ = bf16[148,4096]{1,0:T(8,128)(2,1)S(1)} collective-permute-done((bf16[148,4096]{1,0:T(8,128)(2,1)S(1)}, bf16[148,4096]{1,0:T(8,128)(2,1)S(1)}, u32[]{:S(2)}, u32[]{:S(2)}) %collective-permute-start.6) | collective-permute-done | bytes 1212448 | tf_op jit(solution)/shard_map/ppermute | solution.py:619
  142.1 11.0 %project.10 = (f32[1,3,148,768]{3,2,1,0:T(8,128)}, f32[1,148,32]{2,1,0:T(8,128)}) custom-call(bf16[148,4096]{1,0:T(8,128)(2,1)} %copy-done.7, bf16[6144,768]{1,0:T(8,128)(2,1)} %refs_1_.10, bf16[6144,768]{1,0:T(8,128)(2,1)} %refs_2_.12, bf16[6144,768]{1,0:T(8,128)(2,1)} %refs_3_.11, bf16[6144,32]{1,0:T(8,128)(2,1)} %copy.17.refs_4_.refs_5_, ...), custom_call_target="tpu_custom_call" | custom-call | tf_op jit(solution)/shard_map/project/pallas_call | solution.py:291
  154.0 7.8 %project.11.refs_4_ = bf16[3,148,768]{2,1,0:T(8,128)(2,1)} custom-call(bf16[148,2048]{1,0:T(8,128)(2,1)} %copy-done.12, bf16[6144,768]{1,0:T(8,128)(2,1)} %refs_1_.10, bf16[6144,768]{1,0:T(8,128)(2,1)} %refs_2_.12, bf16[6144,768]{1,0:T(8,128)(2,1)} %refs_3_.11, bf16[6144,32]{1,0:T(8,128)(2,1)} %copy.17.refs_4_.refs_5_, bf16[32,768]{1,0:T(8,128)(2,1)} %pad.8.refs_5_.refs_6_, ...), custom_call_target="tpu_custom_call" | custom-call | tf_op jit(solution)/shard_map/project/pallas_call | solution.py:291
  163.1 7.1 %attention.1 = (bf16[148,768]{1,0:T(8,128)(2,1)}, bf16[148,768]{1,0:T(8,128)(2,1)}, bf16[148,768]{1,0:T(8,128)(2,1)}, bf16[148,768]{1,0:T(8,128)(2,1)}) custom-call(s32[1]{0:T(128)} %bitcast.place.refs_0_, bf16[3,148,768]{2,1,0:T(8,128)(2,1)} %project.6.refs_0_, bf16[3,148,768]{2,1,0:T(8,128)(2,1)} %get-tuple-element.46.refs_1_, ...), custom_call_target="tpu_custom_call" | custom-call | tf_op jit(solution)/shard_map/attention/pallas_call | solution.py:366
  170.2 4.6 %collective-permute-start.7 = (bf16[148,768]{1,0:T(8,128)(2,1)}, bf16[148,768]{1,0:T(8,128)(2,1)S(1)}, u32[]{:S(2)}, u32[]{:S(2)}) collective-permute-start(bf16[148,768]{1,0:T(8,128)(2,1)} %get-tuple-element.67.mine), channel_id=1, source_target_pairs={{0,1},{3,2},{4,5},{7,6},{8,9},{11,10},{12,13},{15,14},{16,17},{19,... | collective-permute-start | bytes 681992 | tf_op jit(solution)/shard_map/ppermute | solution.py:619
  176.3 6.4 %edge_sums.1 = bf16[148,6144]{1,0:T(8,128)(2,1)} custom-call(bf16[148,768]{1,0:T(8,128)(2,1)} %get-tuple-element.63.edge, bf16[768,6144]{1,0:T(8,128)(2,1)} %own.9), custom_call_target="tpu_custom_call" | custom-call | tf_op jit(solution)/shard_map/edge_sums/pallas_call | solution.py:390
  186.8 5.8 %pair_sum.4 = bf16[148,3072]{1,0:T(8,128)(2,1)} custom-call(bf16[148,768]{1,0:T(8,128)(2,1)} %get-tuple-element.67.mine, bf16[148,768]{1,0:T(8,128)(2,1)} %copy-done.11, bf16[768,6144]{1,0:T(8,128)(2,1)} %own.9, bf16[768,6144]{1,0:T(8,128)(2,1)} %all-gather.3.cloned.1.call-done.got), custom_call_target="tpu_custom_call" | custom-call | tf_op jit(solution)/shard_map/pair_sum/pallas_call | solution.py:415
  193.8 5.7 %pair_sum.5 = bf16[148,3072]{1,0:T(8,128)(2,1)} custom-call(bf16[148,768]{1,0:T(8,128)(2,1)} %get-tuple-element.68.mine, bf16[148,768]{1,0:T(8,128)(2,1)} %copy-done.10, bf16[768,6144]{1,0:T(8,128)(2,1)} %own.9, bf16[768,6144]{1,0:T(8,128)(2,1)} %all-gather.3.cloned.1.call-done.got), custom_call_target="tpu_custom_call" | custom-call | tf_op jit(solution)/shard_map/pair_sum/pallas_call | solution.py:415
  199.5 5.7 %pair_sum.6 = bf16[148,3072]{1,0:T(8,128)(2,1)} custom-call(bf16[148,768]{1,0:T(8,128)(2,1)} %get-tuple-element.67.mine, bf16[148,768]{1,0:T(8,128)(2,1)} %copy-done.11, bf16[768,6144]{1,0:T(8,128)(2,1)} %own.9, bf16[768,6144]{1,0:T(8,128)(2,1)} %all-gather.3.cloned.1.call-done.got), custom_call_target="tpu_custom_call" | custom-call | tf_op jit(solution)/shard_map/pair_sum/pallas_call | solution.py:415
  208.3 6.4 %pair_sum.7 = bf16[148,3072]{1,0:T(8,128)(2,1)} custom-call(bf16[148,768]{1,0:T(8,128)(2,1)} %get-tuple-element.68.mine, bf16[148,768]{1,0:T(8,128)(2,1)} %copy-done.10, bf16[768,6144]{1,0:T(8,128)(2,1)} %own.9, bf16[768,6144]{1,0:T(8,128)(2,1)} %all-gather.3.cloned.1.call-done.got), custom_call_target="tpu_custom_call" | custom-call | tf_op jit(solution)/shard_map/pair_sum/pallas_call | solution.py:415
  227.7 11.1 %own_sums.1.mine = f32[148,6144]{1,0:T(8,128)} custom-call(bf16[148,6144]{1,0:T(8,128)(2,1)} %tokens.3, bf16[148,768]{1,0:T(8,128)(2,1)} %get-tuple-element.56.mine, bf16[148,768]{1,0:T(8,128)(2,1)} %copy-done.14, bf16[768,6144]{1,0:T(8,128)(2,1)} %own.9, bf16[768,6144]{1,0:T(8,128)(2,1)} %all-gather.3.cloned.1.call-done.got), custom_call_target="tpu_custom_call" | custom-call | tf_op jit(solution)/shard_map/own_sums/pallas_call | solution.py:439
  238.8 25.9 %collective-permute-done.12.edge = bf16[148,6144]{1,0:T(8,128)(2,1)S(1)} collective-permute-done((bf16[148,6144]{1,0:T(8,128)(2,1)}, bf16[148,6144]{1,0:T(8,128)(2,1)S(1)}, u32[]{:S(2)}, u32[]{:S(2)}) %collective-permute-start.12) | collective-permute-done | bytes 1818656 | tf_op jit(solution)/shard_map/ppermute | solution.py:619
  265.9 4.7 %finish.2 = (bf16[148,6144]{1,0:T(8,128)(2,1)}, f32[148,512]{1,0:T(8,128)}) custom-call(f32[148,6144]{1,0:T(8,128)} %own_sums.1.mine, bf16[148,6144]{1,0:T(8,128)(2,1)} %copy-done.2, bf16[148,3072]{1,0:T(8,128)(2,1)} %copy-done.9, bf16[148,3072]{1,0:T(8,128)(2,1)} %collective-permute-done.17.near, bf16[6144,512]{1,0:T(8,128)(2,1)} %bitcast.8), custom_call_target="tpu_custom_call" | custom-call | tf_op jit(solution)/shard_map/finish/pallas_call | solution.py:491
  271.5 4.7 %finish.3 = (bf16[148,6144]{1,0:T(8,128)(2,1)}, bf16[2,74,512]{2,1,0:T(8,128)(2,1)}, bf16[1,74,512]{2,1,0:T(8,128)(2,1)}) custom-call(f32[148,6144]{1,0:T(8,128)} %own_sums.1.mine, bf16[148,6144]{1,0:T(8,128)(2,1)} %copy-done.2, bf16[148,3072]{1,0:T(8,128)(2,1)} %copy-done.8, ...), custom_call_target="tpu_custom_call", output_to_operand_aliasing={{0}: (7, {})} | custom-call | tf_op jit(solution)/shard_map/finish/pallas_call | solution.py:491
  283.2 4.3 %collective-permute-done.20.below = bf16[2,74,512]{2,1,0:T(8,128)(2,1)S(1)} collective-permute-done((bf16[2,74,512]{2,1,0:T(8,128)(2,1)}, bf16[2,74,512]{2,1,0:T(8,128)(2,1)S(1)}, u32[]{:S(2)}, u32[]{:S(2)}) %collective-permute-start.20) | collective-permute-done | bytes 151584 | tf_op jit(solution)/shard_map/ppermute | solution.py:570
  288.1 6.3 %joining.1 = bf16[74,2,256]{2,1,0:T(2,128)(2,1)} custom-call(s32[1]{0:T(128)} %bitcast.place.refs_0_, bf16[1,74,512]{2,1,0:T(8,128)(2,1)} %get-tuple-element.86.above_far, bf16[2,74,512]{2,1,0:T(8,128)(2,1)} %copy-done.15, bf16[2,74,512]{2,1,0:T(8,128)(2,1)} %get-tuple-element.79.middle, bf16[2,74,512]{2,1,0:T(8,128)(2,1)} %copy-done.16, ...), custom_call_target="tpu_custom_call" | custom-call | tf_op jit(solution)/shard_map/joining/pallas_call | solution.py:578
  (98 shorter events, 66.0 us)
Async XLA Ops:
  7.2 55.4 %copy-start = (bf16[1536,512]{1,0:T(8,128)(2,1)S(1)}, bf16[1536,512]{1,0:T(8,128)(2,1)}, u32[]{:S(2)}) copy-start(bf16[1536,512]{1,0:T(8,128)(2,1)} %param.24) | copy-start | bytes 4718596
  7.2 179.6 %all-gather.3.cloned.1.call-start = ((), (), s32[]{:S(2)}) async-start(), calls=%async_computation | async-start | bytes 10616832 | tf_op jit(solution)/shard_map/all_gather | solution.py:661
  10.9 45.3 %collective-permute-start = (bf16[148,6144]{1,0:T(8,128)(2,1)}, bf16[148,6144]{1,0:T(8,128)(2,1)S(1)}, u32[]{:S(2)}, u32[]{:S(2)}) collective-permute-start(bf16[148,6144]{1,0:T(8,128)(2,1)} %normalized_rows.1.refs_0_), channel_id=1, source_target_pairs={{0,1},{1,2},{2,3},{4,5},{5,6},{6,7},{8,9},{9,10},{10,11},{12,13},{... | collective-permute-start | bytes 5455880 | tf_op jit(solution)/shard_map/ppermute | solution.py:619
  16.1 44.4 %collective-permute-start.1 = (bf16[148,6144]{1,0:T(8,128)(2,1)}, bf16[148,6144]{1,0:T(8,128)(2,1)}, u32[]{:S(2)}, u32[]{:S(2)}) collective-permute-start(bf16[148,6144]{1,0:T(8,128)(2,1)} %normalized_rows.1.refs_0_), channel_id=1, source_target_pairs={{1,0},{2,1},{3,2},{5,4},{6,5},{7,6},{9,8},{10,9},{11,10},{13,12},{... | collective-permute-start | bytes 5455880 | tf_op jit(solution)/shard_map/ppermute | solution.py:619
  60.5 34.0 %collective-permute-start.3 = (bf16[148,6144]{1,0:T(8,128)(2,1)}, bf16[148,6144]{1,0:T(8,128)(2,1)S(1)}, u32[]{:S(2)}, u32[]{:S(2)}) collective-permute-start(bf16[148,6144]{1,0:T(8,128)(2,1)} %copy-done.6), channel_id=1, source_target_pairs={{1,2},{2,3},{5,6},{6,7},{9,10},{10,11},{13,14},{14,15},{17,18},{18... | collective-permute-start | bytes 5455880 | tf_op jit(solution)/shard_map/ppermute | solution.py:619
  61.2 45.7 %collective-permute-start.4 = (bf16[148,6144]{1,0:T(8,128)(2,1)}, bf16[148,6144]{1,0:T(8,128)(2,1)}, u32[]{:S(2)}, u32[]{:S(2)}) collective-permute-start(bf16[148,6144]{1,0:T(8,128)(2,1)} %collective-permute-done.1.refs_1_), channel_id=1, source_target_pairs={{2,1},{1,0},{6,5},{5,4},{10,9},{9,8},{14,13},{13,12},{18,17},{17,1... | collective-permute-start | bytes 5455880 | tf_op jit(solution)/shard_map/ppermute | solution.py:619
  63.2 12.0 %collective-permute-start.2 = (bf16[192,512]{1,0:T(8,128)(2,1)}, bf16[192,512]{1,0:T(8,128)(2,1)}, u32[]{:S(2)}, u32[]{:S(2)}) collective-permute-start(bf16[192,512]{1,0:T(8,128)(2,1)} %constant_dynamic-slice_fusion.1), channel_id=1, source_target_pairs={{0,1},{3,2},{4,5},{7,6},{8,9},{11,10},{12,13},{15,14},{16,17},{19,... | collective-permute-start | bytes 589832 | tf_op jit(solution)/shard_map/ppermute | solution.py:619
  72.1 36.7 %collective-permute-start.9 = (bf16[96,6144]{1,0:T(8,128)(2,1)S(1)}, bf16[96,6144]{1,0:T(8,128)(2,1)}, u32[]{:S(2)}, u32[]{:S(2)}) collective-permute-start(bf16[96,6144]{1,0:T(8,128)(2,1)S(1)} %constant_dynamic-slice_fusion), channel_id=1, source_target_pairs={{0,1},{3,2},{4,5},{7,6},{8,9},{11,10},{12,13},{15,14},{16,17},{19,... | collective-permute-start | bytes 3538952 | tf_op jit(solution)/shard_map/ppermute | solution.py:619
  108.8 155.8 %all-gather.5.cloned.1.call-start = ((), (), s32[]{:S(2)}) async-start(), calls=%async_computation.1 | async-start | bytes 7077888 | tf_op jit(solution)/shard_map/all_gather | solution.py:709
  108.9 32.2 %collective-permute-start.6 = (bf16[148,4096]{1,0:T(8,128)(2,1)S(1)}, bf16[148,4096]{1,0:T(8,128)(2,1)S(1)}, u32[]{:S(2)}, u32[]{:S(2)}) collective-permute-start(bf16[148,4096]{1,0:T(8,128)(2,1)S(1)} %slice_add_fusion.refs_0_), channel_id=1, source_target_pairs={{1,0},{2,3},{5,4},{6,7},{9,8},{10,11},{13,12},{14,15},{17,16},{18,... | collective-permute-start | bytes 3637256 | tf_op jit(solution)/shard_map/ppermute | solution.py:619
  123.5 29.7 %collective-permute-start.5 = (bf16[148,2048]{1,0:T(8,128)(2,1)S(1)}, bf16[148,2048]{1,0:T(8,128)(2,1)S(1)}, u32[]{:S(2)}, u32[]{:S(2)}) collective-permute-start(bf16[148,2048]{1,0:T(8,128)(2,1)S(1)} %slice_add_fusion.1.refs_0_), channel_id=1, source_target_pairs={{1,0},{2,3},{5,4},{6,7},{9,8},{10,11},{13,12},{14,15},{17,16},{18,... | collective-permute-start | bytes 1818632 | tf_op jit(solution)/shard_map/ppermute | solution.py:619
  125.7 8.5 %collective-permute-start.15 = (bf16[2,192,512]{2,1,0:T(8,128)(2,1)S(1)}, bf16[2,192,512]{2,1,0:T(8,128)(2,1)S(1)}, u32[]{:S(2)}, u32[]{:S(2)}) collective-permute-start(bf16[2,192,512]{2,1,0:T(8,128)(2,1)S(1)} %pad_maximum_fusion.1), channel_id=1, source_target_pairs={{1,2},{2,1},{5,6},{6,5},{9,10},{10,9},{13,14},{14,13},{17,18},{18,... | collective-permute-start | bytes 1179656 | tf_op jit(solution)/shard_map/ppermute | solution.py:619
  161.8 20.9 %collective-permute-start.16 = (bf16[3,192,512]{2,1,0:T(8,128)(2,1)S(1)}, bf16[3,192,512]{2,1,0:T(8,128)(2,1)S(1)}, u32[]{:S(2)}, u32[]{:S(2)}) collective-permute-start(bf16[3,192,512]{2,1,0:T(8,128)(2,1)S(1)} %pad_maximum_fusion), channel_id=1, source_target_pairs={{1,0},{2,3},{5,4},{6,7},{9,8},{10,11},{13,12},{14,15},{17,16},{18,... | collective-permute-start | bytes 1769480 | tf_op jit(solution)/shard_map/ppermute | solution.py:619
  170.2 12.5 %collective-permute-start.7 = (bf16[148,768]{1,0:T(8,128)(2,1)}, bf16[148,768]{1,0:T(8,128)(2,1)S(1)}, u32[]{:S(2)}, u32[]{:S(2)}) collective-permute-start(bf16[148,768]{1,0:T(8,128)(2,1)} %get-tuple-element.67.mine), channel_id=1, source_target_pairs={{0,1},{3,2},{4,5},{7,6},{8,9},{11,10},{12,13},{15,14},{16,17},{19,... | collective-permute-start | bytes 681992 | tf_op jit(solution)/shard_map/ppermute | solution.py:619
  174.8 7.9 %collective-permute-start.8 = (bf16[148,768]{1,0:T(8,128)(2,1)}, bf16[148,768]{1,0:T(8,128)(2,1)S(1)}, u32[]{:S(2)}, u32[]{:S(2)}) collective-permute-start(bf16[148,768]{1,0:T(8,128)(2,1)} %get-tuple-element.68.mine), channel_id=1, source_target_pairs={{0,1},{3,2},{4,5},{7,6},{8,9},{11,10},{12,13},{15,14},{16,17},{19,... | collective-permute-start | bytes 681992 | tf_op jit(solution)/shard_map/ppermute | solution.py:619
  185.4 79.2 %collective-permute-start.12 = (bf16[148,6144]{1,0:T(8,128)(2,1)}, bf16[148,6144]{1,0:T(8,128)(2,1)S(1)}, u32[]{:S(2)}, u32[]{:S(2)}) collective-permute-start(bf16[148,6144]{1,0:T(8,128)(2,1)} %edge_sums.1), channel_id=1, source_target_pairs={{1,0},{2,3},{5,4},{6,7},{9,8},{10,11},{13,12},{14,15},{17,16},{18,... | collective-permute-start | bytes 5455880 | tf_op jit(solution)/shard_map/ppermute | solution.py:619
  192.5 26.6 %collective-permute-start.10 = (bf16[148,3072]{1,0:T(8,128)(2,1)}, bf16[148,3072]{1,0:T(8,128)(2,1)S(1)}, u32[]{:S(2)}, u32[]{:S(2)}) collective-permute-start(bf16[148,3072]{1,0:T(8,128)(2,1)} %pair_sum.4), channel_id=1, source_target_pairs={{1,3},{2,0},{5,7},{6,4},{9,11},{10,8},{13,15},{14,12},{17,19},{18,... | collective-permute-start | bytes 2727944 | tf_op jit(solution)/shard_map/ppermute | solution.py:619
  205.3 65.3 %collective-permute-start.13 = (bf16[148,3072]{1,0:T(8,128)(2,1)}, bf16[148,3072]{1,0:T(8,128)(2,1)S(1)}, u32[]{:S(2)}, u32[]{:S(2)}) collective-permute-start(bf16[148,3072]{1,0:T(8,128)(2,1)} %pair_sum.6), channel_id=1, source_target_pairs={{1,3},{2,0},{5,7},{6,4},{9,11},{10,8},{13,15},{14,12},{17,19},{18,... | collective-permute-start | bytes 2727944 | tf_op jit(solution)/shard_map/ppermute | solution.py:619
  206.7 58.0 %collective-permute-start.17 = (bf16[148,3072]{1,0:T(8,128)(2,1)}, bf16[148,3072]{1,0:T(8,128)(2,1)}, u32[]{:S(2)}, u32[]{:S(2)}) collective-permute-start(bf16[148,3072]{1,0:T(8,128)(2,1)} %pair_sum.5), channel_id=1, source_target_pairs={{1,2},{2,1},{5,6},{6,5},{9,10},{10,9},{13,14},{14,13},{17,18},{18,... | collective-permute-start | bytes 2727944 | tf_op jit(solution)/shard_map/ppermute | solution.py:619
  214.7 55.9 %collective-permute-start.14 = (bf16[148,3072]{1,0:T(8,128)(2,1)}, bf16[148,3072]{1,0:T(8,128)(2,1)}, u32[]{:S(2)}, u32[]{:S(2)}) collective-permute-start(bf16[148,3072]{1,0:T(8,128)(2,1)} %pair_sum.7), channel_id=1, source_target_pairs={{1,2},{2,1},{5,6},{6,5},{9,10},{10,9},{13,14},{14,13},{17,18},{18,... | collective-permute-start | bytes 2727944 | tf_op jit(solution)/shard_map/ppermute | solution.py:619
  219.1 7.8 %collective-permute-start.11 = (bf16[148,768]{1,0:T(8,128)(2,1)S(1)}, bf16[148,768]{1,0:T(8,128)(2,1)S(1)}, u32[]{:S(2)}, u32[]{:S(2)}) collective-permute-start(bf16[148,768]{1,0:T(8,128)(2,1)S(1)} %copy-done.13), channel_id=1, source_target_pairs={{0,1},{3,2},{4,5},{7,6},{8,9},{11,10},{12,13},{15,14},{16,17},{19,... | collective-permute-start | bytes 681992 | tf_op jit(solution)/shard_map/ppermute | solution.py:619
  276.3 5.6 %collective-permute-start.18 = (bf16[1,74,512]{2,1,0:T(8,128)(2,1)}, bf16[1,74,512]{2,1,0:T(8,128)(2,1)S(1)}, u32[]{:S(2)}, u32[]{:S(2)}) collective-permute-start(bf16[1,74,512]{2,1,0:T(8,128)(2,1)} %get-tuple-element.78), channel_id=1, source_target_pairs={{0,2},{1,3},{2,0},{3,1},{4,6},{5,7},{6,4},{7,5},{8,10},{9,11},{10,... | collective-permute-start | bytes 227336 | tf_op jit(solution)/shard_map/ppermute | solution.py:570
  278.2 5.0 %collective-permute-start.19 = (bf16[2,74,512]{2,1,0:T(8,128)(2,1)}, bf16[2,74,512]{2,1,0:T(8,128)(2,1)S(1)}, u32[]{:S(2)}, u32[]{:S(2)}) collective-permute-start(bf16[2,74,512]{2,1,0:T(8,128)(2,1)} %get-tuple-element.79.middle), channel_id=1, source_target_pairs={{0,1},{1,2},{2,3},{4,5},{5,6},{6,7},{8,9},{9,10},{10,11},{12,13},{... | collective-permute-start | bytes 454664 | tf_op jit(solution)/shard_map/ppermute | solution.py:570
  280.0 7.4 %collective-permute-start.20 = (bf16[2,74,512]{2,1,0:T(8,128)(2,1)}, bf16[2,74,512]{2,1,0:T(8,128)(2,1)S(1)}, u32[]{:S(2)}, u32[]{:S(2)}) collective-permute-start(bf16[2,74,512]{2,1,0:T(8,128)(2,1)} %get-tuple-element.79.middle), channel_id=1, source_target_pairs={{1,0},{2,1},{3,2},{5,4},{6,5},{7,6},{9,8},{10,9},{11,10},{13,12},{... | collective-permute-start | bytes 454664 | tf_op jit(solution)/shard_map/ppermute | solution.py:570
  (20 other events, 102.3 us)
Sparse Core Ops, SparseCore 0:
  108.9 58.1 all-gather.2
  185.6 43.9 all-gather.4
